TPU v7x, 512 devices: a whole 4x4x16 slice. The times are simulated.
512 devices in a mesh: seq: 16 (over z), tensor: 4 (over y), dp: 8 (over x, core).
Axes of the slice: x: 4, y: 4, z: 16, core: 2. Of those that a mesh axis runs over, the one named last changes fastest.
Arguments:
- seq_values: bfloat16 [8, 2048, 8192], P('dp', 'seq', 'tensor'), may hold values from -6 to 6
- proj_b: bfloat16 [8, 2048, 512], P('dp', 'seq', 'tensor'), may hold values from -0.75 to 0.75
- proj_c: bfloat16 [8, 2048, 512], P('dp', 'seq', 'tensor'), may hold values from -0.75 to 0.75
- time_step: float32 [8, 2048, 128], P('dp', 'seq', 'tensor'), may hold values from 0.5 to 6144, as said below
- decay_level: int32 [8, 16, 128], P('dp', 'seq', 'tensor'), may hold values from 0 to 7
- decay_rate: float32 [128, 8], P('tensor'), may hold values from 4.8828125e-05 to 0.06666667, as said below
- skip_gain: float32 [128], P('tensor'), may hold values from 0.5 to 2
- grad_out: bfloat16 [8, 2048, 8192], P('dp', 'seq', 'tensor'), may hold values from -12 to 12
- layer_input: bfloat16 [8, 2048, 8192], P('dp', 'seq', 'tensor'), may hold values from -64 to 64
- weight_c: float32 [8192, 512], P(('seq', 'dp'), 'tensor'), may hold values from -0.75 to 0.75
- moment_one: float32 [8192, 512], P(('seq', 'dp'), 'tensor'), may hold values from -4 to 4
- moment_two: float32 [8192, 512], P(('seq', 'dp'), 'tensor'), may hold values from 0.01 to 0.1
Outputs:
- grad_values: bfloat16 [8, 2048, 8192], P('dp', 'seq', 'tensor')
- grad_b: bfloat16 [8, 2048, 512], P('dp', 'seq', 'tensor')
- grad_c: bfloat16 [8, 2048, 512], P('dp', 'seq', 'tensor')
- grad_lograte: float32 [128, 8], P('tensor')
- grad_skip: float32 [128], P('tensor')
- new_weight: float32 [8192, 512], P(('seq', 'dp'), 'tensor')
- new_moment: float32 [8192, 512], P(('seq', 'dp'), 'tensor')
- new_second: float32 [8192, 512], P(('seq', 'dp'), 'tensor')
Inputs may be any that keep to these rules, and one draw needn't show every extreme that they name: `decay_rate`: positive decay rates. `time_step`: positive step sizes.
All inputs are finite; a program needn't handle non-finite values.
Results may differ from a plain program's by a relative error of at most 0.015.
Values may be sent and summed in bfloat16 or wider, within the bound.
No kernel may reach another device: no remote copies, remote signals or barrier semaphores. Data moves between devices by JAX's collectives and lax.ppermute only.
A program may use at most 128 MiB of HBM per device.

v0:
```python
import math

import jax
import jax.numpy as jnp
from jax import lax
from jax.sharding import PartitionSpec as P

D = 8192
P_SIZE = 64
N = 128
G = 4


beta_one = 0.9
beta_two = 0.95
adam_eps = 1e-08
learn_rate = 0.02
decay_weight = 0.1
step_count = 10


def carried_in(x, axis, combine, identity, reverse):
    count, position = (lax.axis_size(axis), lax.axis_index(axis))
    everything = jax.tree.map(lambda part: lax.all_gather(part, axis), x)
    start = jax.tree.map(
        lambda part, zero: jnp.broadcast_to(jnp.asarray(zero, part.dtype), part.shape), x, identity
    )

    def hop(k, before):
        at = count - 1 - k if reverse else k
        reached = at > position if reverse else at < position
        new = combine(before, jax.tree.map(lambda part: part[at], everything))
        return jax.tree.map(lambda a, b: jnp.where(reached, a, b), new, before)

    return lax.fori_loop(0, count, hop, start)


def combine_states(earlier, later):
    return (earlier[0] + later[0], jnp.exp(later[0])[:, None, None] * earlier[1] + later[1])


def slice_forward(values, b_piece, c_piece, gram, log_decay, skip_piece, start_piece):
    cumulative = jnp.cumsum(log_decay, axis=0)
    tok_count = values.shape[0]
    row_ids = lax.broadcasted_iota(jnp.int32, (1, tok_count, tok_count), 1)
    col_ids = lax.broadcasted_iota(jnp.int32, (1, tok_count, tok_count), 2)
    diff = cumulative.T[:, :, None] - cumulative.T[:, None, :]
    weights = jnp.where(row_ids >= col_ids, jnp.exp(jnp.minimum(diff, 0.0)), 0.0) * gram[None]
    output = jnp.einsum("hts,shp->thp", weights, values)
    carried = jnp.exp(cumulative)[:, :, None] * jnp.einsum("tn,hnp->thp", c_piece, start_piece)
    output = output + carried + skip_piece[None, :, None] * values
    last_cum = cumulative[-1]
    tail = jnp.exp(last_cum[None, :] - cumulative)
    final_state = jnp.exp(last_cum)[:, None, None] * start_piece + jnp.einsum(
        "tn,th,thp->hnp", b_piece, tail, values
    )
    return (output, final_state)


def local(
    seq_values,
    proj_b,
    proj_c,
    time_step,
    decay_level,
    decay_rate,
    skip_gain,
    grad_out,
    layer_input,
    weight_c,
    moment_one,
    moment_two,
):
    tok_count = seq_values.shape[1]
    head_count = skip_gain.shape[0]
    group_count = proj_b.shape[2] // N
    per_group = head_count // group_count
    piece_heads = math.gcd(per_group, 4)
    piece_count = head_count // piece_heads
    pieces_group = piece_count // group_count
    level_count = decay_rate.shape[1]
    values = seq_values[0].astype(jnp.float32).reshape(tok_count, head_count, P_SIZE)
    cotangent = grad_out[0].astype(jnp.float32).reshape(tok_count, head_count, P_SIZE)
    b_rows = proj_b[0].astype(jnp.float32).reshape(tok_count, group_count, N)
    c_rows = proj_c[0].astype(jnp.float32).reshape(tok_count, group_count, N)
    span_len = tok_count // decay_level.shape[1]
    tok_level = jnp.repeat(decay_level[0], span_len, axis=0)
    level_ids = lax.broadcasted_iota(jnp.int32, (1, 1, level_count), 2)
    onehot = (tok_level[:, :, None] == level_ids).astype(jnp.float32)
    tok_rate = jnp.sum(onehot * decay_rate[None], axis=2)
    log_decay = -tok_rate * time_step[0]
    cumulative = jnp.cumsum(log_decay, axis=0)
    last_cum = cumulative[-1]
    b_heads = jnp.repeat(b_rows, per_group, axis=1)
    c_heads = jnp.repeat(c_rows, per_group, axis=1)
    local_state = jnp.einsum(
        "thn,th,thp->hnp", b_heads, jnp.exp(last_cum[None, :] - cumulative), values
    )
    local_grad = jnp.einsum("thn,th,thp->hnp", c_heads, jnp.exp(cumulative), cotangent)
    zero_state = jnp.zeros_like(local_state)
    zero_total = jnp.zeros_like(last_cum)
    start_state = carried_in(
        (last_cum, local_state), "seq", combine_states, (zero_total, zero_state), False
    )[1]
    end_grad = carried_in(
        (last_cum, local_grad), "seq", combine_states, (zero_total, zero_state), True
    )[1]
    gram_all = jnp.einsum("tgn,sgn->gts", c_rows, b_rows)

    def arrange(array):
        return jnp.moveaxis(
            array.reshape((tok_count, piece_count, piece_heads) + array.shape[2:]), 1, 0
        )

    group_of = lax.iota(jnp.int32, piece_count) * piece_heads // per_group

    def slice_grads(packed):
        x_piece, dy_piece, decay_piece, skip_piece, state_piece, grad_piece, group_index = packed
        b_piece = lax.dynamic_index_in_dim(b_rows, group_index, 1, keepdims=False)
        c_piece = lax.dynamic_index_in_dim(c_rows, group_index, 1, keepdims=False)
        gram_piece = lax.dynamic_index_in_dim(gram_all, group_index, 0, keepdims=False)
        _, pullback = jax.vjp(
            slice_forward,
            x_piece,
            b_piece,
            c_piece,
            gram_piece,
            decay_piece,
            skip_piece,
            state_piece,
        )
        return pullback((dy_piece, grad_piece))[:6]

    state_shape = (piece_count, piece_heads, N, P_SIZE)
    d_values, d_b, d_c, d_gram, d_decay, d_skip = lax.map(
        slice_grads,
        (
            arrange(values),
            arrange(cotangent),
            arrange(log_decay),
            skip_gain.reshape(piece_count, piece_heads),
            start_state.reshape(state_shape),
            end_grad.reshape(state_shape),
            group_of,
        ),
    )
    d_b_group = jnp.sum(d_b.reshape(group_count, pieces_group, tok_count, N), axis=1)
    d_c_group = jnp.sum(d_c.reshape(group_count, pieces_group, tok_count, N), axis=1)
    d_gram_group = jnp.sum(d_gram.reshape(group_count, pieces_group, tok_count, tok_count), axis=1)
    b_total = jnp.moveaxis(d_b_group, 0, 1) + jnp.einsum("gts,tgn->sgn", d_gram_group, c_rows)
    c_total = jnp.moveaxis(d_c_group, 0, 1) + jnp.einsum("gts,sgn->tgn", d_gram_group, b_rows)
    grad_values = (
        jnp.moveaxis(d_values, 0, 1).reshape(tok_count, head_count * P_SIZE).astype(jnp.bfloat16)
    )
    grad_b = b_total.reshape(tok_count, group_count * N).astype(jnp.bfloat16)
    grad_rows = c_total.reshape(tok_count, group_count * N).astype(jnp.bfloat16)
    decay_grad = jnp.moveaxis(d_decay, 0, 1).reshape(tok_count, head_count)
    lograte_local = jnp.sum(onehot * (decay_grad * log_decay)[:, :, None], axis=0)
    skip_local = d_skip.reshape(head_count)
    grad_lograte, grad_skip = lax.psum((lograte_local, skip_local), ("seq", "dp"))
    features = lax.all_gather(layer_input[0], "tensor", axis=1, tiled=True)
    seq_part = lax.psum_scatter(
        lax.dot_general(
            features, grad_rows, (((0,), (0,)), ((), ())), preferred_element_type=jnp.float32
        ).astype(jnp.bfloat16),
        "seq",
        scatter_dimension=0,
        tiled=True,
    )
    grad_shard = lax.psum_scatter(seq_part, "dp", scatter_dimension=0, tiled=True).astype(
        jnp.float32
    )
    square_total = lax.psum(jnp.sum(grad_shard * grad_shard), ("seq", "tensor", "dp"))
    limit = 0.25 * math.sqrt(D * G * N)
    clipped = grad_shard * (limit / jnp.maximum(jnp.sqrt(square_total), limit))
    new_moment = beta_one * moment_one + (1.0 - beta_one) * clipped
    new_second = beta_two * moment_two + (1.0 - beta_two) * clipped * clipped
    direction = (
        new_moment
        / (1.0 - beta_one**step_count)
        / (jnp.sqrt(new_second / (1.0 - beta_two**step_count)) + adam_eps)
    )
    new_weight = weight_c - learn_rate * (direction + decay_weight * weight_c)
    return (
        grad_values[None],
        grad_b[None],
        grad_rows[None],
        grad_lograte,
        grad_skip,
        new_weight,
        new_moment,
        new_second,
    )


def solution(mesh):
    placed = (
        P("dp", "seq", "tensor"),
        P("dp", "seq", "tensor"),
        P("dp", "seq", "tensor"),
        P("dp", "seq", "tensor"),
        P("dp", "seq", "tensor"),
        P("tensor", None),
        P("tensor"),
        P("dp", "seq", "tensor"),
        P("dp", "seq", "tensor"),
        P(("seq", "dp"), "tensor"),
        P(("seq", "dp"), "tensor"),
        P(("seq", "dp"), "tensor"),
    )
    return jax.shard_map(
        local,
        mesh=mesh,
        in_specs=placed,
        out_specs=(
            P("dp", "seq", "tensor"),
            P("dp", "seq", "tensor"),
            P("dp", "seq", "tensor"),
            P("tensor", None),
            P("tensor"),
            P(("seq", "dp"), "tensor"),
            P(("seq", "dp"), "tensor"),
            P(("seq", "dp"), "tensor"),
        ),
        check_vma=False,
    )
```

profile of v0, /device:TPU:1, one launch (start us, length us, event | category | flops | bytes accessed | tf_op | source)
XLA Modules:
  0.0 1271.7 jit_solution(3410172349455850983)
XLA Ops:
  18.3 30.4 %all-gather.3 = f32[16,1,32]{2,1,0:T(1,128)S(1)} all-gather(f32[1,1,32]{2,1,0:T(1,128)S(1)} %get-tuple-element.675), channel_id=1, replica_groups=mesh['seq'=16,'tensor'=4,'dp'=8] {'seq'}, dimensions={0}, use_global_device_ids=true | all-gather | bytes 2176 | tf_op jit(solution)/shard_map/all_gather | solution.py:24
  50.0 159.5 %all-gather.8.cloned.1.call-done = f32[512,128,64]{1,2,0:T(8,128)} async-done(((f32[32,128,64]{1,2,0:T(8,128)}), f32[512,128,64]{1,2,0:T(8,128)}) %all-gather.8.cloned.1.call-update) | async-done | bytes 16777232 | tf_op jit(solution)/shard_map/all_gather | solution.py:24
  209.5 81.6 %while.52 = (s32[]{:T(128)}, f32[32,128,64]{2,1,0:T(8,128)}, s32[]{:T(128)}, f32[16,32]{1,0:T(8,128)S(1)}, f32[16,32,128,64]{2,3,1,0:T(8,128)}, /*index=5*/s32[]{:T(128)}, s32[]{:T(128)}, s32[]{:T(128)}, s32[]{:T(128)}) while((s32[]{:T(128)}, f32[32,128,64]{2,1,0:T(8,128)}, s32[]{:T(128)}, f32[16,32]{1,0:T(8,128)S(1)}, ...), condition=%wide.region_5.6_spmd.clone, body=%wide.region_4.5_spmd.clone.sunk | while | flops 1048584 | bytes 7340583 | solution.py:35
  225.3 3.4 fusion.121
  294.2 105.5 %all-gather.10.cloned.1.call-done = f32[512,128,64]{1,2,0:T(8,128)} async-done(((f32[32,128,64]{1,2,0:T(8,128)}), f32[512,128,64]{1,2,0:T(8,128)}) %all-gather.10.cloned.1.call-update) | async-done | bytes 16777232 | tf_op jit(solution)/shard_map/all_gather | solution.py:24
  399.7 82.2 %while.53 = (s32[]{:T(128)}, f32[32,128,64]{2,1,0:T(8,128)}, s32[]{:T(128)}, f32[16,32]{1,0:T(8,128)S(1)}, f32[16,32,128,64]{2,3,1,0:T(8,128)}, /*index=5*/s32[]{:T(128)}, s32[]{:T(128)}) while((s32[]{:T(128)}, f32[32,128,64]{2,1,0:T(8,128)}, s32[]{:T(128)}, f32[16,32]{1,0:T(8,128)S(1)}, f32[16,32,128,64]{2,3,1,0:T(8,128)}, ...), condition=%wide.region_3.4_spmd.clone, body=%wide.region_2.3_spmd.clone.sunk | while | flops 1048580 | bytes 7340521 | solution.py:35
  405.3 3.3 fusion.122
  410.5 3.3 fusion.122
  415.7 3.4 fusion.122
  421.1 3.3 fusion.122
  426.3 3.3 fusion.122
  431.6 3.3 fusion.122
  436.8 3.3 fusion.122
  442.0 3.3 fusion.122
  447.3 3.3 fusion.122
  452.5 3.3 fusion.122
  457.7 3.3 fusion.122
  462.9 3.3 fusion.122
  468.2 3.3 fusion.122
  484.3 105.7 %while.51 = (s32[]{:T(128)}, bf16[8,128,4,64]{1,3,2,0:T(8,128)(2,1)S(1)}, f32[8,128,128]{2,1,0:T(8,128)}, f32[8,128,128]{2,1,0:T(8,128)}, f32[8,128,128]{2,1,0:T...) while((s32[]{:T(128)}, ...), condition=%wide.region_16.17_spmd, body=%wide.region_6.16_spmd.sunk | while | flops 52169212 | bytes 2763313 | solution.py:135
  591.3 3.7 fusion.60
  596.2 59.9 %reduce-scatter.5.cloned.1.call-done = bf16[512,128]{0,1:T(8,128)(2,1)} async-done(((bf16[8192,128]{0,1:T(8,128)(2,1)}), bf16[512,128]{0,1:T(8,128)(2,1)}) %reduce-scatter.5.cloned.1.call-update) | async-done | bytes 131088 | tf_op jit(solution)/shard_map/reduce_scatter | solution.py:162
  658.1 496.3 %all-reduce.1 = (f32[32,8]{1,0:T(8,128)S(1)}, f32[32]{0:T(128)}) all-reduce(f32[32,8]{1,0:T(8,128)S(1)} %select_reduce_fusion, f32[32]{0:T(128)S(1)} %reshape.232), channel_id=1, replica_groups=mesh['seq'=16,'tensor'=4,'dp'=8] {'seq','dp'}, use_global_device_ids=true, to_apply=%region_21.22 | all-reduce | flops 288 | bytes 2304 | tf_op jit(solution)/shard_map/psum | solution.py:160
  1158.2 104.8 %psum.23 = f32[]{:T(128)} all-reduce(f32[]{:T(128)} %fusion.75), channel_id=1, replica_groups=mesh['seq'=16,'tensor'=4,'dp'=8] {'seq','tensor','dp'}, use_global_device_ids=true, to_apply=%region_26.27 | all-reduce | flops 1 | bytes 8 | tf_op jit(solution)/shard_map/psum | solution.py:173
  (440 shorter events, 248.9 us)
Async XLA Ops:
  7.2 5.1 copy-start.4
  7.2 202.3 %all-gather.8.cloned.1.call-start = ((), (), s32[]{:S(2)}) async-start(), calls=%async_computation.3 | async-start | bytes 17825792 | tf_op jit(solution)/shard_map/all_gather | solution.py:24
  9.5 1.8 copy-start.11
  11.2 2.6 copy-start.6
  13.8 385.9 %all-gather.10.cloned.1.call-start = ((), (), s32[]{:S(2)}) async-start(), calls=%async_computation.4 | async-start | bytes 17825792 | tf_op jit(solution)/shard_map/all_gather | solution.py:24
  14.2 34.4 %copy-start.21 = (f32[32]{0:T(128)S(1)}, f32[32]{0:T(128)}, u32[]{:S(2)}) copy-start(f32[32]{0:T(128)} %param.24) | copy-start | bytes 388
  14.3 35.1 %copy-start.14 = (f32[1,128,32]{1,2,0:T(8,128)S(1)}, f32[1,128,32]{1,2,0:T(8,128)}, u32[]{:S(2)}) copy-start(f32[1,128,32]{1,2,0:T(8,128)} %param.21) | copy-start | bytes 49156
  16.6 574.6 %all-gather.12.cloned.1.call-start = ((), (), s32[]{:S(2)}) async-start(), calls=%async_computation.5 | async-start | bytes 2621440 | tf_op jit(solution)/shard_map/all_gather | solution.py:161
  17.4 638.7 %reduce-scatter.5.cloned.1.call-start = ((), (), s32[]{:S(2)}) async-start(), calls=%async_computation.2 | async-start | bytes 2228224 | tf_op jit(solution)/shard_map/reduce_scatter | solution.py:162
  481.9 2.3 copy-start.1
  481.9 2.3 copy-start.5
  481.9 2.4 copy-start.7
  488.3 1.6 copy-start.10
  501.5 1.6 copy-start.10
  514.7 1.6 copy-start.10
  541.1 1.6 copy-start.10
  591.2 3.7 copy-start.13
  595.0 62.8 %copy-start.20 = (s32[1,1,32]{2,1,0:T(1,128)S(1)}, s32[1,1,32]{2,1,0:T(1,128)}, u32[]{:S(2)}) copy-start(s32[1,1,32]{2,1,0:T(1,128)} %param.22) | copy-start | bytes 388
  595.0 63.0 %copy-start.19 = (f32[8,4]{1,0:T(8,128)S(1)}, f32[8,4]{1,0:T(8,128)}, u32[]{:S(2)}) copy-start(f32[8,4]{1,0:T(8,128)} %get-tuple-element.364) | copy-start | bytes 388
  595.0 560.1 %copy-start.8 = (f32[8,128,128]{2,1,0:T(8,128)S(1)}, f32[8,128,128]{2,1,0:T(8,128)}, u32[]{:S(2)}) copy-start(f32[8,128,128]{2,1,0:T(8,128)} %get-tuple-element.360) | copy-start | bytes 1572868
  595.0 668.8 %copy-start.16 = (f32[64,128]{1,0:T(8,128)S(1)}, f32[64,128]{1,0:T(8,128)}, u32[]{:S(2)}) copy-start(f32[64,128]{1,0:T(8,128)} %param.27) | copy-start | bytes 98308
  595.0 668.8 %copy-start.17 = (f32[64,128]{1,0:T(8,128)S(1)}, f32[64,128]{1,0:T(8,128)}, u32[]{:S(2)}) copy-start(f32[64,128]{1,0:T(8,128)} %param.28) | copy-start | bytes 98308
  595.0 668.8 %copy-start.18 = (f32[64,128]{1,0:T(8,128)S(1)}, f32[64,128]{1,0:T(8,128)}, u32[]{:S(2)}) copy-start(f32[64,128]{1,0:T(8,128)} %param.29) | copy-start | bytes 98308
  595.0 560.9 %reduce-scatter.7.cloned.1.call-start = ((), (), s32[]{:S(2)}) async-start(), calls=%async_computation.6 | async-start | bytes 147456 | tf_op jit(solution)/shard_map/reduce_scatter | solution.py:170
  (17 other events, 23.0 us)
Sparse Core Ops, SparseCore 0:
  13.9 195.5 all-gather.7
  211.5 188.0 all-gather.9
  401.8 36.4 all-gather.11
  595.2 60.8 reduce-scatter.4
  659.3 44.5 reduce-scatter.6
where the time goes:
time: 1280 us; the launch traced here: 1270 us
  blocking collectives  632 us (49%)
  waiting for transfers between devices  326 us (25%)
  other arithmetic  130 us (10%)
  local copies, waits for them, and re-layouts  109 us (9%)
  matrix products  59.2 us (5%)
  between operations  14.8 us (1%)
    psum x1, blocking collectives, local(): lax.psum((lograte_local, skip_local), ('seq', 'dp'))  496 us
    all_gather x2, waiting for transfers between devices, carried_in(): everything = jax.tree.map(lambda part: lax.all_gather(part, axis), x)  265 us
    psum x1, blocking collectives, local(): lax.psum(jnp.sum(grad_shard * grad_shard), ('seq', 'tensor', 'dp'))  105 us
    select_n x32, other arithmetic, hop(): return jax.tree.map(lambda a, b: jnp.where(reached, a, b), new, before)  102 us
    dynamic_slice x64, local copies, waits for them, and re-layouts, hop(): new = combine(before, jax.tree.map(lambda part: part[at], everything))  60.9 us
    reduce_scatter x1, waiting for transfers between devices, local(): lax.psum_scatter(lax.dot_general(features, grad_rows, (((0,), (0,)), ((),...  59.9 us
    all_gather x1, blocking collectives, carried_in(): everything = jax.tree.map(lambda part: lax.all_gather(part, axis), x)  30.4 us
  transfers between devices with their start and end apart: 5, of which 3 were waited for; matrix products, arithmetic and copies ran while one was open for 22% of the time, Pallas kernels for 0%

commit v1 on v0

v1 whole, which is shorter than its diff:
```python
import math

import jax
import jax.numpy as jnp
from jax import lax
from jax.experimental import pallas as pl
from jax.experimental.pallas import tpu as pltpu
from jax.sharding import PartitionSpec as P

P_SIZE = 64
N = 128
SPAN = 128
PAIR = 2 * P_SIZE
LOG_ROWS = 16

beta_one = 0.9
beta_two = 0.95
adam_eps = 1e-08
learn_rate = 0.02
decay_weight = 0.1
step_count = 10

f32 = jnp.float32
bf16 = jnp.bfloat16
HIGHEST = lax.Precision.HIGHEST


def iota(shape, dim):
    return lax.broadcasted_iota(jnp.int32, shape, dim)


def dot(a, b):
    return jnp.dot(a, b, preferred_element_type=f32)


def dot_nt(a, b):
    return lax.dot_general(a, b, (((1,), (1,)), ((), ())), preferred_element_type=f32)


def first_head():
    return iota((SPAN, PAIR), 1) < P_SIZE


def spread(cols, j, first):
    return jnp.where(
        first[: cols.shape[0]], cols[:, 2 * j : 2 * j + 1], cols[:, 2 * j + 1 : 2 * j + 2]
    )


def states_kernel(dt, lev, rate_t, x, dy, b, c, st, xt, dye, loga, cum, onehot):
    heads = dt.shape[1]
    levels = rate_t.shape[0]
    hit = iota((levels, heads), 0) == lev[...]
    rate = jnp.sum(jnp.where(hit, rate_t[...], 0.0), axis=0, keepdims=True)
    onehot[...] = jnp.zeros_like(onehot)
    onehot[:, :heads] = jnp.where(hit, 1.0, 0.0)
    loga[...] = jnp.zeros_like(loga)
    loga[:, :heads] = -rate * dt[...]
    lower = (iota((SPAN, SPAN), 0) >= iota((SPAN, SPAN), 1)).astype(f32)
    total = jnp.dot(lower, loga[...], precision=HIGHEST, preferred_element_type=f32)
    cum[...] = total
    last = total[SPAN - 1 :, :]
    tail = jnp.exp(last - total)
    grow = jnp.exp(total)
    b_t = b[...].astype(f32).T.astype(bf16)
    c_t = c[...].astype(f32).T.astype(bf16)
    first = first_head()
    row = iota((LOG_ROWS, PAIR), 0)
    heads_piece = PAIR // P_SIZE * (heads // 2) // st.shape[0]
    for j in range(heads // 2):
        piece, at = 2 * j // heads_piece, (2 * j % heads_piece) // 2 * PAIR
        lanes = slice(j * PAIR, (j + 1) * PAIR)
        spot = slice(at, at + PAIR)
        xs = (x[:, lanes].astype(f32) * spread(tail, j, first)).astype(bf16)
        ds = (dy[:, lanes].astype(f32) * spread(grow, j, first)).astype(bf16)
        xt[:, lanes] = xs
        dye[:, lanes] = ds
        st[piece, :N, spot] = dot(b_t, xs).astype(bf16)
        st[piece, N : 2 * N, spot] = dot(c_t, ds).astype(bf16)
        whole = spread(last, j, first)
        high = whole.astype(bf16).astype(f32)
        middle = (whole - high).astype(bf16).astype(f32)
        low = whole - high - middle
        st[piece, 2 * N :, spot] = jnp.where(
            row == 0, high, jnp.where(row == 1, middle, jnp.where(row == 2, low, 0.0))
        ).astype(bf16)


def scan_kernel(got, starts, ends):
    count = got.shape[0]
    decay = []
    for k in range(count):
        logs = got[k, 2 * N :, :].astype(f32)
        decay.append(jnp.exp(logs[0:1] + logs[1:2] + logs[2:3]))
    state = jnp.zeros((N, got.shape[2]), f32)
    for k in range(count):
        starts[k] = state.astype(bf16)
        state = decay[k] * state + got[k, :N, :].astype(f32)
    state = jnp.zeros((N, got.shape[2]), f32)
    for k in reversed(range(count)):
        ends[k] = state.astype(bf16)
        state = decay[k] * state + got[k, N : 2 * N, :].astype(f32)


def intra_kernel(cum, x, dy, b, c, skip, dxp, dc, db, dcum, rows):
    heads = skip.shape[1]
    total = cum[...]
    total_t = total.T
    keep = iota((SPAN, SPAN), 1) >= iota((SPAN, SPAN), 0)
    lane = iota((SPAN, SPAN), 1)
    first = first_head()
    gain = skip[...]
    mask_a = jnp.where(first, 1.0, 0.0).astype(bf16)
    mask_b = jnp.where(first, 0.0, 1.0).astype(bf16)
    gram_t = dot_nt(b[...], c[...])
    dgram_t = jnp.zeros((SPAN, SPAN), f32)
    columns = jnp.zeros((SPAN, SPAN), f32)
    rows[...] = jnp.zeros_like(rows)
    for j in range(heads // 2):
        lanes = slice(j * PAIR, (j + 1) * PAIR)
        x_pair, dy_pair = x[:, lanes], dy[:, lanes]
        x_two = jnp.concatenate([x_pair * mask_a, x_pair * mask_b], axis=0)
        dy_two = jnp.concatenate([dy_pair * mask_a, dy_pair * mask_b], axis=0)
        dm_two = dot_nt(x_two, dy_pair)
        mixes = []
        for k in range(2):
            h = 2 * j + k
            dm = dm_two[k * SPAN : (k + 1) * SPAN]
            diff = total_t[h : h + 1, :] - total[:, h : h + 1]
            w = jnp.exp(jnp.where(keep, jnp.minimum(diff, 0.0), -1e30))
            wd = w * dm
            dgram_t = dgram_t + wd
            q = wd * gram_t
            columns = jnp.where(lane == h, jnp.sum(q, axis=1, keepdims=True), columns)
            rows[h : h + 1, :] = jnp.sum(q, axis=0, keepdims=True)
            mixes.append((w * gram_t).astype(bf16))
        dx = dot(jnp.concatenate(mixes, axis=1), dy_two)
        dxp[:, lanes] = dx + spread(gain, j, first) * dy_pair.astype(f32)
    dcum[...] = rows[...].T - columns
    high = dgram_t.astype(bf16)
    dc[...] = dot(high.astype(f32).T.astype(bf16), b[...])
    db[...] = dot(high, c[...])


def grad_c_kernel(dc, dye, starts, grad_c, copies):
    total = dc[...]
    pieces, width = starts.shape[0], starts.shape[2]
    for j in range(pieces):
        total = total + dot_nt(dye[:, j * width : (j + 1) * width], starts[j])
    out = total.astype(bf16)
    grad_c[...] = out
    for k in range(copies.shape[0]):
        copies[k] = out


def halves(a):
    high = a.astype(bf16)
    return high, (a - high.astype(f32)).astype(bf16)


def rest_kernel(
    starts, ends, x, dy, xt, dye, cum, loga, onehot, b, c, dxp, db, dcum, grad_x, grad_b, small
):
    heads = x.shape[1] // P_SIZE
    pairs_piece = starts.shape[2] // PAIR
    total = cum[...]
    last = total[SPAN - 1 :, :]
    tail = jnp.exp(last - total)
    end = jnp.exp(last)
    first = first_head()
    row = iota((SPAN, PAIR), 0)
    lane_head = iota((PAIR, 128), 0) // P_SIZE
    column = iota((PAIR, 128), 1)
    b_total = db[...]
    d_total = dcum[...]
    skips = jnp.zeros((8, 128), f32)
    for j in range(heads // 2):
        piece, at = j // pairs_piece, j % pairs_piece * PAIR
        lanes = slice(j * PAIR, (j + 1) * PAIR)
        start, stop = starts[piece, :, at : at + PAIR], ends[piece, :, at : at + PAIR]
        xs = xt[:, lanes]
        carried = dye[:, lanes].astype(f32) * dot(c[...], start)
        back = dot(b[...], stop)
        left = xs.astype(f32) * back
        grad_x[:, lanes] = (dxp[:, lanes] + spread(tail, j, first) * back).astype(bf16)
        b_total = b_total + dot_nt(xs, stop)
        at_end = jnp.sum(left, axis=0, keepdims=True) + spread(end, j, first) * jnp.sum(
            start.astype(f32) * stop.astype(f32), axis=0, keepdims=True
        )
        moved = carried - left + jnp.where(row == SPAN - 1, at_end, 0.0)
        skip = jnp.sum(x[:, lanes].astype(f32) * dy[:, lanes].astype(f32), axis=0, keepdims=True)
        skip = jnp.broadcast_to(skip, (8, PAIR))
        to_head = jnp.where(column == 2 * j + lane_head, 1.0, 0.0).astype(bf16)
        to_skip = jnp.where(column == heads + 2 * j + lane_head, 1.0, 0.0).astype(bf16)
        high, low = halves(moved)
        d_total = d_total + dot(high, to_head) + dot(low, to_head)
        high, low = halves(skip)
        skips = skips + dot(high, to_skip) + dot(low, to_skip)
    grad_b[...] = b_total.astype(bf16)
    upper = (iota((SPAN, SPAN), 1) >= iota((SPAN, SPAN), 0)).astype(f32)
    dlog = jnp.dot(upper, d_total, precision=HIGHEST, preferred_element_type=f32)
    rates = jnp.sum(dlog * loga[...], axis=0, keepdims=True)
    small[...] = onehot[...] * rates + jnp.where(iota((8, 128), 0) == 0, skips, 0.0)


def shard_kernel(parts, small, shard, copies):
    total = jnp.sum(parts[...].astype(f32), axis=0)
    shard[...] = total
    square = jnp.sum(total * total)
    here = (iota((8, 128), 0) == 0) & (iota((8, 128), 1) == 127)
    out = small[...] + jnp.where(here, square, 0.0)
    for k in range(copies.shape[0]):
        copies[k] = out


def call(kernel, out_shapes, *args, scratch=(), flops=0):
    size = sum(math.prod(a.shape) * a.dtype.itemsize for a in (*args, *out_shapes))
    return pl.pallas_call(
        kernel,
        out_shape=tuple(out_shapes),
        scratch_shapes=list(scratch),
        compiler_params=pltpu.CompilerParams(vmem_limit_bytes=48 * 1024 * 1024),
        cost_estimate=pl.CostEstimate(flops=flops, bytes_accessed=size, transcendentals=0),
    )(*args)


def shaped(shape, dtype):
    return jax.ShapeDtypeStruct(shape, dtype)


def swap(a, axis):
    return lax.all_to_all(a, axis, 0, 0, tiled=True)


def local(
    seq_values,
    proj_b,
    proj_c,
    time_step,
    decay_level,
    decay_rate,
    skip_gain,
    grad_out,
    layer_input,
    weight_c,
    moment_one,
    moment_two,
):
    seqs, streams, tensors = (lax.axis_size(a) for a in ("seq", "dp", "tensor"))
    x, dy, b, c = seq_values[0], grad_out[0], proj_b[0], proj_c[0]
    heads = skip_gain.shape[0]
    width = heads * P_SIZE
    piece = width // seqs
    tile = shaped((SPAN, 128), f32)
    wide = shaped((SPAN, width), bf16)
    st, xt, dye, loga, cum, onehot = call(
        states_kernel,
        [shaped((seqs, 2 * N + LOG_ROWS, piece), bf16), wide, wide, tile, tile, shaped((8, 128), f32)],
        time_step[0],
        decay_level[0],
        decay_rate.T,
        x,
        dy,
        b,
        c,
        flops=4 * SPAN * N * width,
    )
    got = swap(st, "seq")

    rows = weight_c.shape[0]
    per_tensor = layer_input.shape[2] // (streams * rows)
    features = jnp.transpose(
        layer_input[0].reshape(SPAN, per_tensor, streams, rows), (2, 0, 1, 3)
    ).reshape(streams, SPAN, per_tensor * rows)
    features = lax.all_gather(swap(features, "dp"), "tensor", axis=0)
    features = features.reshape(tensors, streams * SPAN, per_tensor * rows)

    dxp, dc, db, dcum = call(
        intra_kernel,
        [shaped((SPAN, width), f32), tile, tile, tile],
        cum,
        x,
        dy,
        b,
        c,
        skip_gain[None],
        scratch=[pltpu.VMEM((SPAN, SPAN), f32)],
        flops=20 * SPAN * SPAN * width,
    )
    state = shaped((seqs, N, piece), bf16)
    starts, ends = call(scan_kernel, [state, state], got, flops=8 * N * width)
    starts = swap(starts, "seq")
    ends = swap(ends, "seq")
    grad_c, copies = call(
        grad_c_kernel,
        [shaped((SPAN, N), bf16), shaped((streams, SPAN, N), bf16)],
        dc,
        dye,
        starts,
        flops=2 * SPAN * N * width,
    )
    all_c = swap(copies, "dp").reshape(streams * SPAN, N)
    partial = lax.dot_general(
        features, all_c, (((1,), (0,)), ((), ())), preferred_element_type=f32
    ).astype(bf16)
    parts = swap(partial.reshape(seqs, rows, N), "seq")
    grad_x, grad_b, small = call(
        rest_kernel,
        [shaped((SPAN, width), bf16), shaped((SPAN, N), bf16), shaped((8, 128), f32)],
        starts,
        ends,
        x,
        dy,
        xt,
        dye,
        cum,
        loga,
        onehot,
        b,
        c,
        dxp,
        db,
        dcum,
        flops=6 * SPAN * N * width,
    )
    shard, sums = call(
        shard_kernel,
        [shaped((rows, N), f32), shaped((seqs, 8, 128), f32)],
        parts,
        small,
        flops=seqs * rows * N,
    )
    sums = jnp.sum(swap(sums, "seq"), axis=0)
    sums = jnp.sum(swap(jnp.broadcast_to(sums[None], (streams, 8, 128)), "dp"), axis=0)
    squares = jnp.broadcast_to(sums[None], (tensors, 8, 128))
    square_total = jnp.sum(swap(squares, "tensor")[:, 0, 127])
    levels = decay_rate.shape[1]
    grad_lograte = sums[:levels, :heads].T
    grad_skip = sums[0, heads : 2 * heads]

    dim = weight_c.shape[0] * seqs * streams * weight_c.shape[1] * tensors
    limit = 0.25 * math.sqrt(dim)
    clipped = shard * (limit / jnp.maximum(jnp.sqrt(square_total), limit))
    new_moment = beta_one * moment_one + (1.0 - beta_one) * clipped
    new_second = beta_two * moment_two + (1.0 - beta_two) * clipped * clipped
    direction = (
        new_moment
        / (1.0 - beta_one**step_count)
        / (jnp.sqrt(new_second / (1.0 - beta_two**step_count)) + adam_eps)
    )
    new_weight = weight_c - learn_rate * (direction + decay_weight * weight_c)
    return (
        grad_x[None],
        grad_b[None],
        grad_c[None],
        grad_lograte,
        grad_skip,
        new_weight,
        new_moment,
        new_second,
    )


def solution(mesh):
    wide = P("dp", "seq", "tensor")
    shard = P(("seq", "dp"), "tensor")
    return jax.shard_map(
        local,
        mesh=mesh,
        in_specs=(
            wide,
            wide,
            wide,
            wide,
            wide,
            P("tensor", None),
            P("tensor"),
            wide,
            wide,
            shard,
            shard,
            shard,
        ),
        out_specs=(wide, wide, wide, P("tensor", None), P("tensor"), shard, shard, shard),
        check_vma=False,
    )
```

time: 1280 us -> 255 us (0.20)
  blocking collectives: 632 us -> 48.6 us
  waiting for transfers between devices: 326 us -> 96.3 us
  other arithmetic: 130 us -> 2.15 us
  local copies, waits for them, and re-layouts: 109 us -> 19.5 us
  starting transfers between devices: 0.2 us -> 56.7 us
  matrix products: 59.2 us -> 2.93 us
    psum x2 -> x0, blocking collectives: 601 us -> none  [the longest x1 496 us: local(): lax.psum((lograte_local, skip_local), ('seq', 'dp'))]
    all_gather x3 -> x1, waiting for transfers between devices: 265 us -> 0.02 us  [local(): features = lax.all_gather(swap(features, 'dp'), 'tensor', axis=0)]
    select_n x32 -> x0, other arithmetic: 102 us -> none  [hop(): return jax.tree.map(lambda a, b: jnp.where(reached, a, b), new, before)]
    all_to_all x0 -> x6, waiting for transfers between devices: none -> 96.3 us  [swap(): return lax.all_to_all(a, axis, 0, 0, tiled=True)]
    dynamic_slice x80 -> x0, local copies, waits for them, and re-layouts: 67.3 us -> none  [the longest x64 60.9 us: hop(): new = combine(before, jax.tree.map(lambda part: part[at], everything))]
    reduce_scatter x2 -> x0, waiting for transfers between devices: 59.9 us -> none  [the longest x1 59.9 us: local(): lax.psum_scatter(lax.dot_general(features, grad_rows, (((0,), (0,)), ((),...]
    all_to_all x0 -> x6, starting transfers between devices: none -> 56.7 us  [swap(): return lax.all_to_all(a, axis, 0, 0, tiled=True)]
    dot_general x54 -> x1, matrix products: 59.2 us -> 2.93 us  [local(): lax.dot_general(features, all_c, (((1,), (0,)), ((), ())), preferred_elem...]
  transfers between devices with their start and end apart: 5 -> 7, of which waited for: 3 -> 6; matrix products, arithmetic and copies ran while one was open for 22% -> 3% of each run, Pallas kernels for 0% -> 4%
where the time goes in v1:
time: 255 us; the launch traced here: 254 us
  waiting for transfers between devices  96.3 us (38%)
  starting transfers between devices  56.7 us (22%)
  blocking collectives  48.6 us (19%)
  local copies, waits for them, and re-layouts  19.5 us (8%)
  between operations  15 us (6%)
  Pallas kernels  12.5 us (5%)
  matrix products  2.93 us (1%)
    all_to_all x6, waiting for transfers between devices, swap(): return lax.all_to_all(a, axis, 0, 0, tiled=True)  96.3 us
    all_to_all x6, starting transfers between devices, swap(): return lax.all_to_all(a, axis, 0, 0, tiled=True)  56.7 us
    all_to_all x3, blocking collectives, swap(): return lax.all_to_all(a, axis, 0, 0, tiled=True)  48.6 us
    unnamed x48, local copies, waits for them, and re-layouts  13 us
    pallas_call x6, Pallas kernels, call(): pl.pallas_call(kernel, out_shape=tuple(out_shapes), scratch_shapes=list(s...  12.5 us
  transfers between devices with their start and end apart: 7, of which 6 were waited for; matrix products, arithmetic and copies ran while one was open for 3% of the time, Pallas kernels for 4%

profile of v1, /device:TPU:1, one launch (start us, length us, event | category | flops | bytes accessed | tf_op | source)
XLA Modules:
  0.0 253.6 jit_solution(5474391932983591500)
XLA Ops:
  12.9 2.8 %shard_map.179 = (bf16[16,272,128]{2,1,0:T(8,128)(2,1)}, bf16[128,2048]{1,0:T(8,128)(2,1)S(1)}, bf16[128,2048]{1,0:T(8,128)(2,1)S(1)}, f32[128,128]{1,0:T(8,128)...) custom-call(f32[128,32]{1,0:T(8,128)S(1)} %bitcast.40, s32[1,32]{1,0:T(1,128)S(1)} %bitcast.48, f32[8,32]{1,0:T(8,128)S(1)} %bitcast.47, ...), custom_call_target="tpu_custom_call" | custom-call | flops 134217728 | bytes 3429504 | tf_op jit(solution)/shard_map/pallas_call | solution.py:218
  16.6 15.9 %all-to-all-start = ((bf16[16,272,128]{2,1,0:T(8,128)(2,1)}), bf16[16,272,128]{2,1,0:T(8,128)(2,1)S(1)}, u32[]{:S(2)}, u32[]{:S(2)}) async-start(bf16[16,272,128]{2,1,0:T(8,128)(2,1)} %get-tuple-element.27), calls=%async_computation | async-start | bytes 2228224 | tf_op jit(solution)/shard_map/all_to_all | solution.py:232
  33.6 46.1 %all-to-all-done.got = bf16[16,272,128]{2,1,0:T(8,128)(2,1)S(1)} async-done(((bf16[16,272,128]{2,1,0:T(8,128)(2,1)}), bf16[16,272,128]{2,1,0:T(8,128)(2,1)S(1)}, u32[]{:S(2)}, u32[]{:S(2)}) %all-to-all-start) | async-done | bytes 1114144 | tf_op jit(solution)/shard_map/all_to_all | solution.py:232
  79.7 10.6 %all-to-all-start.4 = ((bf16[8,128,256]{1,2,0:T(8,128)(2,1)}), bf16[8,128,256]{1,2,0:T(8,128)(2,1)}, u32[]{:S(2)}, u32[]{:S(2)}) async-start(bf16[8,128,256]{1,2,0:T(8,128)(2,1)} %bitcast.14), calls=%async_computation.4 | async-start | bytes 1048576 | tf_op jit(solution)/shard_map/all_to_all | solution.py:232
  92.1 7.8 %all-to-all-done.4 = bf16[8,128,256]{1,2,0:T(8,128)(2,1)} async-done(((bf16[8,128,256]{1,2,0:T(8,128)(2,1)}), bf16[8,128,256]{1,2,0:T(8,128)(2,1)}, u32[]{:S(2)}, u32[]{:S(2)}) %all-to-all-start.4) | async-done | bytes 524320 | tf_op jit(solution)/shard_map/all_to_all | solution.py:232
  99.8 7.8 %all-to-all-start.1 = ((bf16[16,128,128]{2,1,0:T(8,128)(2,1)}), bf16[16,128,128]{2,1,0:T(8,128)(2,1)S(1)}, u32[]{:S(2)}, u32[]{:S(2)}) async-start(bf16[16,128,128]{2,1,0:T(8,128)(2,1)} %copy-done.8), calls=%async_computation.1 | async-start | bytes 1048576 | tf_op jit(solution)/shard_map/all_to_all | solution.py:232
  107.7 2.1 copy.45
  109.9 3.6 %shard_map.181 = (f32[128,2048]{1,0:T(8,128)S(1)}, f32[128,128]{1,0:T(8,128)S(1)}, f32[128,128]{1,0:T(8,128)S(1)}, f32[128,128]{1,0:T(8,128)S(1)}) custom-call(f32[128,128]{1,0:T(8,128)S(1)} %get-tuple-element.32.cum, bf16[128,2048]{1,0:T(8,128)(2,1)S(1)} %bitcast.35, bf16[128,2048]{1,0:T(8,128)(2,1)S(1)} %bitcast.38, bf16[128,128]{1,0:T(8,128)(2,1)S(1)} %bitcast.42, ...), custom_call_target="tpu_custom_call" | custom-call | flops 671088640 | bytes 2424960 | tf_op jit(solution)/shard_map/pallas_call | solution.py:218
  115.1 15.5 %all-to-all-done.1.starts = bf16[16,128,128]{2,1,0:T(8,128)(2,1)S(1)} async-done(((bf16[16,128,128]{2,1,0:T(8,128)(2,1)}), bf16[16,128,128]{2,1,0:T(8,128)(2,1)S(1)}, u32[]{:S(2)}, u32[]{:S(2)}) %all-to-all-start.1) | async-done | bytes 524320 | tf_op jit(solution)/shard_map/all_to_all | solution.py:232
  130.6 1.1 shard_map.183
  131.7 16.7 %all_to_all.45 = bf16[8,128,128]{2,1,0:T(8,128)(2,1)} all-to-all(bf16[8,128,128]{2,1,0:T(8,128)(2,1)S(1)} %get-tuple-element.42), channel_id=1, replica_groups=mesh['seq'=16,'tensor'=4,'dp'=8] {'dp'}, dimensions={0} | all-to-all | bytes 524288 | tf_op jit(solution)/shard_map/all_to_all | solution.py:232
  148.4 6.1 %all-to-all-start.2 = ((bf16[16,128,128]{2,1,0:T(8,128)(2,1)}), bf16[16,128,128]{2,1,0:T(8,128)(2,1)S(1)}, u32[]{:S(2)}, u32[]{:S(2)}) async-start(bf16[16,128,128]{2,1,0:T(8,128)(2,1)} %get-tuple-element.29), calls=%async_computation.2 | async-start | bytes 1048576 | tf_op jit(solution)/shard_map/all_to_all | solution.py:232
  154.5 2.9 %fusion.1 = bf16[4,256,128]{1,2,0:T(8,128)(2,1)} fusion(bf16[4,8,128,256]{3,2,1,0:T(8,128)(2,1)} %bitcast.50, bf16[8,128,128]{2,1,0:T(8,128)(2,1)} %all_to_all.45), kind=kOutput, calls=%fused_computation.2 | convolution fusion | flops 268566528 | bytes 2621440 | tf_op jit(solution)/shard_map/dot_general | solution.py:303
  157.4 1.8 copy.47
  159.2 18.0 %all-to-all-done.2.ends = bf16[16,128,128]{2,1,0:T(8,128)(2,1)S(1)} async-done(((bf16[16,128,128]{2,1,0:T(8,128)(2,1)}), bf16[16,128,128]{2,1,0:T(8,128)(2,1)S(1)}, u32[]{:S(2)}, u32[]{:S(2)}) %all-to-all-start.2) | async-done | bytes 524320 | tf_op jit(solution)/shard_map/all_to_all | solution.py:232
  177.2 12.1 %all-to-all-start.5 = ((bf16[16,64,128]{2,1,0:T(8,128)(2,1)}), bf16[16,64,128]{2,1,0:T(8,128)(2,1)S(1)}, u32[]{:S(2)}, u32[]{:S(2)}) async-start(bf16[16,64,128]{2,1,0:T(8,128)(2,1)} %bitcast.52), calls=%async_computation.5 | async-start | bytes 524288 | tf_op jit(solution)/shard_map/all_to_all | solution.py:232
  189.4 1.2 copy-done.5
  193.1 3.8 %shard_map.182 = (bf16[128,2048]{1,0:T(8,128)(2,1)}, bf16[128,128]{1,0:T(8,128)(2,1)}, f32[8,128]{1,0:T(8,128)S(1)}) custom-call(bf16[16,128,128]{2,1,0:T(8,128)(2,1)S(1)} %all-to-all-done.1.starts, bf16[16,128,128]{2,1,0:T(8,128)(2,1)S(1)} %all-to-all-done.2.ends, bf16[128,2048]{1,0:T(8,128)(2,1)S(1)} %bitcast.36, bf16[128,2048]{1,0:T(8,128)(2,1)S(1)} %bitcast.39, ...), custom_call_target="tpu_custom_call" | custom-call | flops 201326592 | bytes 5087232 | tf_op jit(solution)/shard_map/pallas_call | solution.py:218
  196.9 5.2 %all-to-all-done.5.parts = bf16[16,64,128]{2,1,0:T(8,128)(2,1)S(1)} async-done(((bf16[16,64,128]{2,1,0:T(8,128)(2,1)}), bf16[16,64,128]{2,1,0:T(8,128)(2,1)S(1)}, u32[]{:S(2)}, u32[]{:S(2)}) %all-to-all-start.5) | async-done | bytes 262176 | tf_op jit(solution)/shard_map/all_to_all | solution.py:232
  202.3 22.7 %all_to_all.46 = f32[16,8,128]{2,1,0:T(8,128)S(1)} all-to-all(f32[16,8,128]{2,1,0:T(8,128)S(1)} %get-tuple-element.44), channel_id=1, replica_groups=mesh['seq'=16,'tensor'=4,'dp'=8] {'seq'}, dimensions={0} | all-to-all | bytes 131072 | tf_op jit(solution)/shard_map/all_to_all | solution.py:232
  225.0 9.3 %all_to_all.47 = f32[8,8,128]{2,1,0:T(8,128)S(1)} all-to-all(f32[8,8,128]{2,1,0:T(8,128)S(1)} %broadcast_in_dim.28), channel_id=1, replica_groups=mesh['seq'=16,'tensor'=4,'dp'=8] {'dp'}, dimensions={0} | all-to-all | bytes 65536 | tf_op jit(solution)/shard_map/all_to_all | solution.py:232
  235.5 4.2 %all-to-all-start.8 = ((f32[4,8,128]{2,1,0:T(8,128)}), f32[4,8,128]{2,1,0:T(8,128)S(1)}, u32[]{:S(2)}, u32[]{:S(2)}) async-start(f32[4,8,128]{2,1,0:T(8,128)} %broadcast_in_dim.29), calls=%async_computation.8 | async-start | bytes 32768 | tf_op jit(solution)/shard_map/all_to_all | solution.py:232
  240.3 3.6 %all-to-all-done.8 = f32[4,8,128]{2,1,0:T(8,128)S(1)} async-done(((f32[4,8,128]{2,1,0:T(8,128)}), f32[4,8,128]{2,1,0:T(8,128)S(1)}, u32[]{:S(2)}, u32[]{:S(2)}) %all-to-all-start.8) | async-done | bytes 16416 | tf_op jit(solution)/shard_map/all_to_all | solution.py:232
  245.3 1.4 multiply_subtract_fusion
  (60 shorter events, 16.3 us)
Async XLA Ops:
  8.0 1.0 copy-start
  9.0 1.0 copy-start.2
  16.6 93.3 %copy-start.13 = (f32[128,128]{1,0:T(8,128)}, f32[128,128]{1,0:T(8,128)S(1)}, u32[]{:S(2)}) copy-start(f32[128,128]{1,0:T(8,128)S(1)} %get-tuple-element.32.cum) | copy-start | bytes 196612
  16.6 15.9 %copy-start.22 = (bf16[1,128,2048]{2,1,0:T(8,128)(2,1)S(1)}, bf16[1,128,2048]{2,1,0:T(8,128)(2,1)}, u32[]{:S(2)}) copy-start(bf16[1,128,2048]{2,1,0:T(8,128)(2,1)} %param.20) | copy-start | bytes 1572868
  16.6 63.1 %all-to-all-start = ((bf16[16,272,128]{2,1,0:T(8,128)(2,1)}), bf16[16,272,128]{2,1,0:T(8,128)(2,1)S(1)}, u32[]{:S(2)}, u32[]{:S(2)}) async-start(bf16[16,272,128]{2,1,0:T(8,128)(2,1)} %get-tuple-element.27), calls=%async_computation | async-start | bytes 2228224 | tf_op jit(solution)/shard_map/all_to_all | solution.py:232
  79.7 20.2 %all-to-all-start.4 = ((bf16[8,128,256]{1,2,0:T(8,128)(2,1)}), bf16[8,128,256]{1,2,0:T(8,128)(2,1)}, u32[]{:S(2)}, u32[]{:S(2)}) async-start(bf16[8,128,256]{1,2,0:T(8,128)(2,1)} %bitcast.14), calls=%async_computation.4 | async-start | bytes 1048576 | tf_op jit(solution)/shard_map/all_to_all | solution.py:232
  90.3 19.6 %copy-start.1 = (bf16[1,128,2048]{2,1,0:T(8,128)(2,1)S(1)}, bf16[1,128,2048]{2,1,0:T(8,128)(2,1)}, u32[]{:S(2)}) copy-start(bf16[1,128,2048]{2,1,0:T(8,128)(2,1)} %param.12) | copy-start | bytes 1572868
  90.3 19.6 %copy-start.3 = (bf16[1,128,2048]{2,1,0:T(8,128)(2,1)S(1)}, bf16[1,128,2048]{2,1,0:T(8,128)(2,1)}, u32[]{:S(2)}) copy-start(bf16[1,128,2048]{2,1,0:T(8,128)(2,1)} %param.19) | copy-start | bytes 1572868
  90.3 19.6 %copy-start.10 = (bf16[1,128,128]{2,1,0:T(8,128)(2,1)S(1)}, bf16[1,128,128]{2,1,0:T(8,128)(2,1)}, u32[]{:S(2)}) copy-start(bf16[1,128,128]{2,1,0:T(8,128)(2,1)} %param.13) | copy-start | bytes 98308
  90.3 19.6 %copy-start.12 = (bf16[1,128,128]{2,1,0:T(8,128)(2,1)S(1)}, bf16[1,128,128]{2,1,0:T(8,128)(2,1)}, u32[]{:S(2)}) copy-start(bf16[1,128,128]{2,1,0:T(8,128)(2,1)} %param.14) | copy-start | bytes 98308
  90.3 19.6 %copy-start.21 = (f32[32]{0:T(128)S(1)}, f32[32]{0:T(128)}, u32[]{:S(2)}) copy-start(f32[32]{0:T(128)} %param.18) | copy-start | bytes 388
  91.3 0.8 copy-start.8
  99.8 30.7 %all-to-all-start.1 = ((bf16[16,128,128]{2,1,0:T(8,128)(2,1)}), bf16[16,128,128]{2,1,0:T(8,128)(2,1)S(1)}, u32[]{:S(2)}, u32[]{:S(2)}) async-start(bf16[16,128,128]{2,1,0:T(8,128)(2,1)} %copy-done.8), calls=%async_computation.1 | async-start | bytes 1048576 | tf_op jit(solution)/shard_map/all_to_all | solution.py:232
  107.7 46.8 %all-gather.3.cloned.1.call-start = ((), (), s32[]{:S(2)}) async-start(), calls=%async_computation.9 | async-start | bytes 2621440 | tf_op jit(solution)/shard_map/all_gather | solution.py:275
  113.5 1.0 copy-start.4
  115.1 42.3 %copy-start.17 = (f32[128,128]{1,0:T(8,128)}, f32[128,128]{1,0:T(8,128)S(1)}, u32[]{:S(2)}) copy-start(f32[128,128]{1,0:T(8,128)S(1)} %get-tuple-element.37.dcum) | copy-start | bytes 196612
  148.4 28.9 %all-to-all-start.2 = ((bf16[16,128,128]{2,1,0:T(8,128)(2,1)}), bf16[16,128,128]{2,1,0:T(8,128)(2,1)S(1)}, u32[]{:S(2)}, u32[]{:S(2)}) async-start(bf16[16,128,128]{2,1,0:T(8,128)(2,1)} %get-tuple-element.29), calls=%async_computation.2 | async-start | bytes 1048576 | tf_op jit(solution)/shard_map/all_to_all | solution.py:232
  154.4 35.0 %copy-start.7 = (bf16[128,2048]{1,0:T(8,128)(2,1)S(1)}, bf16[128,2048]{1,0:T(8,128)(2,1)}, u32[]{:S(2)}) copy-start(bf16[128,2048]{1,0:T(8,128)(2,1)} %copy-done.6) | copy-start | bytes 1572868
  177.2 24.9 %all-to-all-start.5 = ((bf16[16,64,128]{2,1,0:T(8,128)(2,1)}), bf16[16,64,128]{2,1,0:T(8,128)(2,1)S(1)}, u32[]{:S(2)}, u32[]{:S(2)}) async-start(bf16[16,64,128]{2,1,0:T(8,128)(2,1)} %bitcast.52), calls=%async_computation.5 | async-start | bytes 524288 | tf_op jit(solution)/shard_map/all_to_all | solution.py:232
  189.4 1.2 copy-start.5
  190.6 0.8 copy-start.14
  191.4 0.8 copy-start.16
  192.3 0.8 copy-start.18
  235.5 8.4 %all-to-all-start.8 = ((f32[4,8,128]{2,1,0:T(8,128)}), f32[4,8,128]{2,1,0:T(8,128)S(1)}, u32[]{:S(2)}, u32[]{:S(2)}) async-start(f32[4,8,128]{2,1,0:T(8,128)} %broadcast_in_dim.29), calls=%async_computation.8 | async-start | bytes 32768 | tf_op jit(solution)/shard_map/all_to_all | solution.py:232
  (6 other events, 4.3 us)
Sparse Core Ops, SparseCore 0:
  110.6 38.4 all-gather.2

commit v2 on v1

v2 whole, which is shorter than its diff:
```python
import functools
import math

import jax
import jax.numpy as jnp
from jax import lax
from jax.experimental import pallas as pl
from jax.experimental.pallas import tpu as pltpu
from jax.sharding import PartitionSpec as P

P_SIZE = 64
N = 128
SPAN = 128
PAIR = 2 * P_SIZE
LOG_ROWS = 16
GROUP = 4

beta_one = 0.9
beta_two = 0.95
adam_eps = 1e-08
learn_rate = 0.02
decay_weight = 0.1
step_count = 10

f32 = jnp.float32
bf16 = jnp.bfloat16
HIGHEST = lax.Precision.HIGHEST


def iota(shape, dim):
    return lax.broadcasted_iota(jnp.int32, shape, dim)


def dot(a, b):
    return jnp.dot(a, b, preferred_element_type=f32)


def dot_nt(a, b):
    return lax.dot_general(a, b, (((1,), (1,)), ((), ())), preferred_element_type=f32)


def first_head():
    return iota((SPAN, PAIR), 1) < P_SIZE


def spread(cols, j, first):
    return jnp.where(
        first[: cols.shape[0]], cols[:, 2 * j : 2 * j + 1], cols[:, 2 * j + 1 : 2 * j + 2]
    )


def log_rows(whole):
    row = iota((LOG_ROWS, whole.shape[1]), 0)
    high = whole.astype(bf16).astype(f32)
    middle = (whole - high).astype(bf16).astype(f32)
    low = whole - high - middle
    return jnp.where(
        row == 0, high, jnp.where(row == 1, middle, jnp.where(row == 2, low, 0.0))
    ).astype(bf16)


def row_logs(rows):
    rows = rows.astype(f32)
    return rows[0:1] + rows[1:2] + rows[2:3]


def states_kernel(dt_t, lev, rate_t, x, dy, b, c, st, loga, cum, onehot):
    heads = dt_t.shape[0]
    levels = rate_t.shape[0]
    hit = iota((levels, heads), 0) == lev[...]
    onehot[...] = jnp.zeros_like(onehot)
    onehot[:levels, :heads] = jnp.where(hit, 1.0, 0.0)
    cum[...] = jnp.zeros_like(cum)
    cum[:levels, :heads] = jnp.where(hit, rate_t[...], 0.0)
    rate = jnp.sum(cum[:levels, :], axis=0, keepdims=True)
    cum[:heads, :] = dt_t[...]
    cum[heads:, :] = jnp.zeros_like(cum[heads:, :])
    loga[...] = -rate * cum[...].T
    lower = (iota((SPAN, SPAN), 0) >= iota((SPAN, SPAN), 1)).astype(f32)
    total = jnp.dot(lower, loga[...], precision=HIGHEST, preferred_element_type=f32)
    cum[...] = total
    last = total[SPAN - 1 :, :]
    tail = jnp.exp(last - total)
    grow = jnp.exp(total)
    b_t = b[...].astype(f32).T.astype(bf16)
    c_t = c[...].astype(f32).T.astype(bf16)
    first = first_head()
    heads_piece = heads // st.shape[0]
    for j in range(heads // 2):
        piece, at = 2 * j // heads_piece, 2 * j % heads_piece * P_SIZE
        lanes = slice(j * PAIR, (j + 1) * PAIR)
        spot = slice(at, at + PAIR)
        xs = (x[:, lanes].astype(f32) * spread(tail, j, first)).astype(bf16)
        ds = (dy[:, lanes].astype(f32) * spread(grow, j, first)).astype(bf16)
        st[piece, :N, spot] = dot(b_t, xs).astype(bf16)
        st[piece, N : 2 * N, spot] = dot(c_t, ds).astype(bf16)
        st[piece, 2 * N :, spot] = log_rows(spread(last, j, first))


def group_kernel(me, got, out):
    here = me[0] // GROUP
    count = got.shape[0]
    for at in range(0, got.shape[2], PAIR):
        lanes = slice(at, at + PAIR)
        logs = [row_logs(got[k, 2 * N :, lanes]) for k in range(count)]
        decay = [jnp.exp(a) for a in logs]
        ahead = back = jnp.zeros((N, PAIR), f32)
        for k in range(count):
            ahead = decay[k] * ahead + got[k, :N, lanes].astype(f32)
        for k in reversed(range(count)):
            back = decay[k] * back + got[k, N : 2 * N, lanes].astype(f32)
        rows = log_rows(sum(logs[1:], logs[0]))
        for k in range(out.shape[0]):
            out[k, :N, lanes] = jnp.where(k > here, ahead, back).astype(bf16)
            out[k, N:, lanes] = rows


def scan_kernel(me, got, groups, out):
    here = me[0] // GROUP
    count = got.shape[0]
    for at in range(0, got.shape[2], PAIR):
        lanes = slice(at, at + PAIR)
        decay = [jnp.exp(row_logs(got[k, 2 * N :, lanes])) for k in range(count)]
        state = back = jnp.zeros((N, PAIR), f32)
        for k in range(groups.shape[0]):
            new = jnp.exp(row_logs(groups[k, N:, lanes])) * state + groups[k, :N, lanes].astype(f32)
            state = jnp.where(k < here, new, state)
        for k in reversed(range(groups.shape[0])):
            new = jnp.exp(row_logs(groups[k, N:, lanes])) * back + groups[k, :N, lanes].astype(f32)
            back = jnp.where(k > here, new, back)
        for k in range(count):
            out[k, :N, lanes] = state.astype(bf16)
            state = decay[k] * state + got[k, :N, lanes].astype(f32)
        for k in reversed(range(count)):
            out[k, N:, lanes] = back.astype(bf16)
            back = decay[k] * back + got[k, N : 2 * N, lanes].astype(f32)


def feature_kernel(rows, me, layer, *refs):
    outs, held = refs[:-1], refs[-1]
    streams = held.shape[0]
    for at in range(0, layer.shape[1], PAIR):
        turned = layer[:, at : at + PAIR].astype(f32).T.astype(bf16)
        for part in range(0, PAIR, rows):
            index = (at + part) // rows
            stream, spot = index % streams, index // streams * rows
            held[stream, spot : spot + rows, :] = turned[part : part + rows, :]
    for k, out in enumerate(outs):
        out[...] = held[me[1] ^ k]


def stack_kernel(*refs):
    for k, part in enumerate(refs[:-1]):
        refs[-1][k] = part[...]


def weight_kernel(me, all_c, *refs):
    features, out = refs[:-1], refs[-1]
    rows = out.shape[1]
    for k, block in enumerate(features):
        total = dot(block[0], all_c[me[1]])
        for j in range(1, block.shape[0]):
            total = total + dot(block[j], all_c[me[1] ^ j])
        for q in range(block.shape[1] // rows):
            out[(me[2] ^ k) * (block.shape[1] // rows) + q] = total[q * rows : (q + 1) * rows].astype(bf16)


def intra_kernel(cum, x, dy, b, c, skip, dxp, xt, dye, dc, db, dcum, rows):
    heads = skip.shape[1]
    total = cum[...]
    tail = jnp.exp(total[SPAN - 1 :, :] - total)
    grow = jnp.exp(total)
    total_t = total.T
    keep = iota((SPAN, SPAN), 1) >= iota((SPAN, SPAN), 0)
    lane = iota((SPAN, SPAN), 1)
    first = first_head()
    gain = skip[...]
    mask_a = jnp.where(first, 1.0, 0.0).astype(bf16)
    mask_b = jnp.where(first, 0.0, 1.0).astype(bf16)
    gram_t = dot_nt(b[...], c[...])
    dgram_t = jnp.zeros((SPAN, SPAN), f32)
    columns = jnp.zeros((SPAN, SPAN), f32)
    rows[...] = jnp.zeros_like(rows)
    for j in range(heads // 2):
        lanes = slice(j * PAIR, (j + 1) * PAIR)
        x_pair, dy_pair = x[:, lanes], dy[:, lanes]
        x_two = jnp.concatenate([x_pair * mask_a, x_pair * mask_b], axis=0)
        dy_two = jnp.concatenate([dy_pair * mask_a, dy_pair * mask_b], axis=0)
        dm_two = dot_nt(x_two, dy_pair)
        mixes = []
        for k in range(2):
            h = 2 * j + k
            dm = dm_two[k * SPAN : (k + 1) * SPAN]
            diff = total_t[h : h + 1, :] - total[:, h : h + 1]
            w = jnp.exp(jnp.where(keep, jnp.minimum(diff, 0.0), -1e30))
            wd = w * dm
            dgram_t = dgram_t + wd
            q = wd * gram_t
            columns = jnp.where(lane == h, jnp.sum(q, axis=1, keepdims=True), columns)
            rows[h : h + 1, :] = jnp.sum(q, axis=0, keepdims=True)
            mixes.append((w * gram_t).astype(bf16))
        dx = dot(jnp.concatenate(mixes, axis=1), dy_two)
        dy_wide = dy_pair.astype(f32)
        dxp[:, lanes] = dx + spread(gain, j, first) * dy_wide
        xt[:, lanes] = (x_pair.astype(f32) * spread(tail, j, first)).astype(bf16)
        dye[:, lanes] = (dy_wide * spread(grow, j, first)).astype(bf16)
    dcum[...] = rows[...].T - columns
    high = dgram_t.astype(bf16)
    dc[...] = dot(high.astype(f32).T.astype(bf16), b[...])
    db[...] = dot(high, c[...])


def grad_c_kernel(dc, dye, starts, grad_c, copies):
    total = dc[...]
    pieces, width = starts.shape[0], starts.shape[2]
    for j in range(pieces):
        total = total + dot_nt(dye[:, j * width : (j + 1) * width], starts[j, :N, :])
    out = total.astype(bf16)
    grad_c[...] = out
    for k in range(copies.shape[0]):
        copies[k] = out


def halves(a):
    high = a.astype(bf16)
    return high, (a - high.astype(f32)).astype(bf16)


def rest_kernel(
    states, x, dy, xt, cum, loga, onehot, b, c, dxp, db, dcum, grad_x, grad_b, small
):
    heads = x.shape[1] // P_SIZE
    pairs_piece = states.shape[2] // PAIR
    total = cum[...]
    last = total[SPAN - 1 :, :]
    tail = jnp.exp(last - total)
    grow = jnp.exp(total)
    end = jnp.exp(last)
    first = first_head()
    row = iota((SPAN, PAIR), 0)
    lane_head = iota((PAIR, 128), 0) // P_SIZE
    column = iota((PAIR, 128), 1)
    b_total = db[...]
    d_total = dcum[...]
    skips = jnp.zeros((8, 128), f32)
    for j in range(heads // 2):
        piece, at = j // pairs_piece, j % pairs_piece * PAIR
        lanes = slice(j * PAIR, (j + 1) * PAIR)
        start, stop = states[piece, :N, at : at + PAIR], states[piece, N:, at : at + PAIR]
        xs = xt[:, lanes]
        x_wide, dy_wide = x[:, lanes].astype(f32), dy[:, lanes].astype(f32)
        falling = spread(tail, j, first)
        carried = dy_wide * spread(grow, j, first) * dot(c[...], start)
        back = falling * dot(b[...], stop)
        left = x_wide * back
        grad_x[:, lanes] = (dxp[:, lanes] + back).astype(bf16)
        b_total = b_total + dot_nt(xs, stop)
        at_end = jnp.sum(left, axis=0, keepdims=True) + spread(end, j, first) * jnp.sum(
            start.astype(f32) * stop.astype(f32), axis=0, keepdims=True
        )
        moved = carried - left + jnp.where(row == SPAN - 1, at_end, 0.0)
        skip = jnp.sum(x_wide * dy_wide, axis=0, keepdims=True)
        skip = jnp.broadcast_to(skip, (8, PAIR))
        to_head = jnp.where(column == 2 * j + lane_head, 1.0, 0.0).astype(bf16)
        to_skip = jnp.where(column == heads + 2 * j + lane_head, 1.0, 0.0).astype(bf16)
        high, low = halves(moved)
        d_total = d_total + dot(high, to_head) + dot(low, to_head)
        high, low = halves(skip)
        skips = skips + dot(high, to_skip) + dot(low, to_skip)
    grad_b[...] = b_total.astype(bf16)
    upper = (iota((SPAN, SPAN), 1) >= iota((SPAN, SPAN), 0)).astype(f32)
    dlog = jnp.dot(upper, d_total, precision=HIGHEST, preferred_element_type=f32)
    rates = jnp.sum(dlog * loga[...], axis=0, keepdims=True)
    small[...] = onehot[...] * rates + jnp.where(iota((8, 128), 0) == 0, skips, 0.0)


def shard_kernel(parts, small, shard, copies):
    total = jnp.sum(parts[...].astype(f32), axis=0)
    shard[...] = total
    square = jnp.sum(total * total)
    here = (iota((8, 128), 0) == 0) & (iota((8, 128), 1) == 127)
    out = small[...] + jnp.where(here, square, 0.0)
    for k in range(copies.shape[0]):
        copies[k] = out


def sum_kernel(got, copies):
    out = jnp.sum(got[...], axis=0)
    for k in range(copies.shape[0]):
        copies[k] = out


def update_kernel(streams, size, me, got, shard, weight, moment_one, moment_two, new_w, new_m, new_s, rates, skips):
    total = jnp.sum(got[...], axis=0)
    mine = got[me[2] * streams]
    for k in range(1, streams):
        mine = mine + got[me[2] * streams + k]
    here = (iota((8, 128), 0) == 0) & (iota((8, 128), 1) == 127)
    square = jnp.sum(jnp.where(here, total, 0.0), keepdims=True)
    heads = rates.shape[1]
    rates[...] = mine[: rates.shape[0], :heads]
    skips[...] = mine[0:1, heads : 2 * heads]
    limit = 0.25 * math.sqrt(size)
    clipped = shard[...] * (limit / jnp.maximum(jnp.sqrt(square), limit))
    moment = beta_one * moment_one[...] + (1.0 - beta_one) * clipped
    second = beta_two * moment_two[...] + (1.0 - beta_two) * clipped * clipped
    direction = (
        moment
        / (1.0 - beta_one**step_count)
        / (jnp.sqrt(second / (1.0 - beta_two**step_count)) + adam_eps)
    )
    new_w[...] = weight[...] - learn_rate * (direction + decay_weight * weight[...])
    new_m[...] = moment
    new_s[...] = second


def call(kernel, out_shapes, *args, scratch=(), flops=0, limit=32):
    size = sum(math.prod(a.shape) * a.dtype.itemsize for a in (*args, *out_shapes))
    whole = pl.BlockSpec(memory_space=pltpu.VMEM)
    scalars = pl.BlockSpec(memory_space=pltpu.SMEM)
    out = pl.pallas_call(
        kernel,
        out_shape=tuple(out_shapes),
        in_specs=[scalars if a.shape == (3,) else whole for a in args],
        scratch_shapes=list(scratch),
        compiler_params=pltpu.CompilerParams(vmem_limit_bytes=limit * 1024 * 1024),
        cost_estimate=pl.CostEstimate(flops=flops, bytes_accessed=size, transcendentals=0),
    )(*args)
    return out[0] if len(out_shapes) == 1 else out


def shaped(shape, dtype):
    return jax.ShapeDtypeStruct(shape, dtype)


def swap(a, axis, groups=None):
    return lax.all_to_all(a, axis, 0, 0, tiled=True, axis_index_groups=groups)


def trade(a, axis, k):
    count = lax.axis_size(axis)
    return lax.ppermute(a, axis, [(i, i ^ k) for i in range(count)])


def local(
    seq_values,
    proj_b,
    proj_c,
    time_step,
    decay_level,
    decay_rate,
    skip_gain,
    grad_out,
    layer_input,
    weight_c,
    moment_one,
    moment_two,
):
    seqs, streams, tensors = (lax.axis_size(a) for a in ("seq", "dp", "tensor"))
    me = jnp.stack([lax.axis_index(a) for a in ("seq", "dp", "tensor")]).astype(jnp.int32)
    x, dy, b, c = seq_values[0], grad_out[0], proj_b[0], proj_c[0]
    heads = skip_gain.shape[0]
    width = heads * P_SIZE
    piece = width // GROUP
    near = [[i + k for k in range(GROUP)] for i in range(0, seqs, GROUP)]
    far = [list(range(i, seqs, GROUP)) for i in range(GROUP)]
    tile = shaped((SPAN, 128), f32)
    small_tile = shaped((8, 128), f32)
    wide = shaped((SPAN, width), bf16)
    st, loga, cum, onehot = call(
        states_kernel,
        [shaped((GROUP, 2 * N + LOG_ROWS, piece), bf16), tile, tile, small_tile],
        time_step[0].T,
        decay_level[0],
        decay_rate.T,
        x,
        dy,
        b,
        c,
        flops=4 * SPAN * N * width,
        limit=60,
    )
    layer, st = lax.optimization_barrier((layer_input[0], st))
    got = swap(st, "seq", near)

    rows = weight_c.shape[0]
    block = layer.shape[1] // streams
    pieces = call(
        functools.partial(feature_kernel, rows),
        [shaped((block, SPAN), bf16)] * streams,
        me,
        layer,
        scratch=[pltpu.VMEM((streams, block, SPAN), bf16)],
        flops=0,
    )
    pieces = [pieces] if streams == 1 else pieces
    arrived = [trade(pieces[k], "dp", k) for k in range(1, streams)]
    got, *arrived = lax.optimization_barrier((got, *arrived))
    mine = call(stack_kernel, [shaped((streams, block, SPAN), bf16)], pieces[0], *arrived)
    features = [trade(mine, "tensor", k) for k in range(1, tensors)]

    dxp, xt, dye, dc, db, dcum = call(
        intra_kernel,
        [shaped((SPAN, width), f32), wide, wide, tile, tile, tile],
        cum,
        x,
        dy,
        b,
        c,
        skip_gain[None],
        scratch=[pltpu.VMEM((SPAN, SPAN), f32)],
        flops=20 * SPAN * SPAN * width,
    )
    ahead = call(
        group_kernel,
        [shaped((seqs // GROUP, N + LOG_ROWS, piece), bf16)],
        me,
        got,
        flops=8 * N * width,
    )
    groups = swap(ahead, "seq", far)
    groups, *features = lax.optimization_barrier((groups, *features))
    features = [mine, *features]
    states = call(
        scan_kernel,
        [shaped((GROUP, 2 * N, piece), bf16)],
        me,
        got,
        groups,
        flops=8 * N * width,
    )
    states = swap(states, "seq", near)
    grad_c, copies = call(
        grad_c_kernel,
        [shaped((SPAN, N), bf16), shaped((streams, SPAN, N), bf16)],
        dc,
        dye,
        states,
        flops=2 * SPAN * N * width,
    )
    all_c = swap(copies, "dp")
    partial = call(
        weight_kernel,
        [shaped((seqs, rows, N), bf16)],
        me,
        all_c,
        *features,
        flops=2 * tensors * layer.shape[1] * SPAN * N,
    )
    parts = swap(partial, "seq")
    grad_x, grad_b, small = call(
        rest_kernel,
        [wide, shaped((SPAN, N), bf16), small_tile],
        states,
        x,
        dy,
        xt,
        cum,
        loga,
        onehot,
        b,
        c,
        dxp,
        db,
        dcum,
        flops=6 * SPAN * N * width,
    )
    shard, sums = call(
        shard_kernel,
        [shaped((rows, N), f32), shaped((seqs, 8, 128), f32)],
        parts,
        small,
        flops=seqs * rows * N,
    )
    sums = call(sum_kernel, [shaped((tensors * streams, 8, 128), f32)], swap(sums, "seq"))
    matrix = shaped((rows, N), f32)
    size = rows * seqs * streams * N * tensors
    new_weight, new_moment, new_second, rates, skips = call(
        functools.partial(update_kernel, streams, size),
        [matrix, matrix, matrix, shaped((decay_rate.shape[1], heads), f32), shaped((1, heads), f32)],
        me,
        swap(sums, ("tensor", "dp")),
        shard,
        weight_c,
        moment_one,
        moment_two,
    )
    return (
        grad_x[None],
        grad_b[None],
        grad_c[None],
        rates.T,
        skips[0],
        new_weight,
        new_moment,
        new_second,
    )


def solution(mesh):
    wide = P("dp", "seq", "tensor")
    shard = P(("seq", "dp"), "tensor")
    return jax.shard_map(
        local,
        mesh=mesh,
        in_specs=(
            wide,
            wide,
            wide,
            wide,
            wide,
            P("tensor", None),
            P("tensor"),
            wide,
            wide,
            shard,
            shard,
            shard,
        ),
        out_specs=(wide, wide, wide, P("tensor", None), P("tensor"), shard, shard, shard),
        check_vma=False,
    )
```

time: 255 us -> 197 us (0.77)
  waiting for transfers between devices: 96.3 us -> 51.3 us
  between operations: 15 us -> 0.91 us
  starting transfers between devices: 56.7 us -> 69.7 us
  local copies, waits for them, and re-layouts: 19.5 us -> 6.51 us
  Pallas kernels: 12.5 us -> 22.1 us
  blocking collectives: 48.6 us -> 45.4 us
  matrix products: 2.93 us -> 0 us
    all_to_all x6 -> x4, waiting for transfers between devices: 96.3 us -> 26.2 us  [swap(): return lax.all_to_all(a, axis, 0, 0, tiled=True, axis_index_groups=groups)]
    ppermute x0 -> x10, starting transfers between devices: none -> 34.8 us  [trade(): return lax.ppermute(a, axis, [(i, i ^ k) for i in range(count)])]
    ppermute x0 -> x10, waiting for transfers between devices: none -> 25.1 us  [trade(): return lax.ppermute(a, axis, [(i, i ^ k) for i in range(count)])]
    all_to_all x6 -> x4, starting transfers between devices: 56.7 us -> 34.9 us  [swap(): return lax.all_to_all(a, axis, 0, 0, tiled=True, axis_index_groups=groups)]
    pallas_call x6 -> x12, Pallas kernels: 12.5 us -> 22.1 us  [call(): pl.pallas_call(kernel, out_shape=tuple(out_shapes), in_specs=[scalars if...]
    unnamed x48 -> x44, local copies, waits for them, and re-layouts: 13 us -> 6.51 us
    all_to_all x3, blocking collectives: 48.6 us -> 45.4 us  [swap(): return lax.all_to_all(a, axis, 0, 0, tiled=True, axis_index_groups=groups)]
    dot_general x1 -> x0, matrix products: 2.93 us -> none  [local(): lax.dot_general(features, all_c, (((1,), (0,)), ((), ())), preferred_elem...]
  transfers between devices with their start and end apart: 7 -> 14, of which waited for: 6 -> 7; matrix products, arithmetic and copies ran while one was open for 3% -> 0% of each run, Pallas kernels for 4% -> 5%
where the time goes in v2:
time: 197 us; the launch traced here: 196 us
  starting transfers between devices  69.7 us (35%)
  waiting for transfers between devices  51.3 us (26%)
  blocking collectives  45.4 us (23%)
  Pallas kernels  22.1 us (11%)
  local copies, waits for them, and re-layouts  6.51 us (3%)
    all_to_all x3, blocking collectives, swap(): return lax.all_to_all(a, axis, 0, 0, tiled=True, axis_index_groups=groups)  45.4 us
    all_to_all x4, starting transfers between devices, swap(): return lax.all_to_all(a, axis, 0, 0, tiled=True, axis_index_groups=groups)  34.9 us
    ppermute x10, starting transfers between devices, trade(): return lax.ppermute(a, axis, [(i, i ^ k) for i in range(count)])  34.8 us
    all_to_all x4, waiting for transfers between devices, swap(): return lax.all_to_all(a, axis, 0, 0, tiled=True, axis_index_groups=groups)  26.2 us
    ppermute x10, waiting for transfers between devices, trade(): return lax.ppermute(a, axis, [(i, i ^ k) for i in range(count)])  25.1 us
    pallas_call x12, Pallas kernels, call(): pl.pallas_call(kernel, out_shape=tuple(out_shapes), in_specs=[scalars if...  22.1 us
    unnamed x44, local copies, waits for them, and re-layouts  6.51 us
  transfers between devices with their start and end apart: 14, of which 7 were waited for; matrix products, arithmetic and copies ran while one was open for 0% of the time, Pallas kernels for 5%

profile of v2, /device:TPU:1, one launch (start us, length us, event | category | flops | bytes accessed | tf_op | source)
XLA Modules:
  0.0 196.0 jit_solution(4401859721678476017)
XLA Ops:
  0.6 4.2 %shard_map.179 = (bf16[4,272,512]{2,1,0:T(8,128)(2,1)}, f32[128,128]{1,0:T(8,128)}, f32[128,128]{1,0:T(8,128)}, f32[8,128]{1,0:T(8,128)}) custom-call(f32[32,128]{1,0:T(8,128)} %bitcast.33, s32[1,32]{1,0:T(1,128)} %bitcast.35, f32[8,32]{1,0:T(8,128)} %bitcast.34, bf16[128,2048]{1,0:T(8,128)(2,1)} %bitcast.19, bf16[128,2048]{1,0:T(8,128)(2,1)} %bitcast.22, ...), custom_call_target="tpu_custom_call" | custom-call | flops 134217728 | bytes 2380928 | tf_op jit(solution)/shard_map/pallas_call | solution.py:321
  4.8 6.6 %all-to-all-start = ((bf16[4,272,512]{2,1,0:T(8,128)(2,1)}), bf16[4,272,512]{2,1,0:T(8,128)(2,1)S(1)}, u32[]{:S(2)}, u32[]{:S(2)}) async-start(bf16[4,272,512]{2,1,0:T(8,128)(2,1)} %get-tuple-element.53), calls=%async_computation | async-start | bytes 2228224 | tf_op jit(solution)/shard_map/all_to_all | solution.py:337
  12.3 5.9 %collective-permute-start = (bf16[256,128]{1,0:T(8,128)(2,1)S(1)}, bf16[256,128]{1,0:T(8,128)(2,1)S(1)}, u32[]{:S(2)}, u32[]{:S(2)}) collective-permute-start(bf16[256,128]{1,0:T(8,128)(2,1)S(1)} %get-tuple-element.55), channel_id=1, source_target_pairs={{0,1},{1,0},{2,3},{3,2},{4,5},{5,4},{6,7},{7,6},{8,9},{9,8},{10,11... | collective-permute-start | bytes 196616 | tf_op jit(solution)/shard_map/ppermute | solution.py:342
  20.1 3.5 %collective-permute-start.2 = (bf16[256,128]{1,0:T(8,128)(2,1)S(1)}, bf16[256,128]{1,0:T(8,128)(2,1)S(1)}, u32[]{:S(2)}, u32[]{:S(2)}) collective-permute-start(bf16[256,128]{1,0:T(8,128)(2,1)S(1)} %get-tuple-element.57), channel_id=1, source_target_pairs={{0,3},{1,2},{2,1},{3,0},{4,7},{5,6},{6,5},{7,4},{8,11},{9,10},{10,... | collective-permute-start | bytes 196616 | tf_op jit(solution)/shard_map/ppermute | solution.py:342
  25.6 5.2 %collective-permute-start.4 = (bf16[256,128]{1,0:T(8,128)(2,1)S(1)}, bf16[256,128]{1,0:T(8,128)(2,1)S(1)}, u32[]{:S(2)}, u32[]{:S(2)}) collective-permute-start(bf16[256,128]{1,0:T(8,128)(2,1)S(1)} %get-tuple-element.59), channel_id=1, source_target_pairs={{0,5},{1,4},{2,7},{3,6},{4,1},{5,0},{6,3},{7,2},{8,13},{9,12},{10,... | collective-permute-start | bytes 196616 | tf_op jit(solution)/shard_map/ppermute | solution.py:342
  32.8 4.8 %collective-permute-start.6 = (bf16[256,128]{1,0:T(8,128)(2,1)S(1)}, bf16[256,128]{1,0:T(8,128)(2,1)S(1)}, u32[]{:S(2)}, u32[]{:S(2)}) collective-permute-start(bf16[256,128]{1,0:T(8,128)(2,1)S(1)} %get-tuple-element.61), channel_id=1, source_target_pairs={{0,7},{1,6},{2,5},{3,4},{4,3},{5,2},{6,1},{7,0},{8,15},{9,14},{10,... | collective-permute-start | bytes 196616 | tf_op jit(solution)/shard_map/ppermute | solution.py:342
  37.6 2.0 %collective-permute-done.6.refs_7_ = bf16[256,128]{1,0:T(8,128)(2,1)S(1)} collective-permute-done((bf16[256,128]{1,0:T(8,128)(2,1)S(1)}, bf16[256,128]{1,0:T(8,128)(2,1)S(1)}, u32[]{:S(2)}, u32[]{:S(2)}) %collective-permute-start.6) | collective-permute-done | bytes 65568 | tf_op jit(solution)/shard_map/ppermute | solution.py:342
  41.4 12.1 %all-to-all-start.1 = ((bf16[4,144,512]{2,1,0:T(8,128)(2,1)}), bf16[4,144,512]{2,1,0:T(8,128)(2,1)S(1)}, u32[]{:S(2)}, u32[]{:S(2)}) async-start(bf16[4,144,512]{2,1,0:T(8,128)(2,1)} %shard_map.181), calls=%async_computation.1 | async-start | bytes 1179648 | tf_op jit(solution)/shard_map/all_to_all | solution.py:337
  53.5 3.2 %collective-permute-start.7 = (bf16[8,256,128]{2,1,0:T(8,128)(2,1)S(1)}, bf16[8,256,128]{2,1,0:T(8,128)(2,1)S(1)}, u32[]{:S(2)}, u32[]{:S(2)}) collective-permute-start(bf16[8,256,128]{2,1,0:T(8,128)(2,1)S(1)} %shard_map.182.refs_0_), channel_id=1, source_target_pairs={{0,8},{8,0},{16,24},{24,16},{1,9},{9,1},{17,25},{25,17},{2,10},{10... | collective-permute-start | bytes 1572872 | tf_op jit(solution)/shard_map/ppermute | solution.py:342
  56.7 4.5 %collective-permute-start.8 = (bf16[8,256,128]{2,1,0:T(8,128)(2,1)S(1)}, bf16[8,256,128]{2,1,0:T(8,128)(2,1)S(1)}, u32[]{:S(2)}, u32[]{:S(2)}) collective-permute-start(bf16[8,256,128]{2,1,0:T(8,128)(2,1)S(1)} %shard_map.182.refs_0_), channel_id=1, source_target_pairs={{0,16},{8,24},{16,0},{24,8},{1,17},{9,25},{17,1},{25,9},{2,18},{10... | collective-permute-start | bytes 1572872 | tf_op jit(solution)/shard_map/ppermute | solution.py:342
  63.2 5.0 %collective-permute-done.7.refs_1_ = bf16[8,256,128]{2,1,0:T(8,128)(2,1)S(1)} collective-permute-done((bf16[8,256,128]{2,1,0:T(8,128)(2,1)S(1)}, bf16[8,256,128]{2,1,0:T(8,128)(2,1)S(1)}, u32[]{:S(2)}, u32[]{:S(2)}) %collective-permute-start.7) | collective-permute-done | bytes 524320 | tf_op jit(solution)/shard_map/ppermute | solution.py:342
  69.0 12.9 %collective-permute-done.8.refs_2_ = bf16[8,256,128]{2,1,0:T(8,128)(2,1)S(1)} collective-permute-done((bf16[8,256,128]{2,1,0:T(8,128)(2,1)S(1)}, bf16[8,256,128]{2,1,0:T(8,128)(2,1)S(1)}, u32[]{:S(2)}, u32[]{:S(2)}) %collective-permute-start.8) | collective-permute-done | bytes 524320 | tf_op jit(solution)/shard_map/ppermute | solution.py:342
  82.7 5.0 %collective-permute-done.9.refs_3_ = bf16[8,256,128]{2,1,0:T(8,128)(2,1)S(1)} collective-permute-done((bf16[8,256,128]{2,1,0:T(8,128)(2,1)S(1)}, bf16[8,256,128]{2,1,0:T(8,128)(2,1)S(1)}, u32[]{:S(2)}, u32[]{:S(2)}) %collective-permute-start.9) | collective-permute-done | bytes 524320 | tf_op jit(solution)/shard_map/ppermute | solution.py:342
  88.6 2.1 %shard_map.183 = bf16[4,256,512]{2,1,0:T(8,128)(2,1)} custom-call(s32[3]{0:T(128)S(1)} %pad_add_fusion.me, bf16[4,272,512]{2,1,0:T(8,128)(2,1)S(1)} %all-to-all-done.got, bf16[4,144,512]{2,1,0:T(8,128)(2,1)S(1)} %all-to-all-done.1.groups), custom_call_target="tpu_custom_call" | custom-call | flops 2097152 | bytes 2752524 | tf_op jit(solution)/shard_map/pallas_call | solution.py:321
  90.7 4.9 %all-to-all-start.2 = ((bf16[4,256,512]{2,1,0:T(8,128)(2,1)}), bf16[4,256,512]{2,1,0:T(8,128)(2,1)S(1)}, u32[]{:S(2)}, u32[]{:S(2)}) async-start(bf16[4,256,512]{2,1,0:T(8,128)(2,1)} %shard_map.183), calls=%async_computation.2 | async-start | bytes 2097152 | tf_op jit(solution)/shard_map/all_to_all | solution.py:337
  95.6 4.9 %shard_map.184 = (f32[128,2048]{1,0:T(8,128)S(1)}, bf16[128,2048]{1,0:T(8,128)(2,1)S(1)}, bf16[128,2048]{1,0:T(8,128)(2,1)S(1)}, f32[128,128]{1,0:T(8,128)S(1)},...) custom-call(f32[128,128]{1,0:T(8,128)S(1)} %copy-done.16, bf16[128,2048]{1,0:T(8,128)(2,1)S(1)} %bitcast.20, ...), custom_call_target="tpu_custom_call" | custom-call | flops 671088640 | bytes 3473536 | tf_op jit(solution)/shard_map/pallas_call | solution.py:321
  102.4 18.5 %all-to-all-done.2.states.starts = bf16[4,256,512]{2,1,0:T(8,128)(2,1)S(1)} async-done(((bf16[4,256,512]{2,1,0:T(8,128)(2,1)}), bf16[4,256,512]{2,1,0:T(8,128)(2,1)S(1)}, u32[]{:S(2)}, u32[]{:S(2)}) %all-to-all-start.2) | async-done | bytes 1048608 | tf_op jit(solution)/shard_map/all_to_all | solution.py:337
  122.8 10.4 %all_to_all.35.all_c = bf16[8,128,128]{2,1,0:T(8,128)(2,1)S(1)} all-to-all(bf16[8,128,128]{2,1,0:T(8,128)(2,1)S(1)} %get-tuple-element.84), channel_id=1, replica_groups=mesh['seq'=16,'tensor'=4,'dp'=8] {'dp'}, dimensions={0} | all-to-all | bytes 524288 | tf_op jit(solution)/shard_map/all_to_all | solution.py:337
  133.2 2.0 shard_map.187
  135.1 11.3 %all-to-all-start.4 = ((bf16[16,64,128]{2,1,0:T(8,128)(2,1)}), bf16[16,64,128]{2,1,0:T(8,128)(2,1)S(1)}, u32[]{:S(2)}, u32[]{:S(2)}) async-start(bf16[16,64,128]{2,1,0:T(8,128)(2,1)} %shard_map.187), calls=%async_computation.4 | async-start | bytes 524288 | tf_op jit(solution)/shard_map/all_to_all | solution.py:337
  147.7 4.0 %shard_map.185 = (bf16[128,2048]{1,0:T(8,128)(2,1)}, bf16[128,128]{1,0:T(8,128)(2,1)}, f32[8,128]{1,0:T(8,128)S(1)}) custom-call(bf16[4,256,512]{2,1,0:T(8,128)(2,1)S(1)} %all-to-all-done.2.states.starts, bf16[128,2048]{1,0:T(8,128)(2,1)S(1)} %bitcast.21, bf16[128,2048]{1,0:T(8,128)(2,1)S(1)} %bitcast.24, bf16[128,2048]{1,0:T(8,128)(2,1)S(1)} %get-tuple-element.73.xt, ...), custom_call_target="tpu_custom_call" | custom-call | flops 201326592 | bytes 4562944 | tf_op jit(solution)/shard_map/pallas_call | solution.py:321
  151.7 7.7 %all-to-all-done.4.parts = bf16[16,64,128]{2,1,0:T(8,128)(2,1)S(1)} async-done(((bf16[16,64,128]{2,1,0:T(8,128)(2,1)}), bf16[16,64,128]{2,1,0:T(8,128)(2,1)S(1)}, u32[]{:S(2)}, u32[]{:S(2)}) %all-to-all-start.4) | async-done | bytes 262176 | tf_op jit(solution)/shard_map/all_to_all | solution.py:337
  159.6 22.5 %all_to_all.36.got = f32[16,8,128]{2,1,0:T(8,128)S(1)} all-to-all(f32[16,8,128]{2,1,0:T(8,128)S(1)} %get-tuple-element.89), channel_id=1, replica_groups=mesh['seq'=16,'tensor'=4,'dp'=8] {'seq'}, dimensions={0} | all-to-all | bytes 131072 | tf_op jit(solution)/shard_map/all_to_all | solution.py:337
  182.1 12.6 %all_to_all.37.got = f32[32,8,128]{2,1,0:T(8,128)S(1)} all-to-all(f32[32,8,128]{2,1,0:T(8,128)S(1)} %shard_map.189), channel_id=1, replica_groups=mesh['seq'=16,'tensor'=4,'dp'=8] {'tensor','dp'}, dimensions={0} | all-to-all | bytes 262144 | tf_op jit(solution)/shard_map/all_to_all | solution.py:337
  (64 shorter events, 19.4 us)
Async XLA Ops:
  4.8 6.7 %copy-start.6 = (bf16[1,128,2048]{2,1,0:T(8,128)(2,1)S(1)}, bf16[1,128,2048]{2,1,0:T(8,128)(2,1)}, u32[]{:S(2)}) copy-start(bf16[1,128,2048]{2,1,0:T(8,128)(2,1)} %param.20) | copy-start | bytes 1572868
  4.8 34.9 %all-to-all-start = ((bf16[4,272,512]{2,1,0:T(8,128)(2,1)}), bf16[4,272,512]{2,1,0:T(8,128)(2,1)S(1)}, u32[]{:S(2)}, u32[]{:S(2)}) async-start(bf16[4,272,512]{2,1,0:T(8,128)(2,1)} %get-tuple-element.53), calls=%async_computation | async-start | bytes 2228224 | tf_op jit(solution)/shard_map/all_to_all | solution.py:337
  12.3 18.5 %collective-permute-start = (bf16[256,128]{1,0:T(8,128)(2,1)S(1)}, bf16[256,128]{1,0:T(8,128)(2,1)S(1)}, u32[]{:S(2)}, u32[]{:S(2)}) collective-permute-start(bf16[256,128]{1,0:T(8,128)(2,1)S(1)} %get-tuple-element.55), channel_id=1, source_target_pairs={{0,1},{1,0},{2,3},{3,2},{4,5},{5,4},{6,7},{7,6},{8,9},{9,8},{10,11... | collective-permute-start | bytes 196616 | tf_op jit(solution)/shard_map/ppermute | solution.py:342
  18.1 14.6 %collective-permute-start.1 = (bf16[256,128]{1,0:T(8,128)(2,1)S(1)}, bf16[256,128]{1,0:T(8,128)(2,1)S(1)}, u32[]{:S(2)}, u32[]{:S(2)}) collective-permute-start(bf16[256,128]{1,0:T(8,128)(2,1)S(1)} %get-tuple-element.56), channel_id=1, source_target_pairs={{0,2},{1,3},{2,0},{3,1},{4,6},{5,7},{6,4},{7,5},{8,10},{9,11},{10,... | collective-permute-start | bytes 196616 | tf_op jit(solution)/shard_map/ppermute | solution.py:342
  20.1 17.4 %collective-permute-start.2 = (bf16[256,128]{1,0:T(8,128)(2,1)S(1)}, bf16[256,128]{1,0:T(8,128)(2,1)S(1)}, u32[]{:S(2)}, u32[]{:S(2)}) collective-permute-start(bf16[256,128]{1,0:T(8,128)(2,1)S(1)} %get-tuple-element.57), channel_id=1, source_target_pairs={{0,3},{1,2},{2,1},{3,0},{4,7},{5,6},{6,5},{7,4},{8,11},{9,10},{10,... | collective-permute-start | bytes 196616 | tf_op jit(solution)/shard_map/ppermute | solution.py:342
  23.6 13.9 %collective-permute-start.3 = (bf16[256,128]{1,0:T(8,128)(2,1)S(1)}, bf16[256,128]{1,0:T(8,128)(2,1)S(1)}, u32[]{:S(2)}, u32[]{:S(2)}) collective-permute-start(bf16[256,128]{1,0:T(8,128)(2,1)S(1)} %get-tuple-element.58), channel_id=1, source_target_pairs={{0,4},{1,5},{2,6},{3,7},{4,0},{5,1},{6,2},{7,3},{8,12},{9,13},{10,... | collective-permute-start | bytes 196616 | tf_op jit(solution)/shard_map/ppermute | solution.py:342
  25.6 12.0 %collective-permute-start.4 = (bf16[256,128]{1,0:T(8,128)(2,1)S(1)}, bf16[256,128]{1,0:T(8,128)(2,1)S(1)}, u32[]{:S(2)}, u32[]{:S(2)}) collective-permute-start(bf16[256,128]{1,0:T(8,128)(2,1)S(1)} %get-tuple-element.59), channel_id=1, source_target_pairs={{0,5},{1,4},{2,7},{3,6},{4,1},{5,0},{6,3},{7,2},{8,13},{9,12},{10,... | collective-permute-start | bytes 196616 | tf_op jit(solution)/shard_map/ppermute | solution.py:342
  30.8 6.8 %collective-permute-start.5 = (bf16[256,128]{1,0:T(8,128)(2,1)S(1)}, bf16[256,128]{1,0:T(8,128)(2,1)S(1)}, u32[]{:S(2)}, u32[]{:S(2)}) collective-permute-start(bf16[256,128]{1,0:T(8,128)(2,1)S(1)} %get-tuple-element.60), channel_id=1, source_target_pairs={{0,6},{1,7},{2,4},{3,5},{4,2},{5,3},{6,0},{7,1},{8,14},{9,15},{10,... | collective-permute-start | bytes 196616 | tf_op jit(solution)/shard_map/ppermute | solution.py:342
  32.8 6.9 %collective-permute-start.6 = (bf16[256,128]{1,0:T(8,128)(2,1)S(1)}, bf16[256,128]{1,0:T(8,128)(2,1)S(1)}, u32[]{:S(2)}, u32[]{:S(2)}) collective-permute-start(bf16[256,128]{1,0:T(8,128)(2,1)S(1)} %get-tuple-element.61), channel_id=1, source_target_pairs={{0,7},{1,6},{2,5},{3,4},{4,3},{5,2},{6,1},{7,0},{8,15},{9,14},{10,... | collective-permute-start | bytes 196616 | tf_op jit(solution)/shard_map/ppermute | solution.py:342
  41.4 47.2 %all-to-all-start.1 = ((bf16[4,144,512]{2,1,0:T(8,128)(2,1)}), bf16[4,144,512]{2,1,0:T(8,128)(2,1)S(1)}, u32[]{:S(2)}, u32[]{:S(2)}) async-start(bf16[4,144,512]{2,1,0:T(8,128)(2,1)} %shard_map.181), calls=%async_computation.1 | async-start | bytes 1179648 | tf_op jit(solution)/shard_map/all_to_all | solution.py:337
  53.5 14.7 %collective-permute-start.7 = (bf16[8,256,128]{2,1,0:T(8,128)(2,1)S(1)}, bf16[8,256,128]{2,1,0:T(8,128)(2,1)S(1)}, u32[]{:S(2)}, u32[]{:S(2)}) collective-permute-start(bf16[8,256,128]{2,1,0:T(8,128)(2,1)S(1)} %shard_map.182.refs_0_), channel_id=1, source_target_pairs={{0,8},{8,0},{16,24},{24,16},{1,9},{9,1},{17,25},{25,17},{2,10},{10... | collective-permute-start | bytes 1572872 | tf_op jit(solution)/shard_map/ppermute | solution.py:342
  56.7 25.2 %collective-permute-start.8 = (bf16[8,256,128]{2,1,0:T(8,128)(2,1)S(1)}, bf16[8,256,128]{2,1,0:T(8,128)(2,1)S(1)}, u32[]{:S(2)}, u32[]{:S(2)}) collective-permute-start(bf16[8,256,128]{2,1,0:T(8,128)(2,1)S(1)} %shard_map.182.refs_0_), channel_id=1, source_target_pairs={{0,16},{8,24},{16,0},{24,8},{1,17},{9,25},{17,1},{25,9},{2,18},{10... | collective-permute-start | bytes 1572872 | tf_op jit(solution)/shard_map/ppermute | solution.py:342
  61.3 26.5 %collective-permute-start.9 = (bf16[8,256,128]{2,1,0:T(8,128)(2,1)S(1)}, bf16[8,256,128]{2,1,0:T(8,128)(2,1)S(1)}, u32[]{:S(2)}, u32[]{:S(2)}) collective-permute-start(bf16[8,256,128]{2,1,0:T(8,128)(2,1)S(1)} %shard_map.182.refs_0_), channel_id=1, source_target_pairs={{0,24},{8,16},{16,8},{24,0},{1,25},{9,17},{17,9},{25,1},{2,26},{10... | collective-permute-start | bytes 1572872 | tf_op jit(solution)/shard_map/ppermute | solution.py:342
  90.7 5.0 %copy-start.16 = (f32[128,128]{1,0:T(8,128)S(1)}, f32[128,128]{1,0:T(8,128)}, u32[]{:S(2)}) copy-start(f32[128,128]{1,0:T(8,128)} %get-tuple-element.72.cum) | copy-start | bytes 196612
  90.7 30.1 %all-to-all-start.2 = ((bf16[4,256,512]{2,1,0:T(8,128)(2,1)}), bf16[4,256,512]{2,1,0:T(8,128)(2,1)S(1)}, u32[]{:S(2)}, u32[]{:S(2)}) async-start(bf16[4,256,512]{2,1,0:T(8,128)(2,1)} %shard_map.183), calls=%async_computation.2 | async-start | bytes 2097152 | tf_op jit(solution)/shard_map/all_to_all | solution.py:337
  121.9 11.3 %copy-start.8 = (bf16[8,256,128]{2,1,0:T(8,128)(2,1)S(1)}, bf16[8,256,128]{2,1,0:T(8,128)(2,1)}, u32[]{:S(2)}) copy-start(bf16[8,256,128]{2,1,0:T(8,128)(2,1)} %copy-done.7) | copy-start | bytes 1572868
  121.9 11.3 %copy-start.10 = (bf16[8,256,128]{2,1,0:T(8,128)(2,1)S(1)}, bf16[8,256,128]{2,1,0:T(8,128)(2,1)}, u32[]{:S(2)}) copy-start(bf16[8,256,128]{2,1,0:T(8,128)(2,1)} %copy-done.9) | copy-start | bytes 1572868
  121.9 11.3 %copy-start.12 = (bf16[8,256,128]{2,1,0:T(8,128)(2,1)S(1)}, bf16[8,256,128]{2,1,0:T(8,128)(2,1)}, u32[]{:S(2)}) copy-start(bf16[8,256,128]{2,1,0:T(8,128)(2,1)} %copy-done.11) | copy-start | bytes 1572868
  133.2 13.3 %copy-start.15 = (f32[128,128]{1,0:T(8,128)S(1)}, f32[128,128]{1,0:T(8,128)}, u32[]{:S(2)}) copy-start(f32[128,128]{1,0:T(8,128)} %get-tuple-element.74.loga) | copy-start | bytes 196612
  133.2 13.3 %copy-start.20 = (f32[8,128]{1,0:T(8,128)S(1)}, f32[8,128]{1,0:T(8,128)}, u32[]{:S(2)}) copy-start(f32[8,128]{1,0:T(8,128)} %get-tuple-element.75.onehot) | copy-start | bytes 12292
  135.1 24.2 %all-to-all-start.4 = ((bf16[16,64,128]{2,1,0:T(8,128)(2,1)}), bf16[16,64,128]{2,1,0:T(8,128)(2,1)S(1)}, u32[]{:S(2)}, u32[]{:S(2)}) async-start(bf16[16,64,128]{2,1,0:T(8,128)(2,1)} %shard_map.187), calls=%async_computation.4 | async-start | bytes 524288 | tf_op jit(solution)/shard_map/all_to_all | solution.py:337
  147.7 47.0 %copy-start.17 = (f32[64,128]{1,0:T(8,128)S(1)}, f32[64,128]{1,0:T(8,128)}, u32[]{:S(2)}) copy-start(f32[64,128]{1,0:T(8,128)} %weight.1) | copy-start | bytes 98308
  147.7 47.0 %copy-start.18 = (f32[64,128]{1,0:T(8,128)S(1)}, f32[64,128]{1,0:T(8,128)}, u32[]{:S(2)}) copy-start(f32[64,128]{1,0:T(8,128)} %moment_one.1) | copy-start | bytes 98308
  147.7 47.0 %copy-start.19 = (f32[64,128]{1,0:T(8,128)S(1)}, f32[64,128]{1,0:T(8,128)}, u32[]{:S(2)}) copy-start(f32[64,128]{1,0:T(8,128)} %moment_two.1) | copy-start | bytes 98308
  (12 other events, 31.3 us)

commit v3 on v2

--- a/solution.py
+++ b/solution.py
@@ -64,37 +64,39 @@
     return rows[0:1] + rows[1:2] + rows[2:3]
 
 
-def states_kernel(dt_t, lev, rate_t, x, dy, b, c, st, loga, cum, onehot):
+def states_kernel(dt_t, lev, rate_t, x, dy, b, c, st, loga, cum, onehot, b_t, c_t):
     heads = dt_t.shape[0]
     levels = rate_t.shape[0]
-    hit = iota((levels, heads), 0) == lev[...]
-    onehot[...] = jnp.zeros_like(onehot)
-    onehot[:levels, :heads] = jnp.where(hit, 1.0, 0.0)
-    cum[...] = jnp.zeros_like(cum)
-    cum[:levels, :heads] = jnp.where(hit, rate_t[...], 0.0)
-    rate = jnp.sum(cum[:levels, :], axis=0, keepdims=True)
-    cum[:heads, :] = dt_t[...]
-    cum[heads:, :] = jnp.zeros_like(cum[heads:, :])
-    loga[...] = -rate * cum[...].T
-    lower = (iota((SPAN, SPAN), 0) >= iota((SPAN, SPAN), 1)).astype(f32)
-    total = jnp.dot(lower, loga[...], precision=HIGHEST, preferred_element_type=f32)
-    cum[...] = total
+    step = pl.program_id(0)
+
+    @pl.when(step == 0)
+    def _():
+        hit = iota((levels, heads), 0) == lev[...]
+        onehot[...] = jnp.zeros_like(onehot)
+        onehot[:levels, :heads] = jnp.where(hit, 1.0, 0.0)
+        cum[...] = jnp.zeros_like(cum)
+        cum[:levels, :heads] = jnp.where(hit, rate_t[...], 0.0)
+        rate = jnp.sum(cum[:levels, :], axis=0, keepdims=True)
+        cum[:heads, :] = dt_t[...]
+        loga[...] = -rate * cum[...].T
+        lower = (iota((SPAN, SPAN), 0) >= iota((SPAN, SPAN), 1)).astype(f32)
+        cum[...] = jnp.dot(lower, loga[...], precision=HIGHEST, preferred_element_type=f32)
+        b_t[...] = b[...].astype(f32).T.astype(bf16)
+        c_t[...] = c[...].astype(f32).T.astype(bf16)
+
+    count = st.shape[2] // P_SIZE
+    total = pltpu.roll(cum[...], (128 - step * count) % 128, 1)
     last = total[SPAN - 1 :, :]
     tail = jnp.exp(last - total)
     grow = jnp.exp(total)
-    b_t = b[...].astype(f32).T.astype(bf16)
-    c_t = c[...].astype(f32).T.astype(bf16)
     first = first_head()
-    heads_piece = heads // st.shape[0]
-    for j in range(heads // 2):
-        piece, at = 2 * j // heads_piece, 2 * j % heads_piece * P_SIZE
+    for j in range(count // 2):
         lanes = slice(j * PAIR, (j + 1) * PAIR)
-        spot = slice(at, at + PAIR)
         xs = (x[:, lanes].astype(f32) * spread(tail, j, first)).astype(bf16)
         ds = (dy[:, lanes].astype(f32) * spread(grow, j, first)).astype(bf16)
-        st[piece, :N, spot] = dot(b_t, xs).astype(bf16)
-        st[piece, N : 2 * N, spot] = dot(c_t, ds).astype(bf16)
-        st[piece, 2 * N :, spot] = log_rows(spread(last, j, first))
+        st[0, :N, lanes] = dot(b_t[...], xs).astype(bf16)
+        st[0, N : 2 * N, lanes] = dot(c_t[...], ds).astype(bf16)
+        st[0, 2 * N :, lanes] = log_rows(spread(last, j, first))
 
 
 def group_kernel(me, got, out):
@@ -115,7 +117,8 @@
             out[k, N:, lanes] = rows
 
 
-def scan_kernel(me, got, groups, out):
+def scan_kernel(me, got, groups, ahead, *refs):
+    backs, held = refs[:-1], refs[-1]
     here = me[0] // GROUP
     count = got.shape[0]
     for at in range(0, got.shape[2], PAIR):
@@ -129,15 +132,16 @@
             new = jnp.exp(row_logs(groups[k, N:, lanes])) * back + groups[k, :N, lanes].astype(f32)
             back = jnp.where(k > here, new, back)
         for k in range(count):
-            out[k, :N, lanes] = state.astype(bf16)
+            ahead[k, :, lanes] = state.astype(bf16)
             state = decay[k] * state + got[k, :N, lanes].astype(f32)
         for k in reversed(range(count)):
-            out[k, N:, lanes] = back.astype(bf16)
+            held[k, :, lanes] = back.astype(bf16)
             back = decay[k] * back + got[k, N : 2 * N, lanes].astype(f32)
-
-
-def feature_kernel(rows, me, layer, *refs):
-    outs, held = refs[:-1], refs[-1]
+    for k, out in enumerate(backs):
+        out[...] = held[(me[0] % GROUP) ^ k]
+
+
+def feature_kernel(rows, me, layer, keep, send, held):
     streams = held.shape[0]
     for at in range(0, layer.shape[1], PAIR):
         turned = layer[:, at : at + PAIR].astype(f32).T.astype(bf16)
@@ -145,24 +149,35 @@
             index = (at + part) // rows
             stream, spot = index % streams, index // streams * rows
             held[stream, spot : spot + rows, :] = turned[part : part + rows, :]
+    for k in range(keep.shape[0]):
+        keep[k] = held[me[1] ^ (2 * k)]
+        send[k] = held[me[1] ^ (2 * k + 1)]
+
+
+def pair_kernel(keep, got, *outs):
     for k, out in enumerate(outs):
-        out[...] = held[me[1] ^ k]
+        out[0] = keep[k]
+        out[1] = got[k]
 
 
 def stack_kernel(*refs):
     for k, part in enumerate(refs[:-1]):
-        refs[-1][k] = part[...]
-
-
-def weight_kernel(me, all_c, *refs):
+        refs[-1][2 * k] = part[0]
+        refs[-1][2 * k + 1] = part[1]
+
+
+def weight_kernel(plan, me, all_c, *refs):
     features, out = refs[:-1], refs[-1]
     rows = out.shape[1]
-    for k, block in enumerate(features):
-        total = dot(block[0], all_c[me[1]])
-        for j in range(1, block.shape[0]):
-            total = total + dot(block[j], all_c[me[1] ^ j])
-        for q in range(block.shape[1] // rows):
-            out[(me[2] ^ k) * (block.shape[1] // rows) + q] = total[q * rows : (q + 1) * rows].astype(bf16)
+    for k, blocks in plan:
+        total = None
+        for index, begin in blocks:
+            for j in range(features[index].shape[0]):
+                term = dot(features[index][j], all_c[me[1] ^ (begin + j)])
+                total = term if total is None else total + term
+        count = total.shape[0] // rows
+        for q in range(count):
+            out[(me[2] ^ k) * count + q] = total[q * rows : (q + 1) * rows].astype(bf16)
 
 
 def intra_kernel(cum, x, dy, b, c, skip, dxp, xt, dye, dc, db, dcum, rows):
@@ -214,7 +229,7 @@
     total = dc[...]
     pieces, width = starts.shape[0], starts.shape[2]
     for j in range(pieces):
-        total = total + dot_nt(dye[:, j * width : (j + 1) * width], starts[j, :N, :])
+        total = total + dot_nt(dye[:, j * width : (j + 1) * width], starts[j])
     out = total.astype(bf16)
     grad_c[...] = out
     for k in range(copies.shape[0]):
@@ -227,10 +242,12 @@
 
 
 def rest_kernel(
-    states, x, dy, xt, cum, loga, onehot, b, c, dxp, db, dcum, grad_x, grad_b, small
+    me, starts, end_a, end_b, end_c, end_d, x, dy, xt, cum, loga, onehot, b, c, dxp, db, dcum, grad_x, grad_b, small, ends
 ):
     heads = x.shape[1] // P_SIZE
-    pairs_piece = states.shape[2] // PAIR
+    pairs_piece = starts.shape[2] // PAIR
+    for k, part in enumerate((end_a, end_b, end_c, end_d)):
+        ends[(me[0] % GROUP) ^ k] = part[...]
     total = cum[...]
     last = total[SPAN - 1 :, :]
     tail = jnp.exp(last - total)
@@ -246,7 +263,7 @@
     for j in range(heads // 2):
         piece, at = j // pairs_piece, j % pairs_piece * PAIR
         lanes = slice(j * PAIR, (j + 1) * PAIR)
-        start, stop = states[piece, :N, at : at + PAIR], states[piece, N:, at : at + PAIR]
+        start, stop = starts[piece, :, at : at + PAIR], ends[piece, :, at : at + PAIR]
         xs = xt[:, lanes]
         x_wide, dy_wide = x[:, lanes].astype(f32), dy[:, lanes].astype(f32)
         falling = spread(tail, j, first)
@@ -314,23 +331,29 @@
     new_s[...] = second
 
 
-def call(kernel, out_shapes, *args, scratch=(), flops=0, limit=32):
+def call(kernel, out_shapes, *args, scratch=(), flops=0, limit=60, **grid):
     size = sum(math.prod(a.shape) * a.dtype.itemsize for a in (*args, *out_shapes))
-    whole = pl.BlockSpec(memory_space=pltpu.VMEM)
-    scalars = pl.BlockSpec(memory_space=pltpu.SMEM)
+    if not grid:
+        whole = pl.BlockSpec(memory_space=pltpu.VMEM)
+        scalars = pl.BlockSpec(memory_space=pltpu.SMEM)
+        grid = {"in_specs": [scalars if a.shape == (3,) else whole for a in args]}
     out = pl.pallas_call(
         kernel,
         out_shape=tuple(out_shapes),
-        in_specs=[scalars if a.shape == (3,) else whole for a in args],
         scratch_shapes=list(scratch),
         compiler_params=pltpu.CompilerParams(vmem_limit_bytes=limit * 1024 * 1024),
         cost_estimate=pl.CostEstimate(flops=flops, bytes_accessed=size, transcendentals=0),
+        **grid,
     )(*args)
     return out[0] if len(out_shapes) == 1 else out
 
 
 def shaped(shape, dtype):
     return jax.ShapeDtypeStruct(shape, dtype)
+
+
+def fixed(shape):
+    return pl.BlockSpec(shape, lambda i: (0,) * len(shape))
 
 
 def swap(a, axis, groups=None):
@@ -377,27 +400,46 @@
         dy,
         b,
         c,
+        scratch=[pltpu.VMEM((N, SPAN), bf16)] * 2,
         flops=4 * SPAN * N * width,
-        limit=60,
+        grid=(GROUP,),
+        in_specs=[
+            fixed((heads, SPAN)),
+            fixed((1, heads)),
+            fixed(decay_rate.T.shape),
+            pl.BlockSpec((SPAN, piece), lambda i: (0, i)),
+            pl.BlockSpec((SPAN, piece), lambda i: (0, i)),
+            fixed((SPAN, N)),
+            fixed((SPAN, N)),
+        ],
+        out_specs=(
+            pl.BlockSpec((1, 2 * N + LOG_ROWS, piece), lambda i: (i, 0, 0)),
+            fixed((SPAN, 128)),
+            fixed((SPAN, 128)),
+            fixed((8, 128)),
+        ),
     )
     layer, st = lax.optimization_barrier((layer_input[0], st))
     got = swap(st, "seq", near)
 
     rows = weight_c.shape[0]
     block = layer.shape[1] // streams
-    pieces = call(
+    half = max(streams // 2, 1)
+    keep, send = call(
         functools.partial(feature_kernel, rows),
-        [shaped((block, SPAN), bf16)] * streams,
+        [shaped((half, block, SPAN), bf16)] * 2,
         me,
         layer,
         scratch=[pltpu.VMEM((streams, block, SPAN), bf16)],
-        flops=0,
-    )
-    pieces = [pieces] if streams == 1 else pieces
-    arrived = [trade(pieces[k], "dp", k) for k in range(1, streams)]
-    got, *arrived = lax.optimization_barrier((got, *arrived))
-    mine = call(stack_kernel, [shaped((streams, block, SPAN), bf16)], pieces[0], *arrived)
-    features = [trade(mine, "tensor", k) for k in range(1, tensors)]
+    )
+    pairs = call(
+        pair_kernel, [shaped((2, block, SPAN), bf16)] * half, keep, trade(send, "dp", 1)
+    )
+    pairs = [pairs] if half == 1 else pairs
+    pairs = [pairs[0]] + [trade(pairs[k], "dp", 2 * k) for k in range(1, half)]
+    got, *pairs = lax.optimization_barrier((got, *pairs))
+    mine = call(stack_kernel, [shaped((streams, block, SPAN), bf16)], *pairs)
+    left, right = trade(mine, "tensor", 1), trade(mine, "tensor", 3)
 
     dxp, xt, dye, dc, db, dcum = call(
         intra_kernel,
@@ -419,39 +461,51 @@
         flops=8 * N * width,
     )
     groups = swap(ahead, "seq", far)
-    groups, *features = lax.optimization_barrier((groups, *features))
-    features = [mine, *features]
-    states = call(
+    groups, left, right = lax.optimization_barrier((groups, left, right))
+    far_a = trade(right[:half], "tensor", 1)
+    far_b = trade(left[half:], "tensor", 3)
+    plan = ((0, ((0, 0),)), (1, ((1, 0),)), (3, ((2, 0),)), (2, ((3, 0), (4, half))))
+    starts, *ends = call(
         scan_kernel,
-        [shaped((GROUP, 2 * N, piece), bf16)],
+        [shaped((GROUP, N, piece), bf16)] + [shaped((N, piece), bf16)] * GROUP,
         me,
         got,
         groups,
+        scratch=[pltpu.VMEM((GROUP, N, piece), bf16)],
         flops=8 * N * width,
     )
-    states = swap(states, "seq", near)
+    starts = swap(starts, "seq", near)
+    starts, far_a, far_b = lax.optimization_barrier((starts, far_a, far_b))
     grad_c, copies = call(
         grad_c_kernel,
         [shaped((SPAN, N), bf16), shaped((streams, SPAN, N), bf16)],
         dc,
         dye,
-        states,
+        starts,
         flops=2 * SPAN * N * width,
     )
+    copies, *ends = lax.optimization_barrier((copies, *ends))
+    ends = [ends[0]] + [trade(ends[k], "seq", k) for k in range(1, GROUP)]
     all_c = swap(copies, "dp")
     partial = call(
-        weight_kernel,
+        functools.partial(weight_kernel, plan),
         [shaped((seqs, rows, N), bf16)],
         me,
         all_c,
-        *features,
+        mine,
+        left,
+        right,
+        far_a,
+        far_b,
         flops=2 * tensors * layer.shape[1] * SPAN * N,
     )
     parts = swap(partial, "seq")
     grad_x, grad_b, small = call(
         rest_kernel,
         [wide, shaped((SPAN, N), bf16), small_tile],
-        states,
+        me,
+        starts,
+        *ends,
         x,
         dy,
         xt,
@@ -463,6 +517,7 @@
         dxp,
         db,
         dcum,
+        scratch=[pltpu.VMEM((GROUP, N, piece), bf16)],
         flops=6 * SPAN * N * width,
     )
     shard, sums = call(

time: 197 us -> 209 us (1.061)
  Pallas kernels: 22.1 us -> 40.1 us
  waiting for transfers between devices: 51.3 us -> 41.7 us
  blocking collectives: 45.4 us -> 52.6 us
  starting transfers between devices: 69.7 us -> 66.8 us
    pallas_call x12 -> x13, Pallas kernels: 22.1 us -> 40.1 us  [call(): pl.pallas_call(kernel, out_shape=tuple(out_shapes), scratch_shapes=list(s...]
    all_to_all x4, waiting for transfers between devices: 26.2 us -> 11.5 us  [swap(): return lax.all_to_all(a, axis, 0, 0, tiled=True, axis_index_groups=groups)]
    all_to_all x3, blocking collectives: 45.4 us -> 52.6 us  [swap(): return lax.all_to_all(a, axis, 0, 0, tiled=True, axis_index_groups=groups)]
    all_to_all x4, starting transfers between devices: 34.9 us -> 29 us  [swap(): return lax.all_to_all(a, axis, 0, 0, tiled=True, axis_index_groups=groups)]
    ppermute x10 -> x11, waiting for transfers between devices: 25.1 us -> 30.2 us  [trade(): return lax.ppermute(a, axis, [(i, i ^ k) for i in range(count)])]
    ppermute x10 -> x11, starting transfers between devices: 34.8 us -> 37.8 us  [trade(): return lax.ppermute(a, axis, [(i, i ^ k) for i in range(count)])]
    unnamed x44 -> x36, local copies, waits for them, and re-layouts: 6.51 us -> 4.77 us
  transfers between devices with their start and end apart: 14 -> 15, of which waited for: 7 -> 9; matrix products, arithmetic and copies ran while one was open for 0% -> 0% of each run, Pallas kernels for 5% -> 9%
where the time goes in v3:
time: 209 us; the launch traced here: 208 us
  starting transfers between devices  66.8 us (32%)
  blocking collectives  52.6 us (25%)
  waiting for transfers between devices  41.7 us (20%)
  Pallas kernels  40.1 us (19%)
  local copies, waits for them, and re-layouts  4.81 us (2%)
    all_to_all x3, blocking collectives, swap(): return lax.all_to_all(a, axis, 0, 0, tiled=True, axis_index_groups=groups)  52.6 us
    pallas_call x13, Pallas kernels, call(): pl.pallas_call(kernel, out_shape=tuple(out_shapes), scratch_shapes=list(s...  40.1 us
    ppermute x11, starting transfers between devices, trade(): return lax.ppermute(a, axis, [(i, i ^ k) for i in range(count)])  37.8 us
    ppermute x11, waiting for transfers between devices, trade(): return lax.ppermute(a, axis, [(i, i ^ k) for i in range(count)])  30.2 us
    all_to_all x4, starting transfers between devices, swap(): return lax.all_to_all(a, axis, 0, 0, tiled=True, axis_index_groups=groups)  29 us
    all_to_all x4, waiting for transfers between devices, swap(): return lax.all_to_all(a, axis, 0, 0, tiled=True, axis_index_groups=groups)  11.5 us
    unnamed x36, local copies, waits for them, and re-layouts  4.77 us
  transfers between devices with their start and end apart: 15, of which 9 were waited for; matrix products, arithmetic and copies ran while one was open for 0% of the time, Pallas kernels for 9%

profile of v3, /device:TPU:1, one launch (start us, length us, event | category | flops | bytes accessed | tf_op | source)
XLA Modules:
  0.0 207.6 jit_solution(18337473374776206451)
XLA Ops:
  0.6 5.1 %shard_map.179 = (bf16[4,272,512]{2,1,0:T(8,128)(2,1)}, f32[128,128]{1,0:T(8,128)}, f32[128,128]{1,0:T(8,128)}, f32[8,128]{1,0:T(8,128)}) custom-call(f32[32,128]{1,0:T(8,128)} %bitcast.32, s32[1,32]{1,0:T(1,128)} %bitcast.34, f32[8,32]{1,0:T(8,128)} %bitcast.33, bf16[128,2048]{1,0:T(8,128)(2,1)} %bitcast.19, bf16[128,2048]{1,0:T(8,128)(2,1)} %bitcast.22, ...), custom_call_target="tpu_custom_call" | custom-call | flops 134217728 | bytes 2380928 | tf_op jit(solution)/shard_map/pallas_call | solution.py:340
  5.7 6.4 %all-to-all-start = ((bf16[4,272,512]{2,1,0:T(8,128)(2,1)}), bf16[4,272,512]{2,1,0:T(8,128)(2,1)S(1)}, u32[]{:S(2)}, u32[]{:S(2)}) async-start(bf16[4,272,512]{2,1,0:T(8,128)(2,1)} %get-tuple-element.60), calls=%async_computation | async-start | bytes 2228224 | tf_op jit(solution)/shard_map/all_to_all | solution.py:360
  14.9 5.9 %collective-permute-start = (bf16[4,256,128]{2,1,0:T(8,128)(2,1)}, bf16[4,256,128]{2,1,0:T(8,128)(2,1)S(1)}, u32[]{:S(2)}, u32[]{:S(2)}) collective-permute-start(bf16[4,256,128]{2,1,0:T(8,128)(2,1)} %get-tuple-element.63), channel_id=1, source_target_pairs={{0,1},{1,0},{2,3},{3,2},{4,5},{5,4},{6,7},{7,6},{8,9},{9,8},{10,11... | collective-permute-start | bytes 786440 | tf_op jit(solution)/shard_map/ppermute | solution.py:365
  26.6 2.5 %collective-permute-start.2 = (bf16[2,256,128]{2,1,0:T(8,128)(2,1)}, bf16[2,256,128]{2,1,0:T(8,128)(2,1)S(1)}, u32[]{:S(2)}, u32[]{:S(2)}) collective-permute-start(bf16[2,256,128]{2,1,0:T(8,128)(2,1)} %get-tuple-element.66), channel_id=1, source_target_pairs={{0,4},{1,5},{2,6},{3,7},{4,0},{5,1},{6,2},{7,3},{8,12},{9,13},{10,... | collective-permute-start | bytes 393224 | tf_op jit(solution)/shard_map/ppermute | solution.py:365
  29.1 5.1 %collective-permute-start.3 = (bf16[2,256,128]{2,1,0:T(8,128)(2,1)}, bf16[2,256,128]{2,1,0:T(8,128)(2,1)S(1)}, u32[]{:S(2)}, u32[]{:S(2)}) collective-permute-start(bf16[2,256,128]{2,1,0:T(8,128)(2,1)} %get-tuple-element.67), channel_id=1, source_target_pairs={{0,6},{1,7},{2,4},{3,5},{4,2},{5,3},{6,0},{7,1},{8,14},{9,15},{10,... | collective-permute-start | bytes 393224 | tf_op jit(solution)/shard_map/ppermute | solution.py:365
  41.8 13.1 %all-to-all-start.1 = ((bf16[4,144,512]{2,1,0:T(8,128)(2,1)}), bf16[4,144,512]{2,1,0:T(8,128)(2,1)S(1)}, u32[]{:S(2)}, u32[]{:S(2)}) async-start(bf16[4,144,512]{2,1,0:T(8,128)(2,1)} %shard_map.182), calls=%async_computation.1 | async-start | bytes 1179648 | tf_op jit(solution)/shard_map/all_to_all | solution.py:360
  56.9 4.6 %collective-permute-start.5 = (bf16[8,256,128]{2,1,0:T(8,128)(2,1)}, bf16[8,256,128]{2,1,0:T(8,128)(2,1)S(1)}, u32[]{:S(2)}, u32[]{:S(2)}) collective-permute-start(bf16[8,256,128]{2,1,0:T(8,128)(2,1)} %shard_map.183.refs_0_), channel_id=1, source_target_pairs={{0,24},{8,16},{16,8},{24,0},{1,25},{9,17},{17,9},{25,1},{2,26},{10... | collective-permute-start | bytes 1572872 | tf_op jit(solution)/shard_map/ppermute | solution.py:365
  63.5 8.6 %collective-permute-done.5.refs_2_ = bf16[8,256,128]{2,1,0:T(8,128)(2,1)S(1)} collective-permute-done((bf16[8,256,128]{2,1,0:T(8,128)(2,1)}, bf16[8,256,128]{2,1,0:T(8,128)(2,1)S(1)}, u32[]{:S(2)}, u32[]{:S(2)}) %collective-permute-start.5) | collective-permute-done | bytes 524320 | tf_op jit(solution)/shard_map/ppermute | solution.py:365
  72.1 3.0 %collective-permute-done.4.refs_1_ = bf16[8,256,128]{2,1,0:T(8,128)(2,1)S(1)} collective-permute-done((bf16[8,256,128]{2,1,0:T(8,128)(2,1)}, bf16[8,256,128]{2,1,0:T(8,128)(2,1)S(1)}, u32[]{:S(2)}, u32[]{:S(2)}) %collective-permute-start.4) | collective-permute-done | bytes 524320 | tf_op jit(solution)/shard_map/ppermute | solution.py:365
  75.1 10.5 %all-to-all-done.1.groups = bf16[4,144,512]{2,1,0:T(8,128)(2,1)S(1)} async-done(((bf16[4,144,512]{2,1,0:T(8,128)(2,1)}), bf16[4,144,512]{2,1,0:T(8,128)(2,1)S(1)}, u32[]{:S(2)}, u32[]{:S(2)}) %all-to-all-start.1) | async-done | bytes 589856 | tf_op jit(solution)/shard_map/all_to_all | solution.py:360
  86.4 2.8 %shard_map.184 = (bf16[4,128,512]{2,1,0:T(8,128)(2,1)}, bf16[128,512]{1,0:T(8,128)(2,1)}, bf16[128,512]{1,0:T(8,128)(2,1)}, bf16[128,512]{1,0:T(8,128)(2,1)}, bf16[128,512]{1,0:T(8,128)(2,1)}) custom-call(s32[3]{0:T(128)} %pad_add_fusion.me, bf16[4,272,512]{2,1,0:T(8,128)(2,1)} %copy-done, bf16[4,144,512]{2,1,0:T(8,128)(2,1)} %copy-done.2), custom_call_target="tpu_custom_call" | custom-call | flops 2097152 | bytes 2752524 | tf_op jit(solution)/shard_map/pallas_call | solution.py:340
  89.3 3.5 %all-to-all-start.2 = ((bf16[4,128,512]{2,1,0:T(8,128)(2,1)}), bf16[4,128,512]{2,1,0:T(8,128)(2,1)S(1)}, u32[]{:S(2)}, u32[]{:S(2)}) async-start(bf16[4,128,512]{2,1,0:T(8,128)(2,1)} %get-tuple-element.74), calls=%async_computation.2 | async-start | bytes 1048576 | tf_op jit(solution)/shard_map/all_to_all | solution.py:360
  92.8 4.7 %collective-permute-start.7 = (bf16[4,256,128]{2,1,0:T(8,128)(2,1)S(1)}, bf16[4,256,128]{2,1,0:T(8,128)(2,1)S(1)}, u32[]{:S(2)}, u32[]{:S(2)}) collective-permute-start(bf16[4,256,128]{2,1,0:T(8,128)(2,1)S(1)} %slice.7), channel_id=1, source_target_pairs={{0,24},{8,16},{16,8},{24,0},{1,25},{9,17},{17,9},{25,1},{2,26},{10... | collective-permute-start | bytes 786440 | tf_op jit(solution)/shard_map/ppermute | solution.py:365
  99.4 7.5 %shard_map.185 = (f32[128,2048]{1,0:T(8,128)}, bf16[128,2048]{1,0:T(8,128)(2,1)}, bf16[128,2048]{1,0:T(8,128)(2,1)}, f32[128,128]{1,0:T(8,128)}, f32[128,128]{1,0:T(8,128)}, /*index=5*/f32[128,128]{1,0:T(8,128)}) custom-call(f32[128,128]{1,0:T(8,128)} %get-tuple-element.78.cum, bf16[128,2048]{1,0:T(8,128)(2,1)} %bitcast.20, bf16[128,2048]{1,0:T(8,128)(2,1)} %bitcast.23, ...), custom_call_target="tpu_custom_call" | custom-call | flops 671088640 | bytes 3473536 | tf_op jit(solution)/shard_map/pallas_call | solution.py:340
  110.0 15.5 %all_to_all.35.all_c = bf16[8,128,128]{2,1,0:T(8,128)(2,1)} all-to-all(bf16[8,128,128]{2,1,0:T(8,128)(2,1)} %get-tuple-element.99), channel_id=1, replica_groups=mesh['seq'=16,'tensor'=4,'dp'=8] {'dp'}, dimensions={0} | all-to-all | bytes 524288 | tf_op jit(solution)/shard_map/all_to_all | solution.py:360
  125.5 3.1 %shard_map.188 = bf16[16,64,128]{2,1,0:T(8,128)(2,1)} custom-call(s32[3]{0:T(128)} %pad_add_fusion.me, bf16[8,128,128]{2,1,0:T(8,128)(2,1)} %all_to_all.35.all_c, bf16[8,256,128]{2,1,0:T(8,128)(2,1)} %shard_map.183.refs_0_, bf16[8,256,128]{2,1,0:T(8,128)(2,1)} %copy-done.4, bf16[8,256,128]{2,1,0:T(8,128)(2,1)} %copy-done.3, bf16[4,256,128]{2,1,0:T(8,128)(2,1)} %copy-done.8, ...), custom_call_target="tpu_custom_call" | custom-call | flops 268435456 | bytes 2621452 | tf_op jit(solution)/shard_map/pallas_call | solution.py:340
  128.6 5.9 %all-to-all-start.4 = ((bf16[16,64,128]{2,1,0:T(8,128)(2,1)}), bf16[16,64,128]{2,1,0:T(8,128)(2,1)S(1)}, u32[]{:S(2)}, u32[]{:S(2)}) async-start(bf16[16,64,128]{2,1,0:T(8,128)(2,1)} %shard_map.188), calls=%async_computation.4 | async-start | bytes 524288 | tf_op jit(solution)/shard_map/all_to_all | solution.py:360
  134.5 3.3 %collective-permute-start.8 = (bf16[128,512]{1,0:T(8,128)(2,1)S(1)}, bf16[128,512]{1,0:T(8,128)(2,1)S(1)}, u32[]{:S(2)}, u32[]{:S(2)}) collective-permute-start(bf16[128,512]{1,0:T(8,128)(2,1)S(1)} %copy-done.17), channel_id=1, source_target_pairs={{0,32},{32,0},{64,96},{96,64},{128,160},{160,128},{192,224},{224,1... | collective-permute-start | bytes 393224 | tf_op jit(solution)/shard_map/ppermute | solution.py:365
  137.8 4.0 %collective-permute-start.9 = (bf16[128,512]{1,0:T(8,128)(2,1)S(1)}, bf16[128,512]{1,0:T(8,128)(2,1)S(1)}, u32[]{:S(2)}, u32[]{:S(2)}) collective-permute-start(bf16[128,512]{1,0:T(8,128)(2,1)S(1)} %copy-done.16), channel_id=1, source_target_pairs={{0,64},{32,96},{64,0},{96,32},{128,192},{160,224},{192,128},{224,1... | collective-permute-start | bytes 393224 | tf_op jit(solution)/shard_map/ppermute | solution.py:365
  143.8 9.0 %collective-permute-done.8.end_b = bf16[128,512]{1,0:T(8,128)(2,1)S(1)} collective-permute-done((bf16[128,512]{1,0:T(8,128)(2,1)S(1)}, bf16[128,512]{1,0:T(8,128)(2,1)S(1)}, u32[]{:S(2)}, u32[]{:S(2)}) %collective-permute-start.8) | collective-permute-done | bytes 131104 | tf_op jit(solution)/shard_map/ppermute | solution.py:365
  152.8 5.1 %collective-permute-done.10.end_d = bf16[128,512]{1,0:T(8,128)(2,1)S(1)} collective-permute-done((bf16[128,512]{1,0:T(8,128)(2,1)S(1)}, bf16[128,512]{1,0:T(8,128)(2,1)S(1)}, u32[]{:S(2)}, u32[]{:S(2)}) %collective-permute-start.10) | collective-permute-done | bytes 131104 | tf_op jit(solution)/shard_map/ppermute | solution.py:365
  158.6 6.2 %shard_map.187 = (bf16[128,2048]{1,0:T(8,128)(2,1)}, bf16[128,128]{1,0:T(8,128)(2,1)}, f32[8,128]{1,0:T(8,128)}) custom-call(s32[3]{0:T(128)} %pad_add_fusion.me, bf16[4,128,512]{2,1,0:T(8,128)(2,1)} %copy-done.1, bf16[128,512]{1,0:T(8,128)(2,1)} %get-tuple-element.86.end_a, bf16[128,512]{1,0:T(8,128)(2,1)} %copy-done.9, bf16[128,512]{1,0:T(8,128)(2,1)} %copy-done.10, ...), custom_call_target="tpu_custom_call" | custom-call | flops 201326592 | bytes 4562956 | tf_op jit(solution)/shard_map/pallas_call | solution.py:340
  167.2 22.9 %all_to_all.36.got = f32[16,8,128]{2,1,0:T(8,128)} all-to-all(f32[16,8,128]{2,1,0:T(8,128)} %get-tuple-element.103), channel_id=1, replica_groups=mesh['seq'=16,'tensor'=4,'dp'=8] {'seq'}, dimensions={0} | all-to-all | bytes 131072 | tf_op jit(solution)/shard_map/all_to_all | solution.py:360
  191.6 14.1 %all_to_all.37.got = f32[32,8,128]{2,1,0:T(8,128)} all-to-all(f32[32,8,128]{2,1,0:T(8,128)} %shard_map.190), channel_id=1, replica_groups=mesh['seq'=16,'tensor'=4,'dp'=8] {'tensor','dp'}, dimensions={0} | all-to-all | bytes 262144 | tf_op jit(solution)/shard_map/all_to_all | solution.py:360
  (61 shorter events, 34.2 us)
Async XLA Ops:
  5.7 32.7 %all-to-all-start = ((bf16[4,272,512]{2,1,0:T(8,128)(2,1)}), bf16[4,272,512]{2,1,0:T(8,128)(2,1)S(1)}, u32[]{:S(2)}, u32[]{:S(2)}) async-start(bf16[4,272,512]{2,1,0:T(8,128)(2,1)} %get-tuple-element.60), calls=%async_computation | async-start | bytes 2228224 | tf_op jit(solution)/shard_map/all_to_all | solution.py:360
  14.9 7.2 %collective-permute-start = (bf16[4,256,128]{2,1,0:T(8,128)(2,1)}, bf16[4,256,128]{2,1,0:T(8,128)(2,1)S(1)}, u32[]{:S(2)}, u32[]{:S(2)}) collective-permute-start(bf16[4,256,128]{2,1,0:T(8,128)(2,1)} %get-tuple-element.63), channel_id=1, source_target_pairs={{0,1},{1,0},{2,3},{3,2},{4,5},{5,4},{6,7},{7,6},{8,9},{9,8},{10,11... | collective-permute-start | bytes 786440 | tf_op jit(solution)/shard_map/ppermute | solution.py:365
  24.6 9.6 %collective-permute-start.1 = (bf16[2,256,128]{2,1,0:T(8,128)(2,1)}, bf16[2,256,128]{2,1,0:T(8,128)(2,1)S(1)}, u32[]{:S(2)}, u32[]{:S(2)}) collective-permute-start(bf16[2,256,128]{2,1,0:T(8,128)(2,1)} %get-tuple-element.65), channel_id=1, source_target_pairs={{0,2},{1,3},{2,0},{3,1},{4,6},{5,7},{6,4},{7,5},{8,10},{9,11},{10,... | collective-permute-start | bytes 393224 | tf_op jit(solution)/shard_map/ppermute | solution.py:365
  26.6 8.3 %collective-permute-start.2 = (bf16[2,256,128]{2,1,0:T(8,128)(2,1)}, bf16[2,256,128]{2,1,0:T(8,128)(2,1)S(1)}, u32[]{:S(2)}, u32[]{:S(2)}) collective-permute-start(bf16[2,256,128]{2,1,0:T(8,128)(2,1)} %get-tuple-element.66), channel_id=1, source_target_pairs={{0,4},{1,5},{2,6},{3,7},{4,0},{5,1},{6,2},{7,3},{8,12},{9,13},{10,... | collective-permute-start | bytes 393224 | tf_op jit(solution)/shard_map/ppermute | solution.py:365
  29.1 8.3 %collective-permute-start.3 = (bf16[2,256,128]{2,1,0:T(8,128)(2,1)}, bf16[2,256,128]{2,1,0:T(8,128)(2,1)S(1)}, u32[]{:S(2)}, u32[]{:S(2)}) collective-permute-start(bf16[2,256,128]{2,1,0:T(8,128)(2,1)} %get-tuple-element.67), channel_id=1, source_target_pairs={{0,6},{1,7},{2,4},{3,5},{4,2},{5,3},{6,0},{7,1},{8,14},{9,15},{10,... | collective-permute-start | bytes 393224 | tf_op jit(solution)/shard_map/ppermute | solution.py:365
  34.3 20.7 %copy-start.12 = (bf16[2,256,128]{2,1,0:T(8,128)(2,1)}, bf16[2,256,128]{2,1,0:T(8,128)(2,1)S(1)}, u32[]{:S(2)}) copy-start(bf16[2,256,128]{2,1,0:T(8,128)(2,1)S(1)} %collective-permute-done.1.refs_1_) | copy-start | bytes 393220
  34.9 20.1 %copy-start.13 = (bf16[2,256,128]{2,1,0:T(8,128)(2,1)}, bf16[2,256,128]{2,1,0:T(8,128)(2,1)S(1)}, u32[]{:S(2)}) copy-start(bf16[2,256,128]{2,1,0:T(8,128)(2,1)S(1)} %collective-permute-done.2.refs_2_) | copy-start | bytes 393220
  37.4 17.6 %copy-start.14 = (bf16[2,256,128]{2,1,0:T(8,128)(2,1)}, bf16[2,256,128]{2,1,0:T(8,128)(2,1)S(1)}, u32[]{:S(2)}) copy-start(bf16[2,256,128]{2,1,0:T(8,128)(2,1)S(1)} %collective-permute-done.3.refs_3_) | copy-start | bytes 393220
  41.8 43.8 %all-to-all-start.1 = ((bf16[4,144,512]{2,1,0:T(8,128)(2,1)}), bf16[4,144,512]{2,1,0:T(8,128)(2,1)S(1)}, u32[]{:S(2)}, u32[]{:S(2)}) async-start(bf16[4,144,512]{2,1,0:T(8,128)(2,1)} %shard_map.182), calls=%async_computation.1 | async-start | bytes 1179648 | tf_op jit(solution)/shard_map/all_to_all | solution.py:360
  56.9 15.2 %collective-permute-start.5 = (bf16[8,256,128]{2,1,0:T(8,128)(2,1)}, bf16[8,256,128]{2,1,0:T(8,128)(2,1)S(1)}, u32[]{:S(2)}, u32[]{:S(2)}) collective-permute-start(bf16[8,256,128]{2,1,0:T(8,128)(2,1)} %shard_map.183.refs_0_), channel_id=1, source_target_pairs={{0,24},{8,16},{16,8},{24,0},{1,25},{9,17},{17,9},{25,1},{2,26},{10... | collective-permute-start | bytes 1572872 | tf_op jit(solution)/shard_map/ppermute | solution.py:365
  61.5 13.5 %collective-permute-start.4 = (bf16[8,256,128]{2,1,0:T(8,128)(2,1)}, bf16[8,256,128]{2,1,0:T(8,128)(2,1)S(1)}, u32[]{:S(2)}, u32[]{:S(2)}) collective-permute-start(bf16[8,256,128]{2,1,0:T(8,128)(2,1)} %shard_map.183.refs_0_), channel_id=1, source_target_pairs={{0,8},{8,0},{16,24},{24,16},{1,9},{9,1},{17,25},{25,17},{2,10},{10... | collective-permute-start | bytes 1572872 | tf_op jit(solution)/shard_map/ppermute | solution.py:365
  72.1 37.9 %copy-start.3 = (bf16[8,256,128]{2,1,0:T(8,128)(2,1)}, bf16[8,256,128]{2,1,0:T(8,128)(2,1)S(1)}, u32[]{:S(2)}) copy-start(bf16[8,256,128]{2,1,0:T(8,128)(2,1)S(1)} %collective-permute-done.5.refs_2_) | copy-start | bytes 1572868
  75.1 34.9 %copy-start.4 = (bf16[8,256,128]{2,1,0:T(8,128)(2,1)}, bf16[8,256,128]{2,1,0:T(8,128)(2,1)S(1)}, u32[]{:S(2)}) copy-start(bf16[8,256,128]{2,1,0:T(8,128)(2,1)S(1)} %collective-permute-done.4.refs_1_) | copy-start | bytes 1572868
  89.3 17.6 %all-to-all-start.2 = ((bf16[4,128,512]{2,1,0:T(8,128)(2,1)}), bf16[4,128,512]{2,1,0:T(8,128)(2,1)S(1)}, u32[]{:S(2)}, u32[]{:S(2)}) async-start(bf16[4,128,512]{2,1,0:T(8,128)(2,1)} %get-tuple-element.74), calls=%async_computation.2 | async-start | bytes 1048576 | tf_op jit(solution)/shard_map/all_to_all | solution.py:360
  92.8 14.0 %collective-permute-start.7 = (bf16[4,256,128]{2,1,0:T(8,128)(2,1)S(1)}, bf16[4,256,128]{2,1,0:T(8,128)(2,1)S(1)}, u32[]{:S(2)}, u32[]{:S(2)}) collective-permute-start(bf16[4,256,128]{2,1,0:T(8,128)(2,1)S(1)} %slice.7), channel_id=1, source_target_pairs={{0,24},{8,16},{16,8},{24,0},{1,25},{9,17},{17,9},{25,1},{2,26},{10... | collective-permute-start | bytes 786440 | tf_op jit(solution)/shard_map/ppermute | solution.py:365
  97.5 9.4 %collective-permute-start.6 = (bf16[4,256,128]{2,1,0:T(8,128)(2,1)S(1)}, bf16[4,256,128]{2,1,0:T(8,128)(2,1)S(1)}, u32[]{:S(2)}, u32[]{:S(2)}) collective-permute-start(bf16[4,256,128]{2,1,0:T(8,128)(2,1)S(1)} %slice.6), channel_id=1, source_target_pairs={{0,8},{8,0},{16,24},{24,16},{1,9},{9,1},{17,25},{25,17},{2,10},{10... | collective-permute-start | bytes 786440 | tf_op jit(solution)/shard_map/ppermute | solution.py:365
  106.8 18.6 %copy-start.7 = (bf16[4,256,128]{2,1,0:T(8,128)(2,1)}, bf16[4,256,128]{2,1,0:T(8,128)(2,1)S(1)}, u32[]{:S(2)}) copy-start(bf16[4,256,128]{2,1,0:T(8,128)(2,1)S(1)} %collective-permute-done.7.refs_4_) | copy-start | bytes 786436
  106.9 18.6 %copy-start.8 = (bf16[4,256,128]{2,1,0:T(8,128)(2,1)}, bf16[4,256,128]{2,1,0:T(8,128)(2,1)S(1)}, u32[]{:S(2)}) copy-start(bf16[4,256,128]{2,1,0:T(8,128)(2,1)S(1)} %collective-permute-done.6.refs_3_) | copy-start | bytes 786436
  125.5 12.3 %copy-start.16 = (bf16[128,512]{1,0:T(8,128)(2,1)S(1)}, bf16[128,512]{1,0:T(8,128)(2,1)}, u32[]{:S(2)}) copy-start(bf16[128,512]{1,0:T(8,128)(2,1)} %get-tuple-element.88) | copy-start | bytes 393220
  125.5 16.3 %copy-start.15 = (bf16[128,512]{1,0:T(8,128)(2,1)S(1)}, bf16[128,512]{1,0:T(8,128)(2,1)}, u32[]{:S(2)}) copy-start(bf16[128,512]{1,0:T(8,128)(2,1)} %get-tuple-element.89) | copy-start | bytes 393220
  128.6 36.2 %all-to-all-start.4 = ((bf16[16,64,128]{2,1,0:T(8,128)(2,1)}), bf16[16,64,128]{2,1,0:T(8,128)(2,1)S(1)}, u32[]{:S(2)}, u32[]{:S(2)}) async-start(bf16[16,64,128]{2,1,0:T(8,128)(2,1)} %shard_map.188), calls=%async_computation.4 | async-start | bytes 524288 | tf_op jit(solution)/shard_map/all_to_all | solution.py:360
  134.5 18.3 %collective-permute-start.8 = (bf16[128,512]{1,0:T(8,128)(2,1)S(1)}, bf16[128,512]{1,0:T(8,128)(2,1)S(1)}, u32[]{:S(2)}, u32[]{:S(2)}) collective-permute-start(bf16[128,512]{1,0:T(8,128)(2,1)S(1)} %copy-done.17), channel_id=1, source_target_pairs={{0,32},{32,0},{64,96},{96,64},{128,160},{160,128},{192,224},{224,1... | collective-permute-start | bytes 393224 | tf_op jit(solution)/shard_map/ppermute | solution.py:365
  137.8 15.0 %collective-permute-start.9 = (bf16[128,512]{1,0:T(8,128)(2,1)S(1)}, bf16[128,512]{1,0:T(8,128)(2,1)S(1)}, u32[]{:S(2)}, u32[]{:S(2)}) collective-permute-start(bf16[128,512]{1,0:T(8,128)(2,1)S(1)} %copy-done.16), channel_id=1, source_target_pairs={{0,64},{32,96},{64,0},{96,32},{128,192},{160,224},{192,128},{224,1... | collective-permute-start | bytes 393224 | tf_op jit(solution)/shard_map/ppermute | solution.py:365
  141.8 16.1 %collective-permute-start.10 = (bf16[128,512]{1,0:T(8,128)(2,1)S(1)}, bf16[128,512]{1,0:T(8,128)(2,1)S(1)}, u32[]{:S(2)}, u32[]{:S(2)}) collective-permute-start(bf16[128,512]{1,0:T(8,128)(2,1)S(1)} %copy-done.15), channel_id=1, source_target_pairs={{0,96},{32,64},{64,32},{96,0},{128,224},{160,192},{192,160},{224,1... | collective-permute-start | bytes 393224 | tf_op jit(solution)/shard_map/ppermute | solution.py:365
  (9 other events, 24.1 us)

commit v4 on v2

--- a/solution.py
+++ b/solution.py
@@ -97,7 +97,7 @@
         st[piece, 2 * N :, spot] = log_rows(spread(last, j, first))
 
 
-def group_kernel(me, got, out):
+def group_kernel(me, got, up, down):
     here = me[0] // GROUP
     count = got.shape[0]
     for at in range(0, got.shape[2], PAIR):
@@ -110,24 +110,36 @@
         for k in reversed(range(count)):
             back = decay[k] * back + got[k, N : 2 * N, lanes].astype(f32)
         rows = log_rows(sum(logs[1:], logs[0]))
-        for k in range(out.shape[0]):
-            out[k, :N, lanes] = jnp.where(k > here, ahead, back).astype(bf16)
-            out[k, N:, lanes] = rows
-
-
-def scan_kernel(me, got, groups, out):
+        up[:N, lanes] = jnp.where(here < 3, ahead, back).astype(bf16)
+        up[N:, lanes] = rows
+        down[:N, lanes] = jnp.where(here > 0, back, ahead).astype(bf16)
+        down[N:, lanes] = rows
+
+
+def scan_kernel(me, got, up, down, up_two, down_two, out):
     here = me[0] // GROUP
     count = got.shape[0]
+
+    def pick(options, lanes):
+        parts = [(k, ref[:N, lanes].astype(f32), row_logs(ref[N:, lanes])) for k, ref in options]
+        _, part, log = parts[0]
+        for k, other, other_log in parts[1:]:
+            part = jnp.where(here == k, other, part)
+            log = jnp.where(here == k, other_log, log)
+        return part, jnp.exp(log)
+
+    before = (((1, up), (2, up_two), (3, down)), ((2, up), (3, up_two)), ((3, up),))
+    after = (((2, down), (1, down_two), (0, up)), ((1, down), (0, down_two)), ((0, down),))
     for at in range(0, got.shape[2], PAIR):
         lanes = slice(at, at + PAIR)
         decay = [jnp.exp(row_logs(got[k, 2 * N :, lanes])) for k in range(count)]
         state = back = jnp.zeros((N, PAIR), f32)
-        for k in range(groups.shape[0]):
-            new = jnp.exp(row_logs(groups[k, N:, lanes])) * state + groups[k, :N, lanes].astype(f32)
-            state = jnp.where(k < here, new, state)
-        for k in reversed(range(groups.shape[0])):
-            new = jnp.exp(row_logs(groups[k, N:, lanes])) * back + groups[k, :N, lanes].astype(f32)
-            back = jnp.where(k > here, new, back)
+        for k, options in enumerate(before):
+            part, fade = pick(options, lanes)
+            state = jnp.where(k < here, fade * state + part, state)
+        for k, options in enumerate(after):
+            part, fade = pick(options, lanes)
+            back = jnp.where(3 - k > here, fade * back + part, back)
         for k in range(count):
             out[k, :N, lanes] = state.astype(bf16)
             state = decay[k] * state + got[k, :N, lanes].astype(f32)
@@ -136,8 +148,7 @@
             back = decay[k] * back + got[k, N : 2 * N, lanes].astype(f32)
 
 
-def feature_kernel(rows, me, layer, *refs):
-    outs, held = refs[:-1], refs[-1]
+def feature_kernel(rows, me, layer, keep, send, held):
     streams = held.shape[0]
     for at in range(0, layer.shape[1], PAIR):
         turned = layer[:, at : at + PAIR].astype(f32).T.astype(bf16)
@@ -145,24 +156,35 @@
             index = (at + part) // rows
             stream, spot = index % streams, index // streams * rows
             held[stream, spot : spot + rows, :] = turned[part : part + rows, :]
+    for k in range(keep.shape[0]):
+        keep[k] = held[me[1] ^ (2 * k)]
+        send[k] = held[me[1] ^ (2 * k + 1)]
+
+
+def pair_kernel(keep, got, *outs):
     for k, out in enumerate(outs):
-        out[...] = held[me[1] ^ k]
+        out[0] = keep[k]
+        out[1] = got[k]
 
 
 def stack_kernel(*refs):
     for k, part in enumerate(refs[:-1]):
-        refs[-1][k] = part[...]
-
-
-def weight_kernel(me, all_c, *refs):
+        refs[-1][2 * k] = part[0]
+        refs[-1][2 * k + 1] = part[1]
+
+
+def weight_kernel(plan, me, all_c, *refs):
     features, out = refs[:-1], refs[-1]
     rows = out.shape[1]
-    for k, block in enumerate(features):
-        total = dot(block[0], all_c[me[1]])
-        for j in range(1, block.shape[0]):
-            total = total + dot(block[j], all_c[me[1] ^ j])
-        for q in range(block.shape[1] // rows):
-            out[(me[2] ^ k) * (block.shape[1] // rows) + q] = total[q * rows : (q + 1) * rows].astype(bf16)
+    for k, blocks in plan:
+        total = None
+        for index, begin in blocks:
+            for j in range(features[index].shape[0]):
+                term = dot(features[index][j], all_c[me[1] ^ (begin + j)])
+                total = term if total is None else total + term
+        count = total.shape[0] // rows
+        for q in range(count):
+            out[(me[2] ^ k) * count + q] = total[q * rows : (q + 1) * rows].astype(bf16)
 
 
 def intra_kernel(cum, x, dy, b, c, skip, dxp, xt, dye, dc, db, dcum, rows):
@@ -210,11 +232,11 @@
     db[...] = dot(high, c[...])
 
 
-def grad_c_kernel(dc, dye, starts, grad_c, copies):
+def grad_c_kernel(dc, dye, states, grad_c, copies):
     total = dc[...]
-    pieces, width = starts.shape[0], starts.shape[2]
+    pieces, width = states.shape[0], states.shape[2]
     for j in range(pieces):
-        total = total + dot_nt(dye[:, j * width : (j + 1) * width], starts[j, :N, :])
+        total = total + dot_nt(dye[:, j * width : (j + 1) * width], states[j, :N, :])
     out = total.astype(bf16)
     grad_c[...] = out
     for k in range(copies.shape[0]):
@@ -329,6 +351,11 @@
     return out[0] if len(out_shapes) == 1 else out
 
 
+def shift(a, senders, step):
+    count = lax.axis_size("seq")
+    return lax.ppermute(a, "seq", [(i, (i + step) % count) for i in senders])
+
+
 def shaped(shape, dtype):
     return jax.ShapeDtypeStruct(shape, dtype)
 
@@ -363,7 +390,6 @@
     width = heads * P_SIZE
     piece = width // GROUP
     near = [[i + k for k in range(GROUP)] for i in range(0, seqs, GROUP)]
-    far = [list(range(i, seqs, GROUP)) for i in range(GROUP)]
     tile = shaped((SPAN, 128), f32)
     small_tile = shaped((8, 128), f32)
     wide = shaped((SPAN, width), bf16)
@@ -385,19 +411,20 @@
 
     rows = weight_c.shape[0]
     block = layer.shape[1] // streams
-    pieces = call(
+    half = max(streams // 2, 1)
+    keep, send = call(
         functools.partial(feature_kernel, rows),
-        [shaped((block, SPAN), bf16)] * streams,
+        [shaped((half, block, SPAN), bf16)] * 2,
         me,
         layer,
         scratch=[pltpu.VMEM((streams, block, SPAN), bf16)],
-        flops=0,
-    )
-    pieces = [pieces] if streams == 1 else pieces
-    arrived = [trade(pieces[k], "dp", k) for k in range(1, streams)]
-    got, *arrived = lax.optimization_barrier((got, *arrived))
-    mine = call(stack_kernel, [shaped((streams, block, SPAN), bf16)], pieces[0], *arrived)
-    features = [trade(mine, "tensor", k) for k in range(1, tensors)]
+    )
+    pairs = call(
+        pair_kernel, [shaped((2, block, SPAN), bf16)] * half, keep, trade(send, "dp", 1)
+    )
+    pairs = [pairs] if half == 1 else pairs
+    pairs = [pairs[0]] + [trade(pairs[k], "dp", 2 * k) for k in range(1, half)]
+    got, *pairs = lax.optimization_barrier((got, *pairs))
 
     dxp, xt, dye, dc, db, dcum = call(
         intra_kernel,
@@ -411,24 +438,34 @@
         scratch=[pltpu.VMEM((SPAN, SPAN), f32)],
         flops=20 * SPAN * SPAN * width,
     )
-    ahead = call(
+    up, down = call(
         group_kernel,
-        [shaped((seqs // GROUP, N + LOG_ROWS, piece), bf16)],
+        [shaped((N + LOG_ROWS, piece), bf16)] * 2,
         me,
         got,
         flops=8 * N * width,
     )
-    groups = swap(ahead, "seq", far)
-    groups, *features = lax.optimization_barrier((groups, *features))
-    features = [mine, *features]
+    up, down = shift(up, range(seqs), GROUP), shift(down, range(seqs), -GROUP)
+    inner = range(GROUP, seqs - GROUP)
+    up_two, down_two = shift(up, inner, GROUP), shift(down, inner, -GROUP)
+    up_two, down_two, dye = lax.optimization_barrier((up_two, down_two, dye))
+    plan = ((0, ((0, 0),)), (1, ((1, 0),)), (3, ((2, 0),)), (2, ((3, 0), (4, half))))
     states = call(
         scan_kernel,
         [shaped((GROUP, 2 * N, piece), bf16)],
         me,
         got,
-        groups,
+        up,
+        down,
+        up_two,
+        down_two,
         flops=8 * N * width,
     )
+    states, *pairs = lax.optimization_barrier((states, *pairs))
+    mine = call(stack_kernel, [shaped((streams, block, SPAN), bf16)], *pairs)
+    left, right = trade(mine, "tensor", 1), trade(mine, "tensor", 3)
+    far_a = trade(right[:half], "tensor", 1)
+    far_b = trade(left[half:], "tensor", 3)
     states = swap(states, "seq", near)
     grad_c, copies = call(
         grad_c_kernel,
@@ -440,11 +477,15 @@
     )
     all_c = swap(copies, "dp")
     partial = call(
-        weight_kernel,
+        functools.partial(weight_kernel, plan),
         [shaped((seqs, rows, N), bf16)],
         me,
         all_c,
-        *features,
+        mine,
+        left,
+        right,
+        far_a,
+        far_b,
         flops=2 * tensors * layer.shape[1] * SPAN * N,
     )
     parts = swap(partial, "seq")

time: 197 us -> 193 us (0.980)
  blocking collectives: 45.4 us -> 36 us
  local copies, waits for them, and re-layouts: 6.51 us -> 13 us
  waiting for transfers between devices: 51.3 us -> 49 us
    ppermute x0 -> x4, waiting for transfers between devices: none -> 17.7 us  [shift(): return lax.ppermute(a, 'seq', [(i, (i + step) % count) for i in senders])]
    ppermute x0 -> x4, starting transfers between devices: none -> 14.6 us  [shift(): return lax.ppermute(a, 'seq', [(i, (i + step) % count) for i in senders])]
    ppermute x10 -> x8, waiting for transfers between devices: 25.1 us -> 13.4 us  [trade(): return lax.ppermute(a, axis, [(i, i ^ k) for i in range(count)])]
    all_to_all x3 -> x2, blocking collectives: 45.4 us -> 36 us  [swap(): return lax.all_to_all(a, axis, 0, 0, tiled=True, axis_index_groups=groups)]
    all_to_all x4, waiting for transfers between devices: 26.2 us -> 17.9 us  [swap(): return lax.all_to_all(a, axis, 0, 0, tiled=True, axis_index_groups=groups)]
    all_to_all x4, starting transfers between devices: 34.9 us -> 28.1 us  [swap(): return lax.all_to_all(a, axis, 0, 0, tiled=True, axis_index_groups=groups)]
    ppermute x10 -> x8, starting transfers between devices: 34.8 us -> 28.2 us  [trade(): return lax.ppermute(a, axis, [(i, i ^ k) for i in range(count)])]
    unnamed x44 -> x52, local copies, waits for them, and re-layouts: 6.51 us -> 11.5 us
  transfers between devices with their start and end apart: 14 -> 16, of which waited for: 7 -> 12; matrix products, arithmetic and copies ran while one was open for 0% -> 1% of each run, Pallas kernels for 5% -> 6%
where the time goes in v4:
time: 193 us; the launch traced here: 192 us
  starting transfers between devices  70.9 us (37%)
  waiting for transfers between devices  49 us (25%)
  blocking collectives  36 us (19%)
  Pallas kernels  21.7 us (11%)
  local copies, waits for them, and re-layouts  13 us (7%)
    all_to_all x2, blocking collectives, swap(): return lax.all_to_all(a, axis, 0, 0, tiled=True, axis_index_groups=groups)  36 us
    ppermute x8, starting transfers between devices, trade(): return lax.ppermute(a, axis, [(i, i ^ k) for i in range(count)])  28.2 us
    all_to_all x4, starting transfers between devices, swap(): return lax.all_to_all(a, axis, 0, 0, tiled=True, axis_index_groups=groups)  28.1 us
    pallas_call x13, Pallas kernels, call(): pl.pallas_call(kernel, out_shape=tuple(out_shapes), in_specs=[scalars if...  21.7 us
    all_to_all x4, waiting for transfers between devices, swap(): return lax.all_to_all(a, axis, 0, 0, tiled=True, axis_index_groups=groups)  17.9 us
    ppermute x4, waiting for transfers between devices, shift(): return lax.ppermute(a, 'seq', [(i, (i + step) % count) for i in senders])  17.7 us
    ppermute x4, starting transfers between devices, shift(): return lax.ppermute(a, 'seq', [(i, (i + step) % count) for i in senders])  14.6 us
    ppermute x8, waiting for transfers between devices, trade(): return lax.ppermute(a, axis, [(i, i ^ k) for i in range(count)])  13.4 us
  transfers between devices with their start and end apart: 16, of which 12 were waited for; matrix products, arithmetic and copies ran while one was open for 1% of the time, Pallas kernels for 6%

profile of v4, /device:TPU:1, one launch (start us, length us, event | category | flops | bytes accessed | tf_op | source)
XLA Modules:
  0.0 191.6 jit_solution(18218403832446725824)
XLA Ops:
  0.6 4.2 %shard_map.179 = (bf16[4,272,512]{2,1,0:T(8,128)(2,1)}, f32[128,128]{1,0:T(8,128)}, f32[128,128]{1,0:T(8,128)}, f32[8,128]{1,0:T(8,128)}) custom-call(f32[32,128]{1,0:T(8,128)} %bitcast.33, s32[1,32]{1,0:T(1,128)} %bitcast.35, f32[8,32]{1,0:T(8,128)} %bitcast.34, bf16[128,2048]{1,0:T(8,128)(2,1)} %bitcast.19, bf16[128,2048]{1,0:T(8,128)(2,1)} %bitcast.22, ...), custom_call_target="tpu_custom_call" | custom-call | flops 134217728 | bytes 2380928 | tf_op jit(solution)/shard_map/pallas_call | solution.py:343
  4.9 6.6 %all-to-all-start = ((bf16[4,272,512]{2,1,0:T(8,128)(2,1)}), bf16[4,272,512]{2,1,0:T(8,128)(2,1)S(1)}, u32[]{:S(2)}, u32[]{:S(2)}) async-start(bf16[4,272,512]{2,1,0:T(8,128)(2,1)} %get-tuple-element.54), calls=%async_computation | async-start | bytes 2228224 | tf_op jit(solution)/shard_map/all_to_all | solution.py:364
  12.3 5.9 %collective-permute-start = (bf16[4,256,128]{2,1,0:T(8,128)(2,1)S(1)}, bf16[4,256,128]{2,1,0:T(8,128)(2,1)S(1)}, u32[]{:S(2)}, u32[]{:S(2)}) collective-permute-start(bf16[4,256,128]{2,1,0:T(8,128)(2,1)S(1)} %get-tuple-element.57), channel_id=1, source_target_pairs={{0,1},{1,0},{2,3},{3,2},{4,5},{5,4},{6,7},{7,6},{8,9},{9,8},{10,11... | collective-permute-start | bytes 786440 | tf_op jit(solution)/shard_map/ppermute | solution.py:369
  21.4 2.5 %collective-permute-start.2 = (bf16[2,256,128]{2,1,0:T(8,128)(2,1)S(1)}, bf16[2,256,128]{2,1,0:T(8,128)(2,1)S(1)}, u32[]{:S(2)}, u32[]{:S(2)}) collective-permute-start(bf16[2,256,128]{2,1,0:T(8,128)(2,1)S(1)} %get-tuple-element.60), channel_id=1, source_target_pairs={{0,4},{1,5},{2,6},{3,7},{4,0},{5,1},{6,2},{7,3},{8,12},{9,13},{10,... | collective-permute-start | bytes 393224 | tf_op jit(solution)/shard_map/ppermute | solution.py:369
  23.9 5.1 %collective-permute-start.3 = (bf16[2,256,128]{2,1,0:T(8,128)(2,1)S(1)}, bf16[2,256,128]{2,1,0:T(8,128)(2,1)S(1)}, u32[]{:S(2)}, u32[]{:S(2)}) collective-permute-start(bf16[2,256,128]{2,1,0:T(8,128)(2,1)S(1)} %get-tuple-element.61), channel_id=1, source_target_pairs={{0,6},{1,7},{2,4},{3,5},{4,2},{5,3},{6,0},{7,1},{8,14},{9,15},{10,... | collective-permute-start | bytes 393224 | tf_op jit(solution)/shard_map/ppermute | solution.py:369
  29.5 2.5 %collective-permute-done.3.refs_3_ = bf16[2,256,128]{2,1,0:T(8,128)(2,1)S(1)} collective-permute-done((bf16[2,256,128]{2,1,0:T(8,128)(2,1)S(1)}, bf16[2,256,128]{2,1,0:T(8,128)(2,1)S(1)}, u32[]{:S(2)}, u32[]{:S(2)}) %collective-permute-start.3) | collective-permute-done | bytes 131104 | tf_op jit(solution)/shard_map/ppermute | solution.py:369
  32.0 5.7 %all-to-all-done.got = bf16[4,272,512]{2,1,0:T(8,128)(2,1)S(1)} async-done(((bf16[4,272,512]{2,1,0:T(8,128)(2,1)}), bf16[4,272,512]{2,1,0:T(8,128)(2,1)S(1)}, u32[]{:S(2)}, u32[]{:S(2)}) %all-to-all-start) | async-done | bytes 1114144 | tf_op jit(solution)/shard_map/all_to_all | solution.py:364
  38.5 9.2 %collective-permute-start.4 = (bf16[144,512]{1,0:T(8,128)(2,1)S(1)}, bf16[144,512]{1,0:T(8,128)(2,1)S(1)}, u32[]{:S(2)}, u32[]{:S(2)}) collective-permute-start(bf16[144,512]{1,0:T(8,128)(2,1)S(1)} %get-tuple-element.63), channel_id=1, source_target_pairs={{0,128},{32,160},{64,192},{96,224},{128,256},{160,288},{192,320},{... | collective-permute-start | bytes 442376 | tf_op jit(solution)/shard_map/ppermute | solution.py:356
  47.7 3.5 %collective-permute-start.5 = (bf16[144,512]{1,0:T(8,128)(2,1)S(1)}, bf16[144,512]{1,0:T(8,128)(2,1)S(1)}, u32[]{:S(2)}, u32[]{:S(2)}) collective-permute-start(bf16[144,512]{1,0:T(8,128)(2,1)S(1)} %get-tuple-element.64), channel_id=1, source_target_pairs={{0,384},{32,416},{64,448},{96,480},{128,0},{160,32},{192,64},{224,... | collective-permute-start | bytes 442376 | tf_op jit(solution)/shard_map/ppermute | solution.py:356
  52.9 12.6 %collective-permute-done.5.down = bf16[144,512]{1,0:T(8,128)(2,1)S(1)} collective-permute-done((bf16[144,512]{1,0:T(8,128)(2,1)S(1)}, bf16[144,512]{1,0:T(8,128)(2,1)S(1)}, u32[]{:S(2)}, u32[]{:S(2)}) %collective-permute-start.5) | collective-permute-done | bytes 147488 | tf_op jit(solution)/shard_map/ppermute | solution.py:356
  66.8 4.9 %shard_map.183 = (f32[128,2048]{1,0:T(8,128)S(1)}, bf16[128,2048]{1,0:T(8,128)(2,1)S(1)}, bf16[128,2048]{1,0:T(8,128)(2,1)S(1)}, f32[128,128]{1,0:T(8,128)S(1)},...) custom-call(f32[128,128]{1,0:T(8,128)S(1)} %copy-done.15, bf16[128,2048]{1,0:T(8,128)(2,1)S(1)} %bitcast.20, ...), custom_call_target="tpu_custom_call" | custom-call | flops 671088640 | bytes 3473536 | tf_op jit(solution)/shard_map/pallas_call | solution.py:343
  75.5 4.1 %collective-permute-done.7.down_two = bf16[144,512]{1,0:T(8,128)(2,1)S(1)} collective-permute-done((bf16[144,512]{1,0:T(8,128)(2,1)S(1)}, bf16[144,512]{1,0:T(8,128)(2,1)S(1)}, u32[]{:S(2)}, u32[]{:S(2)}) %collective-permute-start.7) | collective-permute-done | bytes 147488 | tf_op jit(solution)/shard_map/ppermute | solution.py:356
  81.7 5.7 %all-to-all-start.1 = ((bf16[4,256,512]{2,1,0:T(8,128)(2,1)}), bf16[4,256,512]{2,1,0:T(8,128)(2,1)S(1)}, u32[]{:S(2)}, u32[]{:S(2)}) async-start(bf16[4,256,512]{2,1,0:T(8,128)(2,1)} %shard_map.184), calls=%async_computation.1 | async-start | bytes 2097152 | tf_op jit(solution)/shard_map/all_to_all | solution.py:364
  87.4 4.7 %collective-permute-start.9 = (bf16[8,256,128]{2,1,0:T(8,128)(2,1)S(1)}, bf16[8,256,128]{2,1,0:T(8,128)(2,1)S(1)}, u32[]{:S(2)}, u32[]{:S(2)}) collective-permute-start(bf16[8,256,128]{2,1,0:T(8,128)(2,1)S(1)} %shard_map.187.refs_0_), channel_id=1, source_target_pairs={{0,24},{8,16},{16,8},{24,0},{1,25},{9,17},{17,9},{25,1},{2,26},{10... | collective-permute-start | bytes 1572872 | tf_op jit(solution)/shard_map/ppermute | solution.py:369
  94.1 9.0 %collective-permute-done.9.refs_2_ = bf16[8,256,128]{2,1,0:T(8,128)(2,1)S(1)} collective-permute-done((bf16[8,256,128]{2,1,0:T(8,128)(2,1)S(1)}, bf16[8,256,128]{2,1,0:T(8,128)(2,1)S(1)}, u32[]{:S(2)}, u32[]{:S(2)}) %collective-permute-start.9) | collective-permute-done | bytes 524320 | tf_op jit(solution)/shard_map/ppermute | solution.py:369
  107.0 4.1 %collective-permute-start.11 = (bf16[4,256,128]{2,1,0:T(8,128)(2,1)}, bf16[4,256,128]{2,1,0:T(8,128)(2,1)}, u32[]{:S(2)}, u32[]{:S(2)}) collective-permute-start(bf16[4,256,128]{2,1,0:T(8,128)(2,1)} %slice.9), channel_id=1, source_target_pairs={{0,24},{8,16},{16,8},{24,0},{1,25},{9,17},{17,9},{25,1},{2,26},{10... | collective-permute-start | bytes 786440 | tf_op jit(solution)/shard_map/ppermute | solution.py:369
  115.3 6.2 %all-to-all-start.2 = ((bf16[8,128,128]{2,1,0:T(8,128)(2,1)}), bf16[8,128,128]{2,1,0:T(8,128)(2,1)S(1)}, u32[]{:S(2)}, u32[]{:S(2)}) async-start(bf16[8,128,128]{2,1,0:T(8,128)(2,1)} %copy-done.11), calls=%async_computation.2 | async-start | bytes 524288 | tf_op jit(solution)/shard_map/all_to_all | solution.py:364
  121.5 6.5 %all-to-all-done.2.all_c = bf16[8,128,128]{2,1,0:T(8,128)(2,1)S(1)} async-done(((bf16[8,128,128]{2,1,0:T(8,128)(2,1)}), bf16[8,128,128]{2,1,0:T(8,128)(2,1)S(1)}, u32[]{:S(2)}, u32[]{:S(2)}) %all-to-all-start.2) | async-done | bytes 262176 | tf_op jit(solution)/shard_map/all_to_all | solution.py:364
  129.1 2.4 %shard_map.188 = bf16[16,64,128]{2,1,0:T(8,128)(2,1)} custom-call(s32[3]{0:T(128)S(1)} %pad_add_fusion.me, bf16[8,128,128]{2,1,0:T(8,128)(2,1)S(1)} %all-to-all-done.2.all_c, bf16[8,256,128]{2,1,0:T(8,128)(2,1)S(1)} %shard_map.187.refs_0_, bf16[8,256,128]{2,1,0:T(8,128)(2,1)S(1)} %copy-done.3, bf16[8,256,128]{2,1,0:T(8,128)(2,1)S(1)} %collective-permute-done.9.refs_2_, ...), custom_call_target="tpu_custom_call" | custom-call | flops 268435456 | bytes 2621452 | tf_op jit(solution)/shard_map/pallas_call | solution.py:343
  131.5 9.6 %all-to-all-start.3 = ((bf16[16,64,128]{2,1,0:T(8,128)(2,1)}), bf16[16,64,128]{2,1,0:T(8,128)(2,1)S(1)}, u32[]{:S(2)}, u32[]{:S(2)}) async-start(bf16[16,64,128]{2,1,0:T(8,128)(2,1)} %shard_map.188), calls=%async_computation.3 | async-start | bytes 524288 | tf_op jit(solution)/shard_map/all_to_all | solution.py:364
  145.9 3.9 %shard_map.185 = (bf16[128,2048]{1,0:T(8,128)(2,1)}, bf16[128,128]{1,0:T(8,128)(2,1)}, f32[8,128]{1,0:T(8,128)S(1)}) custom-call(bf16[4,256,512]{2,1,0:T(8,128)(2,1)S(1)} %all-to-all-done.1.states, bf16[128,2048]{1,0:T(8,128)(2,1)S(1)} %bitcast.21, bf16[128,2048]{1,0:T(8,128)(2,1)S(1)} %bitcast.24, bf16[128,2048]{1,0:T(8,128)(2,1)S(1)} %copy-done.7, ...), custom_call_target="tpu_custom_call" | custom-call | flops 201326592 | bytes 4562944 | tf_op jit(solution)/shard_map/pallas_call | solution.py:343
  149.8 4.2 %all-to-all-done.3.parts = bf16[16,64,128]{2,1,0:T(8,128)(2,1)S(1)} async-done(((bf16[16,64,128]{2,1,0:T(8,128)(2,1)}), bf16[16,64,128]{2,1,0:T(8,128)(2,1)S(1)}, u32[]{:S(2)}, u32[]{:S(2)}) %all-to-all-start.3) | async-done | bytes 262176 | tf_op jit(solution)/shard_map/all_to_all | solution.py:364
  154.2 22.5 %all_to_all.30.got = f32[16,8,128]{2,1,0:T(8,128)S(1)} all-to-all(f32[16,8,128]{2,1,0:T(8,128)S(1)} %get-tuple-element.91), channel_id=1, replica_groups=mesh['seq'=16,'tensor'=4,'dp'=8] {'seq'}, dimensions={0} | all-to-all | bytes 131072 | tf_op jit(solution)/shard_map/all_to_all | solution.py:364
  176.7 13.5 %all_to_all.31.got = f32[32,8,128]{2,1,0:T(8,128)S(1)} all-to-all(f32[32,8,128]{2,1,0:T(8,128)S(1)} %shard_map.190), channel_id=1, replica_groups=mesh['seq'=16,'tensor'=4,'dp'=8] {'tensor','dp'}, dimensions={0} | all-to-all | bytes 262144 | tf_op jit(solution)/shard_map/all_to_all | solution.py:364
  (78 shorter events, 31.5 us)
Async XLA Ops:
  4.9 32.8 %all-to-all-start = ((bf16[4,272,512]{2,1,0:T(8,128)(2,1)}), bf16[4,272,512]{2,1,0:T(8,128)(2,1)S(1)}, u32[]{:S(2)}, u32[]{:S(2)}) async-start(bf16[4,272,512]{2,1,0:T(8,128)(2,1)} %get-tuple-element.54), calls=%async_computation | async-start | bytes 2228224 | tf_op jit(solution)/shard_map/all_to_all | solution.py:364
  11.4 55.3 %copy-start = (bf16[1,128,2048]{2,1,0:T(8,128)(2,1)S(1)}, bf16[1,128,2048]{2,1,0:T(8,128)(2,1)}, u32[]{:S(2)}) copy-start(bf16[1,128,2048]{2,1,0:T(8,128)(2,1)} %param.12) | copy-start | bytes 1572868
  11.4 55.3 %copy-start.1 = (bf16[1,128,2048]{2,1,0:T(8,128)(2,1)S(1)}, bf16[1,128,2048]{2,1,0:T(8,128)(2,1)}, u32[]{:S(2)}) copy-start(bf16[1,128,2048]{2,1,0:T(8,128)(2,1)} %param.19) | copy-start | bytes 1572868
  11.4 55.3 %copy-start.12 = (bf16[1,128,128]{2,1,0:T(8,128)(2,1)S(1)}, bf16[1,128,128]{2,1,0:T(8,128)(2,1)}, u32[]{:S(2)}) copy-start(bf16[1,128,128]{2,1,0:T(8,128)(2,1)} %param.13) | copy-start | bytes 98308
  11.4 55.3 %copy-start.13 = (bf16[1,128,128]{2,1,0:T(8,128)(2,1)S(1)}, bf16[1,128,128]{2,1,0:T(8,128)(2,1)}, u32[]{:S(2)}) copy-start(bf16[1,128,128]{2,1,0:T(8,128)(2,1)} %param.14) | copy-start | bytes 98308
  11.5 55.3 %copy-start.15 = (f32[128,128]{1,0:T(8,128)S(1)}, f32[128,128]{1,0:T(8,128)}, u32[]{:S(2)}) copy-start(f32[128,128]{1,0:T(8,128)} %get-tuple-element.65.cum) | copy-start | bytes 196612
  11.5 55.3 %copy-start.25 = (f32[32]{0:T(128)S(1)}, f32[32]{0:T(128)}, u32[]{:S(2)}) copy-start(f32[32]{0:T(128)} %param.18) | copy-start | bytes 388
  12.3 7.0 %collective-permute-start = (bf16[4,256,128]{2,1,0:T(8,128)(2,1)S(1)}, bf16[4,256,128]{2,1,0:T(8,128)(2,1)S(1)}, u32[]{:S(2)}, u32[]{:S(2)}) collective-permute-start(bf16[4,256,128]{2,1,0:T(8,128)(2,1)S(1)} %get-tuple-element.57), channel_id=1, source_target_pairs={{0,1},{1,0},{2,3},{3,2},{4,5},{5,4},{6,7},{7,6},{8,9},{9,8},{10,11... | collective-permute-start | bytes 786440 | tf_op jit(solution)/shard_map/ppermute | solution.py:369
  19.4 9.6 %collective-permute-start.1 = (bf16[2,256,128]{2,1,0:T(8,128)(2,1)S(1)}, bf16[2,256,128]{2,1,0:T(8,128)(2,1)S(1)}, u32[]{:S(2)}, u32[]{:S(2)}) collective-permute-start(bf16[2,256,128]{2,1,0:T(8,128)(2,1)S(1)} %get-tuple-element.59), channel_id=1, source_target_pairs={{0,2},{1,3},{2,0},{3,1},{4,6},{5,7},{6,4},{7,5},{8,10},{9,11},{10,... | collective-permute-start | bytes 393224 | tf_op jit(solution)/shard_map/ppermute | solution.py:369
  21.4 8.1 %collective-permute-start.2 = (bf16[2,256,128]{2,1,0:T(8,128)(2,1)S(1)}, bf16[2,256,128]{2,1,0:T(8,128)(2,1)S(1)}, u32[]{:S(2)}, u32[]{:S(2)}) collective-permute-start(bf16[2,256,128]{2,1,0:T(8,128)(2,1)S(1)} %get-tuple-element.60), channel_id=1, source_target_pairs={{0,4},{1,5},{2,6},{3,7},{4,0},{5,1},{6,2},{7,3},{8,12},{9,13},{10,... | collective-permute-start | bytes 393224 | tf_op jit(solution)/shard_map/ppermute | solution.py:369
  23.9 8.1 %collective-permute-start.3 = (bf16[2,256,128]{2,1,0:T(8,128)(2,1)S(1)}, bf16[2,256,128]{2,1,0:T(8,128)(2,1)S(1)}, u32[]{:S(2)}, u32[]{:S(2)}) collective-permute-start(bf16[2,256,128]{2,1,0:T(8,128)(2,1)S(1)} %get-tuple-element.61), channel_id=1, source_target_pairs={{0,6},{1,7},{2,4},{3,5},{4,2},{5,3},{6,0},{7,1},{8,14},{9,15},{10,... | collective-permute-start | bytes 393224 | tf_op jit(solution)/shard_map/ppermute | solution.py:369
  38.5 13.8 %collective-permute-start.4 = (bf16[144,512]{1,0:T(8,128)(2,1)S(1)}, bf16[144,512]{1,0:T(8,128)(2,1)S(1)}, u32[]{:S(2)}, u32[]{:S(2)}) collective-permute-start(bf16[144,512]{1,0:T(8,128)(2,1)S(1)} %get-tuple-element.63), channel_id=1, source_target_pairs={{0,128},{32,160},{64,192},{96,224},{128,256},{160,288},{192,320},{... | collective-permute-start | bytes 442376 | tf_op jit(solution)/shard_map/ppermute | solution.py:356
  47.7 17.7 %collective-permute-start.5 = (bf16[144,512]{1,0:T(8,128)(2,1)S(1)}, bf16[144,512]{1,0:T(8,128)(2,1)S(1)}, u32[]{:S(2)}, u32[]{:S(2)}) collective-permute-start(bf16[144,512]{1,0:T(8,128)(2,1)S(1)} %get-tuple-element.64), channel_id=1, source_target_pairs={{0,384},{32,416},{64,448},{96,480},{128,0},{160,32},{192,64},{224,... | collective-permute-start | bytes 442376 | tf_op jit(solution)/shard_map/ppermute | solution.py:356
  52.2 23.3 %collective-permute-start.6 = (bf16[144,512]{1,0:T(8,128)(2,1)S(1)}, bf16[144,512]{1,0:T(8,128)(2,1)S(1)}, u32[]{:S(2)}, u32[]{:S(2)}) collective-permute-start(bf16[144,512]{1,0:T(8,128)(2,1)S(1)} %collective-permute-done.4.up), channel_id=1, source_target_pairs={{128,256},{160,288},{192,320},{224,352},{256,384},{288,416},{320,4... | collective-permute-start | bytes 442376 | tf_op jit(solution)/shard_map/ppermute | solution.py:356
  65.5 14.2 %collective-permute-start.7 = (bf16[144,512]{1,0:T(8,128)(2,1)S(1)}, bf16[144,512]{1,0:T(8,128)(2,1)S(1)}, u32[]{:S(2)}, u32[]{:S(2)}) collective-permute-start(bf16[144,512]{1,0:T(8,128)(2,1)S(1)} %collective-permute-done.5.down), channel_id=1, source_target_pairs={{128,0},{160,32},{192,64},{224,96},{256,128},{288,160},{320,192},{... | collective-permute-start | bytes 442376 | tf_op jit(solution)/shard_map/ppermute | solution.py:356
  81.7 31.0 %all-to-all-start.1 = ((bf16[4,256,512]{2,1,0:T(8,128)(2,1)}), bf16[4,256,512]{2,1,0:T(8,128)(2,1)S(1)}, u32[]{:S(2)}, u32[]{:S(2)}) async-start(bf16[4,256,512]{2,1,0:T(8,128)(2,1)} %shard_map.184), calls=%async_computation.1 | async-start | bytes 2097152 | tf_op jit(solution)/shard_map/all_to_all | solution.py:364
  87.4 15.7 %collective-permute-start.9 = (bf16[8,256,128]{2,1,0:T(8,128)(2,1)S(1)}, bf16[8,256,128]{2,1,0:T(8,128)(2,1)S(1)}, u32[]{:S(2)}, u32[]{:S(2)}) collective-permute-start(bf16[8,256,128]{2,1,0:T(8,128)(2,1)S(1)} %shard_map.187.refs_0_), channel_id=1, source_target_pairs={{0,24},{8,16},{16,8},{24,0},{1,25},{9,17},{17,9},{25,1},{2,26},{10... | collective-permute-start | bytes 1572872 | tf_op jit(solution)/shard_map/ppermute | solution.py:369
  92.2 14.0 %collective-permute-start.8 = (bf16[8,256,128]{2,1,0:T(8,128)(2,1)S(1)}, bf16[8,256,128]{2,1,0:T(8,128)(2,1)S(1)}, u32[]{:S(2)}, u32[]{:S(2)}) collective-permute-start(bf16[8,256,128]{2,1,0:T(8,128)(2,1)S(1)} %shard_map.187.refs_0_), channel_id=1, source_target_pairs={{0,8},{8,0},{16,24},{24,16},{1,9},{9,1},{17,25},{25,17},{2,10},{10... | collective-permute-start | bytes 1572872 | tf_op jit(solution)/shard_map/ppermute | solution.py:369
  103.8 17.7 %collective-permute-start.10 = (bf16[4,256,128]{2,1,0:T(8,128)(2,1)}, bf16[4,256,128]{2,1,0:T(8,128)(2,1)}, u32[]{:S(2)}, u32[]{:S(2)}) collective-permute-start(bf16[4,256,128]{2,1,0:T(8,128)(2,1)} %slice.8), channel_id=1, source_target_pairs={{0,8},{8,0},{16,24},{24,16},{1,9},{9,1},{17,25},{25,17},{2,10},{10... | collective-permute-start | bytes 786440 | tf_op jit(solution)/shard_map/ppermute | solution.py:369
  107.0 14.5 %collective-permute-start.11 = (bf16[4,256,128]{2,1,0:T(8,128)(2,1)}, bf16[4,256,128]{2,1,0:T(8,128)(2,1)}, u32[]{:S(2)}, u32[]{:S(2)}) collective-permute-start(bf16[4,256,128]{2,1,0:T(8,128)(2,1)} %slice.9), channel_id=1, source_target_pairs={{0,24},{8,16},{16,8},{24,0},{1,25},{9,17},{17,9},{25,1},{2,26},{10... | collective-permute-start | bytes 786440 | tf_op jit(solution)/shard_map/ppermute | solution.py:369
  115.3 12.7 %all-to-all-start.2 = ((bf16[8,128,128]{2,1,0:T(8,128)(2,1)}), bf16[8,128,128]{2,1,0:T(8,128)(2,1)S(1)}, u32[]{:S(2)}, u32[]{:S(2)}) async-start(bf16[8,128,128]{2,1,0:T(8,128)(2,1)} %copy-done.11), calls=%async_computation.2 | async-start | bytes 524288 | tf_op jit(solution)/shard_map/all_to_all | solution.py:364
  131.5 22.5 %all-to-all-start.3 = ((bf16[16,64,128]{2,1,0:T(8,128)(2,1)}), bf16[16,64,128]{2,1,0:T(8,128)(2,1)S(1)}, u32[]{:S(2)}, u32[]{:S(2)}) async-start(bf16[16,64,128]{2,1,0:T(8,128)(2,1)} %shard_map.188), calls=%async_computation.3 | async-start | bytes 524288 | tf_op jit(solution)/shard_map/all_to_all | solution.py:364
  145.9 44.3 %copy-start.22 = (f32[64,128]{1,0:T(8,128)S(1)}, f32[64,128]{1,0:T(8,128)}, u32[]{:S(2)}) copy-start(f32[64,128]{1,0:T(8,128)} %moment_one.1) | copy-start | bytes 98308
  145.9 44.3 %copy-start.23 = (f32[64,128]{1,0:T(8,128)S(1)}, f32[64,128]{1,0:T(8,128)}, u32[]{:S(2)}) copy-start(f32[64,128]{1,0:T(8,128)} %moment_two.1) | copy-start | bytes 98308
  (18 other events, 114.9 us)

commit v5 on v4

--- a/solution.py
+++ b/solution.py
@@ -116,7 +116,8 @@
         down[N:, lanes] = rows
 
 
-def scan_kernel(me, got, up, down, up_two, down_two, out):
+def scan_kernel(me, got, up, down, up_two, down_two, ahead, *refs):
+    backs, held = refs[:-1], refs[-1]
     here = me[0] // GROUP
     count = got.shape[0]
 
@@ -141,11 +142,13 @@
             part, fade = pick(options, lanes)
             back = jnp.where(3 - k > here, fade * back + part, back)
         for k in range(count):
-            out[k, :N, lanes] = state.astype(bf16)
+            ahead[k, :, lanes] = state.astype(bf16)
             state = decay[k] * state + got[k, :N, lanes].astype(f32)
         for k in reversed(range(count)):
-            out[k, N:, lanes] = back.astype(bf16)
+            held[k, :, lanes] = back.astype(bf16)
             back = decay[k] * back + got[k, N : 2 * N, lanes].astype(f32)
+    for k, out in enumerate(backs):
+        out[...] = held[(me[0] % GROUP) ^ k]
 
 
 def feature_kernel(rows, me, layer, keep, send, held):
@@ -232,11 +235,17 @@
     db[...] = dot(high, c[...])
 
 
-def grad_c_kernel(dc, dye, states, grad_c, copies):
+def grad_c_kernel(dc, dye, starts, grad_c, copies, held, sems):
+    pieces, width = starts.shape[0], starts.shape[2]
+    moves = []
+    for j in range(pieces):
+        lanes = slice(j * width, (j + 1) * width)
+        moves.append(pltpu.make_async_copy(dye.at[:, lanes], held.at[:, lanes], sems.at[j]))
+        moves[j].start()
     total = dc[...]
-    pieces, width = states.shape[0], states.shape[2]
     for j in range(pieces):
-        total = total + dot_nt(dye[:, j * width : (j + 1) * width], states[j, :N, :])
+        moves[j].wait()
+        total = total + dot_nt(held[:, j * width : (j + 1) * width], starts[j])
     out = total.astype(bf16)
     grad_c[...] = out
     for k in range(copies.shape[0]):
@@ -249,10 +258,12 @@
 
 
 def rest_kernel(
-    states, x, dy, xt, cum, loga, onehot, b, c, dxp, db, dcum, grad_x, grad_b, small
+    me, starts, end_a, end_b, end_c, end_d, x, dy, xt, cum, loga, onehot, b, c, dxp, db, dcum, grad_x, grad_b, small, ends
 ):
     heads = x.shape[1] // P_SIZE
-    pairs_piece = states.shape[2] // PAIR
+    pairs_piece = starts.shape[2] // PAIR
+    for k, part in enumerate((end_a, end_b, end_c, end_d)):
+        ends[(me[0] % GROUP) ^ k] = part[...]
     total = cum[...]
     last = total[SPAN - 1 :, :]
     tail = jnp.exp(last - total)
@@ -268,7 +279,7 @@
     for j in range(heads // 2):
         piece, at = j // pairs_piece, j % pairs_piece * PAIR
         lanes = slice(j * PAIR, (j + 1) * PAIR)
-        start, stop = states[piece, :N, at : at + PAIR], states[piece, N:, at : at + PAIR]
+        start, stop = starts[piece, :, at : at + PAIR], ends[piece, :, at : at + PAIR]
         xs = xt[:, lanes]
         x_wide, dy_wide = x[:, lanes].astype(f32), dy[:, lanes].astype(f32)
         falling = spread(tail, j, first)
@@ -336,19 +347,52 @@
     new_s[...] = second
 
 
-def call(kernel, out_shapes, *args, scratch=(), flops=0, limit=32):
+def call(kernel, out_shapes, *args, scratch=(), flops=0, limit=32, hbm=(), stay=()):
     size = sum(math.prod(a.shape) * a.dtype.itemsize for a in (*args, *out_shapes))
     whole = pl.BlockSpec(memory_space=pltpu.VMEM)
     scalars = pl.BlockSpec(memory_space=pltpu.SMEM)
+    far = pl.BlockSpec(memory_space=pltpu.HBM)
+    count = len(out_shapes)
+    args = [
+        pltpu.with_memory_space_constraint(a, pltpu.HBM) if at in stay else a
+        for at, a in enumerate(args)
+    ]
+
+    def body(*refs):
+        ins, rest = refs[: len(args)], refs[len(args) :]
+        outs, own, held = rest[:count], rest[count : count + len(scratch)], rest[count + len(scratch) :]
+        shown = list(outs)
+        for k, at in enumerate(hbm):
+            shown[at] = held[k]
+        kernel(*ins, *shown, *own)
+        copies = [
+            pltpu.make_async_copy(held[k], outs[at], held[-1].at[k]) for k, at in enumerate(hbm)
+        ]
+        for copy in copies:
+            copy.start()
+        for copy in copies:
+            copy.wait()
+
+    held = [pltpu.VMEM(out_shapes[at].shape, out_shapes[at].dtype) for at in hbm]
+    if hbm:
+        held.append(pltpu.SemaphoreType.DMA((len(hbm),)))
     out = pl.pallas_call(
-        kernel,
-        out_shape=tuple(out_shapes),
-        in_specs=[scalars if a.shape == (3,) else whole for a in args],
-        scratch_shapes=list(scratch),
+        body,
+        out_shape=tuple(
+            pltpu.HBM(o.shape, o.dtype) if at in hbm else o for at, o in enumerate(out_shapes)
+        ),
+        in_specs=[
+            far if at in stay else scalars if a.shape == (3,) else whole
+            for at, a in enumerate(args)
+        ],
+        out_specs=tuple(
+            far if at in hbm else whole for at in range(count)
+        ),
+        scratch_shapes=[*scratch, *held],
         compiler_params=pltpu.CompilerParams(vmem_limit_bytes=limit * 1024 * 1024),
         cost_estimate=pl.CostEstimate(flops=flops, bytes_accessed=size, transcendentals=0),
     )(*args)
-    return out[0] if len(out_shapes) == 1 else out
+    return out[0] if count == 1 else out
 
 
 def shift(a, senders, step):
@@ -437,6 +481,7 @@
         skip_gain[None],
         scratch=[pltpu.VMEM((SPAN, SPAN), f32)],
         flops=20 * SPAN * SPAN * width,
+        hbm=(0, 1, 2, 4, 5),
     )
     up, down = call(
         group_kernel,
@@ -450,30 +495,35 @@
     up_two, down_two = shift(up, inner, GROUP), shift(down, inner, -GROUP)
     up_two, down_two, dye = lax.optimization_barrier((up_two, down_two, dye))
     plan = ((0, ((0, 0),)), (1, ((1, 0),)), (3, ((2, 0),)), (2, ((3, 0), (4, half))))
-    states = call(
+    starts, *ends = call(
         scan_kernel,
-        [shaped((GROUP, 2 * N, piece), bf16)],
+        [shaped((GROUP, N, piece), bf16)] + [shaped((N, piece), bf16)] * GROUP,
         me,
         got,
         up,
         down,
         up_two,
         down_two,
+        scratch=[pltpu.VMEM((GROUP, N, piece), bf16)],
         flops=8 * N * width,
-    )
-    states, *pairs = lax.optimization_barrier((states, *pairs))
+        hbm=range(GROUP + 1),
+    )
+    starts, *pairs = lax.optimization_barrier((starts, *pairs))
     mine = call(stack_kernel, [shaped((streams, block, SPAN), bf16)], *pairs)
     left, right = trade(mine, "tensor", 1), trade(mine, "tensor", 3)
     far_a = trade(right[:half], "tensor", 1)
     far_b = trade(left[half:], "tensor", 3)
-    states = swap(states, "seq", near)
+    starts = swap(starts, "seq", near)
     grad_c, copies = call(
         grad_c_kernel,
         [shaped((SPAN, N), bf16), shaped((streams, SPAN, N), bf16)],
         dc,
         dye,
-        states,
+        starts,
+        scratch=[pltpu.VMEM((SPAN, width), bf16), pltpu.SemaphoreType.DMA((GROUP,))],
+        stay=(1,),
         flops=2 * SPAN * N * width,
+        hbm=(1,),
     )
     all_c = swap(copies, "dp")
     partial = call(
@@ -488,11 +538,15 @@
         far_b,
         flops=2 * tensors * layer.shape[1] * SPAN * N,
     )
+    partial, *ends = lax.optimization_barrier((partial, *ends))
     parts = swap(partial, "seq")
+    ends = [ends[0]] + [trade(ends[k], "seq", k) for k in range(1, GROUP)]
     grad_x, grad_b, small = call(
         rest_kernel,
         [wide, shaped((SPAN, N), bf16), small_tile],
-        states,
+        me,
+        starts,
+        *ends,
         x,
         dy,
         xt,
@@ -504,6 +558,7 @@
         dxp,
         db,
         dcum,
+        scratch=[pltpu.VMEM((GROUP, N, piece), bf16)],
         flops=6 * SPAN * N * width,
     )
     shard, sums = call(

time: 193 us -> 212 us (1.098)
  starting transfers between devices: 70.9 us -> 81.7 us
  waiting for transfers between devices: 49 us -> 59.8 us
  local copies, waits for them, and re-layouts: 13 us -> 7.19 us
  Pallas kernels: 21.7 us -> 25.5 us
    ppermute x8 -> x11, waiting for transfers between devices: 13.4 us -> 27.5 us  [trade(): return lax.ppermute(a, axis, [(i, i ^ k) for i in range(count)])]
    ppermute x8 -> x11, starting transfers between devices: 28.2 us -> 37.6 us  [trade(): return lax.ppermute(a, axis, [(i, i ^ k) for i in range(count)])]
    unnamed x52 -> x36, local copies, waits for them, and re-layouts: 11.5 us -> 5.74 us
    all_to_all x4, waiting for transfers between devices: 17.9 us -> 12.2 us  [swap(): return lax.all_to_all(a, axis, 0, 0, tiled=True, axis_index_groups=groups)]
    pallas_call x13, Pallas kernels: 21.7 us -> 25.5 us  [call(): pl.pallas_call(body, out_shape=tuple((pltpu.HBM(o.shape, o.dtype) if at i...]
    ppermute x4, waiting for transfers between devices: 17.7 us -> 20.1 us  [shift(): return lax.ppermute(a, 'seq', [(i, (i + step) % count) for i in senders])]
  transfers between devices with their start and end apart: 16 -> 19, of which waited for: 12 -> 12; matrix products, arithmetic and copies ran while one was open for 1% -> 1% of each run, Pallas kernels for 6% -> 7%
where the time goes in v5:
time: 212 us; the launch traced here: 211 us
  starting transfers between devices  81.7 us (39%)
  waiting for transfers between devices  59.8 us (28%)
  blocking collectives  35.7 us (17%)
  Pallas kernels  25.5 us (12%)
  local copies, waits for them, and re-layouts  7.19 us (3%)
    ppermute x11, starting transfers between devices, trade(): return lax.ppermute(a, axis, [(i, i ^ k) for i in range(count)])  37.6 us
    all_to_all x2, blocking collectives, swap(): return lax.all_to_all(a, axis, 0, 0, tiled=True, axis_index_groups=groups)  35.7 us
    all_to_all x4, starting transfers between devices, swap(): return lax.all_to_all(a, axis, 0, 0, tiled=True, axis_index_groups=groups)  29.4 us
    ppermute x11, waiting for transfers between devices, trade(): return lax.ppermute(a, axis, [(i, i ^ k) for i in range(count)])  27.5 us
    pallas_call x13, Pallas kernels, call(): pl.pallas_call(body, out_shape=tuple((pltpu.HBM(o.shape, o.dtype) if at i...  25.5 us
    ppermute x4, waiting for transfers between devices, shift(): return lax.ppermute(a, 'seq', [(i, (i + step) % count) for i in senders])  20.1 us
    ppermute x4, starting transfers between devices, shift(): return lax.ppermute(a, 'seq', [(i, (i + step) % count) for i in senders])  14.6 us
    all_to_all x4, waiting for transfers between devices, swap(): return lax.all_to_all(a, axis, 0, 0, tiled=True, axis_index_groups=groups)  12.2 us
  transfers between devices with their start and end apart: 19, of which 12 were waited for; matrix products, arithmetic and copies ran while one was open for 1% of the time, Pallas kernels for 7%

profile of v5, /device:TPU:1, one launch (start us, length us, event | category | flops | bytes accessed | tf_op | source)
XLA Modules:
  0.0 210.9 jit_solution(8743172367312432817)
XLA Ops:
  0.6 4.2 %shard_map.179 = (bf16[4,272,512]{2,1,0:T(8,128)(2,1)}, f32[128,128]{1,0:T(8,128)}, f32[128,128]{1,0:T(8,128)}, f32[8,128]{1,0:T(8,128)}) custom-call(f32[32,128]{1,0:T(8,128)} %bitcast.33, s32[1,32]{1,0:T(1,128)} %bitcast.35, f32[8,32]{1,0:T(8,128)} %bitcast.34, bf16[128,2048]{1,0:T(8,128)(2,1)} %bitcast.19, bf16[128,2048]{1,0:T(8,128)(2,1)} %bitcast.22, ...), custom_call_target="tpu_custom_call" | custom-call | flops 134217728 | bytes 2380928 | tf_op jit(solution)/shard_map/pallas_call | solution.py:379
  4.8 6.6 %all-to-all-start = ((bf16[4,272,512]{2,1,0:T(8,128)(2,1)}), bf16[4,272,512]{2,1,0:T(8,128)(2,1)S(1)}, u32[]{:S(2)}, u32[]{:S(2)}) async-start(bf16[4,272,512]{2,1,0:T(8,128)(2,1)} %get-tuple-element.64), calls=%async_computation | async-start | bytes 2228224 | tf_op jit(solution)/shard_map/all_to_all | solution.py:408
  12.3 5.9 %collective-permute-start = (bf16[4,256,128]{2,1,0:T(8,128)(2,1)S(1)}, bf16[4,256,128]{2,1,0:T(8,128)(2,1)S(1)}, u32[]{:S(2)}, u32[]{:S(2)}) collective-permute-start(bf16[4,256,128]{2,1,0:T(8,128)(2,1)S(1)} %get-tuple-element.67), channel_id=1, source_target_pairs={{0,1},{1,0},{2,3},{3,2},{4,5},{5,4},{6,7},{7,6},{8,9},{9,8},{10,11... | collective-permute-start | bytes 786440 | tf_op jit(solution)/shard_map/ppermute | solution.py:413
  23.9 5.1 %collective-permute-start.3 = (bf16[2,256,128]{2,1,0:T(8,128)(2,1)S(1)}, bf16[2,256,128]{2,1,0:T(8,128)(2,1)S(1)}, u32[]{:S(2)}, u32[]{:S(2)}) collective-permute-start(bf16[2,256,128]{2,1,0:T(8,128)(2,1)S(1)} %get-tuple-element.71), channel_id=1, source_target_pairs={{0,6},{1,7},{2,4},{3,5},{4,2},{5,3},{6,0},{7,1},{8,14},{9,15},{10,... | collective-permute-start | bytes 393224 | tf_op jit(solution)/shard_map/ppermute | solution.py:413
  31.9 5.7 %all-to-all-done.refs_1_ = bf16[4,272,512]{2,1,0:T(8,128)(2,1)S(1)} async-done(((bf16[4,272,512]{2,1,0:T(8,128)(2,1)}), bf16[4,272,512]{2,1,0:T(8,128)(2,1)S(1)}, u32[]{:S(2)}, u32[]{:S(2)}) %all-to-all-start) | async-done | bytes 1114144 | tf_op jit(solution)/shard_map/all_to_all | solution.py:408
  38.4 9.2 %collective-permute-start.4 = (bf16[144,512]{1,0:T(8,128)(2,1)S(1)}, bf16[144,512]{1,0:T(8,128)(2,1)S(1)}, u32[]{:S(2)}, u32[]{:S(2)}) collective-permute-start(bf16[144,512]{1,0:T(8,128)(2,1)S(1)} %get-tuple-element.73), channel_id=1, source_target_pairs={{0,128},{32,160},{64,192},{96,224},{128,256},{160,288},{192,320},{... | collective-permute-start | bytes 442376 | tf_op jit(solution)/shard_map/ppermute | solution.py:400
  47.7 3.5 %collective-permute-start.5 = (bf16[144,512]{1,0:T(8,128)(2,1)S(1)}, bf16[144,512]{1,0:T(8,128)(2,1)S(1)}, u32[]{:S(2)}, u32[]{:S(2)}) collective-permute-start(bf16[144,512]{1,0:T(8,128)(2,1)S(1)} %get-tuple-element.74), channel_id=1, source_target_pairs={{0,384},{32,416},{64,448},{96,480},{128,0},{160,32},{192,64},{224,... | collective-permute-start | bytes 442376 | tf_op jit(solution)/shard_map/ppermute | solution.py:400
  52.9 12.6 %collective-permute-done.5.refs_3_ = bf16[144,512]{1,0:T(8,128)(2,1)S(1)} collective-permute-done((bf16[144,512]{1,0:T(8,128)(2,1)S(1)}, bf16[144,512]{1,0:T(8,128)(2,1)S(1)}, u32[]{:S(2)}, u32[]{:S(2)}) %collective-permute-start.5) | collective-permute-done | bytes 147488 | tf_op jit(solution)/shard_map/ppermute | solution.py:400
  66.8 6.2 %shard_map.183 = (f32[128,2048]{1,0:T(8,128)}, bf16[128,2048]{1,0:T(8,128)(2,1)}, bf16[128,2048]{1,0:T(8,128)(2,1)}, f32[128,128]{1,0:T(8,128)S(1)}, f32[128,128]{1,0:T(8,128)}, /*index=5*/f32[128,128]{1,0:T(8,128)}) custom-call(f32[128,128]{1,0:T(8,128)S(1)} %copy-done.9, bf16[128,2048]{1,0:T(8,128)(2,1)S(1)} %bitcast.20, bf16[128,2048]{1,0:T(8,128)(2,1)S(1)} %bitcast.23, ...), custom_call_target="tpu_custom_call" | custom-call | flops 671088640 | bytes 3473536 | tf_op jit(solution)/shard_map/pallas_call | solution.py:379
  73.0 6.6 %collective-permute-done.7.refs_5_ = bf16[144,512]{1,0:T(8,128)(2,1)S(1)} collective-permute-done((bf16[144,512]{1,0:T(8,128)(2,1)S(1)}, bf16[144,512]{1,0:T(8,128)(2,1)S(1)}, u32[]{:S(2)}, u32[]{:S(2)}) %collective-permute-start.7) | collective-permute-done | bytes 147488 | tf_op jit(solution)/shard_map/ppermute | solution.py:400
  81.6 5.7 %all-to-all-start.1 = ((bf16[4,128,512]{2,1,0:T(8,128)(2,1)}), bf16[4,128,512]{2,1,0:T(8,128)(2,1)S(1)}, u32[]{:S(2)}, u32[]{:S(2)}) async-start(bf16[4,128,512]{2,1,0:T(8,128)(2,1)} %get-tuple-element.84), calls=%async_computation.1 | async-start | bytes 1048576 | tf_op jit(solution)/shard_map/all_to_all | solution.py:408
  87.4 4.7 %collective-permute-start.9 = (bf16[8,256,128]{2,1,0:T(8,128)(2,1)S(1)}, bf16[8,256,128]{2,1,0:T(8,128)(2,1)S(1)}, u32[]{:S(2)}, u32[]{:S(2)}) collective-permute-start(bf16[8,256,128]{2,1,0:T(8,128)(2,1)S(1)} %shard_map.186.refs_2_), channel_id=1, source_target_pairs={{0,24},{8,16},{16,8},{24,0},{1,25},{9,17},{17,9},{25,1},{2,26},{10... | collective-permute-start | bytes 1572872 | tf_op jit(solution)/shard_map/ppermute | solution.py:413
  94.1 9.0 %collective-permute-done.9.refs_4_ = bf16[8,256,128]{2,1,0:T(8,128)(2,1)S(1)} collective-permute-done((bf16[8,256,128]{2,1,0:T(8,128)(2,1)S(1)}, bf16[8,256,128]{2,1,0:T(8,128)(2,1)S(1)}, u32[]{:S(2)}, u32[]{:S(2)}) %collective-permute-start.9) | collective-permute-done | bytes 524320 | tf_op jit(solution)/shard_map/ppermute | solution.py:413
  106.8 4.1 %collective-permute-start.11 = (bf16[4,256,128]{2,1,0:T(8,128)(2,1)}, bf16[4,256,128]{2,1,0:T(8,128)(2,1)}, u32[]{:S(2)}, u32[]{:S(2)}) collective-permute-start(bf16[4,256,128]{2,1,0:T(8,128)(2,1)} %slice.9), channel_id=1, source_target_pairs={{0,24},{8,16},{16,8},{24,0},{1,25},{9,17},{17,9},{25,1},{2,26},{10... | collective-permute-start | bytes 786440 | tf_op jit(solution)/shard_map/ppermute | solution.py:413
  113.9 6.5 %all-to-all-start.2 = ((bf16[8,128,128]{2,1,0:T(8,128)(2,1)}), bf16[8,128,128]{2,1,0:T(8,128)(2,1)S(1)}, u32[]{:S(2)}, u32[]{:S(2)}) async-start(bf16[8,128,128]{2,1,0:T(8,128)(2,1)} %get-tuple-element.87), calls=%async_computation.2 | async-start | bytes 524288 | tf_op jit(solution)/shard_map/all_to_all | solution.py:408
  120.4 6.5 %all-to-all-done.2.refs_1_ = bf16[8,128,128]{2,1,0:T(8,128)(2,1)S(1)} async-done(((bf16[8,128,128]{2,1,0:T(8,128)(2,1)}), bf16[8,128,128]{2,1,0:T(8,128)(2,1)S(1)}, u32[]{:S(2)}, u32[]{:S(2)}) %all-to-all-start.2) | async-done | bytes 262176 | tf_op jit(solution)/shard_map/all_to_all | solution.py:408
  129.3 10.6 %all-to-all-start.3 = ((bf16[16,64,128]{2,1,0:T(8,128)(2,1)}), bf16[16,64,128]{2,1,0:T(8,128)(2,1)S(1)}, u32[]{:S(2)}, u32[]{:S(2)}) async-start(bf16[16,64,128]{2,1,0:T(8,128)(2,1)} %shard_map.187), calls=%async_computation.3 | async-start | bytes 524288 | tf_op jit(solution)/shard_map/all_to_all | solution.py:408
  139.9 3.3 %collective-permute-start.12 = (bf16[128,512]{1,0:T(8,128)(2,1)}, bf16[128,512]{1,0:T(8,128)(2,1)S(1)}, u32[]{:S(2)}, u32[]{:S(2)}) collective-permute-start(bf16[128,512]{1,0:T(8,128)(2,1)} %get-tuple-element.97), channel_id=1, source_target_pairs={{0,32},{32,0},{64,96},{96,64},{128,160},{160,128},{192,224},{224,1... | collective-permute-start | bytes 393224 | tf_op jit(solution)/shard_map/ppermute | solution.py:413
  143.2 4.0 %collective-permute-start.13 = (bf16[128,512]{1,0:T(8,128)(2,1)}, bf16[128,512]{1,0:T(8,128)(2,1)S(1)}, u32[]{:S(2)}, u32[]{:S(2)}) collective-permute-start(bf16[128,512]{1,0:T(8,128)(2,1)} %get-tuple-element.98), channel_id=1, source_target_pairs={{0,64},{32,96},{64,0},{96,32},{128,192},{160,224},{192,128},{224,1... | collective-permute-start | bytes 393224 | tf_op jit(solution)/shard_map/ppermute | solution.py:413
  149.4 8.9 %collective-permute-done.12.refs_3_ = bf16[128,512]{1,0:T(8,128)(2,1)S(1)} collective-permute-done((bf16[128,512]{1,0:T(8,128)(2,1)}, bf16[128,512]{1,0:T(8,128)(2,1)S(1)}, u32[]{:S(2)}, u32[]{:S(2)}) %collective-permute-start.12) | collective-permute-done | bytes 131104 | tf_op jit(solution)/shard_map/ppermute | solution.py:413
  158.2 5.2 %collective-permute-done.14.refs_5_ = bf16[128,512]{1,0:T(8,128)(2,1)S(1)} collective-permute-done((bf16[128,512]{1,0:T(8,128)(2,1)}, bf16[128,512]{1,0:T(8,128)(2,1)S(1)}, u32[]{:S(2)}, u32[]{:S(2)}) %collective-permute-start.14) | collective-permute-done | bytes 131104 | tf_op jit(solution)/shard_map/ppermute | solution.py:413
  169.1 4.5 %shard_map.188 = (bf16[128,2048]{1,0:T(8,128)(2,1)}, bf16[128,128]{1,0:T(8,128)(2,1)}, f32[8,128]{1,0:T(8,128)S(1)}) custom-call(s32[3]{0:T(128)S(1)} %pad_add_fusion.refs_0_, bf16[4,128,512]{2,1,0:T(8,128)(2,1)S(1)} %all-to-all-done.1.refs_2_.refs_1_, bf16[128,512]{1,0:T(8,128)(2,1)S(1)} %copy-done.7, bf16[128,512]{1,0:T(8,128)(2,1)S(1)} %collective-permute-done.12.refs_3_, ...), custom_call_target="tpu_custom_call" | custom-call | flops 201326592 | bytes 4562956 | tf_op jit(solution)/shard_map/pallas_call | solution.py:379
  173.8 22.5 %all_to_all.30.refs_0_ = f32[16,8,128]{2,1,0:T(8,128)S(1)} all-to-all(f32[16,8,128]{2,1,0:T(8,128)S(1)} %get-tuple-element.111), channel_id=1, replica_groups=mesh['seq'=16,'tensor'=4,'dp'=8] {'seq'}, dimensions={0} | all-to-all | bytes 131072 | tf_op jit(solution)/shard_map/all_to_all | solution.py:408
  196.4 13.2 %all_to_all.31.refs_1_ = f32[32,8,128]{2,1,0:T(8,128)S(1)} all-to-all(f32[32,8,128]{2,1,0:T(8,128)S(1)} %shard_map.190), channel_id=1, replica_groups=mesh['seq'=16,'tensor'=4,'dp'=8] {'tensor','dp'}, dimensions={0} | all-to-all | bytes 262144 | tf_op jit(solution)/shard_map/all_to_all | solution.py:408
  (68 shorter events, 35.8 us)
Async XLA Ops:
  4.8 32.8 %all-to-all-start = ((bf16[4,272,512]{2,1,0:T(8,128)(2,1)}), bf16[4,272,512]{2,1,0:T(8,128)(2,1)S(1)}, u32[]{:S(2)}, u32[]{:S(2)}) async-start(bf16[4,272,512]{2,1,0:T(8,128)(2,1)} %get-tuple-element.64), calls=%async_computation | async-start | bytes 2228224 | tf_op jit(solution)/shard_map/all_to_all | solution.py:408
  11.4 55.3 %copy-start.1 = (bf16[1,128,2048]{2,1,0:T(8,128)(2,1)S(1)}, bf16[1,128,2048]{2,1,0:T(8,128)(2,1)}, u32[]{:S(2)}) copy-start(bf16[1,128,2048]{2,1,0:T(8,128)(2,1)} %param.19) | copy-start | bytes 1572868
  11.4 55.3 %copy-start.5 = (bf16[1,128,128]{2,1,0:T(8,128)(2,1)S(1)}, bf16[1,128,128]{2,1,0:T(8,128)(2,1)}, u32[]{:S(2)}) copy-start(bf16[1,128,128]{2,1,0:T(8,128)(2,1)} %param.13) | copy-start | bytes 98308
  11.4 55.3 %copy-start.6 = (bf16[1,128,128]{2,1,0:T(8,128)(2,1)S(1)}, bf16[1,128,128]{2,1,0:T(8,128)(2,1)}, u32[]{:S(2)}) copy-start(bf16[1,128,128]{2,1,0:T(8,128)(2,1)} %param.14) | copy-start | bytes 98308
  11.4 55.3 %copy-start.9 = (f32[128,128]{1,0:T(8,128)S(1)}, f32[128,128]{1,0:T(8,128)}, u32[]{:S(2)}) copy-start(f32[128,128]{1,0:T(8,128)} %get-tuple-element.75.refs_0_.refs_9_) | copy-start | bytes 196612
  11.4 55.3 %copy-start.17 = (f32[32]{0:T(128)S(1)}, f32[32]{0:T(128)}, u32[]{:S(2)}) copy-start(f32[32]{0:T(128)} %param.18) | copy-start | bytes 388
  12.3 7.0 %collective-permute-start = (bf16[4,256,128]{2,1,0:T(8,128)(2,1)S(1)}, bf16[4,256,128]{2,1,0:T(8,128)(2,1)S(1)}, u32[]{:S(2)}, u32[]{:S(2)}) collective-permute-start(bf16[4,256,128]{2,1,0:T(8,128)(2,1)S(1)} %get-tuple-element.67), channel_id=1, source_target_pairs={{0,1},{1,0},{2,3},{3,2},{4,5},{5,4},{6,7},{7,6},{8,9},{9,8},{10,11... | collective-permute-start | bytes 786440 | tf_op jit(solution)/shard_map/ppermute | solution.py:413
  19.4 9.6 %collective-permute-start.1 = (bf16[2,256,128]{2,1,0:T(8,128)(2,1)S(1)}, bf16[2,256,128]{2,1,0:T(8,128)(2,1)S(1)}, u32[]{:S(2)}, u32[]{:S(2)}) collective-permute-start(bf16[2,256,128]{2,1,0:T(8,128)(2,1)S(1)} %get-tuple-element.69), channel_id=1, source_target_pairs={{0,2},{1,3},{2,0},{3,1},{4,6},{5,7},{6,4},{7,5},{8,10},{9,11},{10,... | collective-permute-start | bytes 393224 | tf_op jit(solution)/shard_map/ppermute | solution.py:413
  21.3 8.1 %collective-permute-start.2 = (bf16[2,256,128]{2,1,0:T(8,128)(2,1)S(1)}, bf16[2,256,128]{2,1,0:T(8,128)(2,1)S(1)}, u32[]{:S(2)}, u32[]{:S(2)}) collective-permute-start(bf16[2,256,128]{2,1,0:T(8,128)(2,1)S(1)} %get-tuple-element.70), channel_id=1, source_target_pairs={{0,4},{1,5},{2,6},{3,7},{4,0},{5,1},{6,2},{7,3},{8,12},{9,13},{10,... | collective-permute-start | bytes 393224 | tf_op jit(solution)/shard_map/ppermute | solution.py:413
  23.9 8.1 %collective-permute-start.3 = (bf16[2,256,128]{2,1,0:T(8,128)(2,1)S(1)}, bf16[2,256,128]{2,1,0:T(8,128)(2,1)S(1)}, u32[]{:S(2)}, u32[]{:S(2)}) collective-permute-start(bf16[2,256,128]{2,1,0:T(8,128)(2,1)S(1)} %get-tuple-element.71), channel_id=1, source_target_pairs={{0,6},{1,7},{2,4},{3,5},{4,2},{5,3},{6,0},{7,1},{8,14},{9,15},{10,... | collective-permute-start | bytes 393224 | tf_op jit(solution)/shard_map/ppermute | solution.py:413
  38.4 13.8 %collective-permute-start.4 = (bf16[144,512]{1,0:T(8,128)(2,1)S(1)}, bf16[144,512]{1,0:T(8,128)(2,1)S(1)}, u32[]{:S(2)}, u32[]{:S(2)}) collective-permute-start(bf16[144,512]{1,0:T(8,128)(2,1)S(1)} %get-tuple-element.73), channel_id=1, source_target_pairs={{0,128},{32,160},{64,192},{96,224},{128,256},{160,288},{192,320},{... | collective-permute-start | bytes 442376 | tf_op jit(solution)/shard_map/ppermute | solution.py:400
  47.7 17.7 %collective-permute-start.5 = (bf16[144,512]{1,0:T(8,128)(2,1)S(1)}, bf16[144,512]{1,0:T(8,128)(2,1)S(1)}, u32[]{:S(2)}, u32[]{:S(2)}) collective-permute-start(bf16[144,512]{1,0:T(8,128)(2,1)S(1)} %get-tuple-element.74), channel_id=1, source_target_pairs={{0,384},{32,416},{64,448},{96,480},{128,0},{160,32},{192,64},{224,... | collective-permute-start | bytes 442376 | tf_op jit(solution)/shard_map/ppermute | solution.py:400
  52.2 20.8 %collective-permute-start.6 = (bf16[144,512]{1,0:T(8,128)(2,1)S(1)}, bf16[144,512]{1,0:T(8,128)(2,1)S(1)}, u32[]{:S(2)}, u32[]{:S(2)}) collective-permute-start(bf16[144,512]{1,0:T(8,128)(2,1)S(1)} %collective-permute-done.4.refs_2_), channel_id=1, source_target_pairs={{128,256},{160,288},{192,320},{224,352},{256,384},{288,416},{320,4... | collective-permute-start | bytes 442376 | tf_op jit(solution)/shard_map/ppermute | solution.py:400
  65.4 14.2 %collective-permute-start.7 = (bf16[144,512]{1,0:T(8,128)(2,1)S(1)}, bf16[144,512]{1,0:T(8,128)(2,1)S(1)}, u32[]{:S(2)}, u32[]{:S(2)}) collective-permute-start(bf16[144,512]{1,0:T(8,128)(2,1)S(1)} %collective-permute-done.5.refs_3_), channel_id=1, source_target_pairs={{128,0},{160,32},{192,64},{224,96},{256,128},{288,160},{320,192},{... | collective-permute-start | bytes 442376 | tf_op jit(solution)/shard_map/ppermute | solution.py:400
  81.6 29.3 %all-to-all-start.1 = ((bf16[4,128,512]{2,1,0:T(8,128)(2,1)}), bf16[4,128,512]{2,1,0:T(8,128)(2,1)S(1)}, u32[]{:S(2)}, u32[]{:S(2)}) async-start(bf16[4,128,512]{2,1,0:T(8,128)(2,1)} %get-tuple-element.84), calls=%async_computation.1 | async-start | bytes 1048576 | tf_op jit(solution)/shard_map/all_to_all | solution.py:408
  87.4 15.7 %collective-permute-start.9 = (bf16[8,256,128]{2,1,0:T(8,128)(2,1)S(1)}, bf16[8,256,128]{2,1,0:T(8,128)(2,1)S(1)}, u32[]{:S(2)}, u32[]{:S(2)}) collective-permute-start(bf16[8,256,128]{2,1,0:T(8,128)(2,1)S(1)} %shard_map.186.refs_2_), channel_id=1, source_target_pairs={{0,24},{8,16},{16,8},{24,0},{1,25},{9,17},{17,9},{25,1},{2,26},{10... | collective-permute-start | bytes 1572872 | tf_op jit(solution)/shard_map/ppermute | solution.py:413
  92.1 14.0 %collective-permute-start.8 = (bf16[8,256,128]{2,1,0:T(8,128)(2,1)S(1)}, bf16[8,256,128]{2,1,0:T(8,128)(2,1)S(1)}, u32[]{:S(2)}, u32[]{:S(2)}) collective-permute-start(bf16[8,256,128]{2,1,0:T(8,128)(2,1)S(1)} %shard_map.186.refs_2_), channel_id=1, source_target_pairs={{0,8},{8,0},{16,24},{24,16},{1,9},{9,1},{17,25},{25,17},{2,10},{10... | collective-permute-start | bytes 1572872 | tf_op jit(solution)/shard_map/ppermute | solution.py:413
  103.8 16.6 %collective-permute-start.10 = (bf16[4,256,128]{2,1,0:T(8,128)(2,1)}, bf16[4,256,128]{2,1,0:T(8,128)(2,1)}, u32[]{:S(2)}, u32[]{:S(2)}) collective-permute-start(bf16[4,256,128]{2,1,0:T(8,128)(2,1)} %slice.8), channel_id=1, source_target_pairs={{0,8},{8,0},{16,24},{24,16},{1,9},{9,1},{17,25},{25,17},{2,10},{10... | collective-permute-start | bytes 786440 | tf_op jit(solution)/shard_map/ppermute | solution.py:413
  106.8 13.6 %collective-permute-start.11 = (bf16[4,256,128]{2,1,0:T(8,128)(2,1)}, bf16[4,256,128]{2,1,0:T(8,128)(2,1)}, u32[]{:S(2)}, u32[]{:S(2)}) collective-permute-start(bf16[4,256,128]{2,1,0:T(8,128)(2,1)} %slice.9), channel_id=1, source_target_pairs={{0,24},{8,16},{16,8},{24,0},{1,25},{9,17},{17,9},{25,1},{2,26},{10... | collective-permute-start | bytes 786440 | tf_op jit(solution)/shard_map/ppermute | solution.py:413
  113.9 13.0 %all-to-all-start.2 = ((bf16[8,128,128]{2,1,0:T(8,128)(2,1)}), bf16[8,128,128]{2,1,0:T(8,128)(2,1)S(1)}, u32[]{:S(2)}, u32[]{:S(2)}) async-start(bf16[8,128,128]{2,1,0:T(8,128)(2,1)} %get-tuple-element.87), calls=%async_computation.2 | async-start | bytes 524288 | tf_op jit(solution)/shard_map/all_to_all | solution.py:408
  129.3 44.3 %all-to-all-start.3 = ((bf16[16,64,128]{2,1,0:T(8,128)(2,1)}), bf16[16,64,128]{2,1,0:T(8,128)(2,1)S(1)}, u32[]{:S(2)}, u32[]{:S(2)}) async-start(bf16[16,64,128]{2,1,0:T(8,128)(2,1)} %shard_map.187), calls=%async_computation.3 | async-start | bytes 524288 | tf_op jit(solution)/shard_map/all_to_all | solution.py:408
  139.9 18.3 %collective-permute-start.12 = (bf16[128,512]{1,0:T(8,128)(2,1)}, bf16[128,512]{1,0:T(8,128)(2,1)S(1)}, u32[]{:S(2)}, u32[]{:S(2)}) collective-permute-start(bf16[128,512]{1,0:T(8,128)(2,1)} %get-tuple-element.97), channel_id=1, source_target_pairs={{0,32},{32,0},{64,96},{96,64},{128,160},{160,128},{192,224},{224,1... | collective-permute-start | bytes 393224 | tf_op jit(solution)/shard_map/ppermute | solution.py:413
  143.2 15.1 %collective-permute-start.13 = (bf16[128,512]{1,0:T(8,128)(2,1)}, bf16[128,512]{1,0:T(8,128)(2,1)S(1)}, u32[]{:S(2)}, u32[]{:S(2)}) collective-permute-start(bf16[128,512]{1,0:T(8,128)(2,1)} %get-tuple-element.98), channel_id=1, source_target_pairs={{0,64},{32,96},{64,0},{96,32},{128,192},{160,224},{192,128},{224,1... | collective-permute-start | bytes 393224 | tf_op jit(solution)/shard_map/ppermute | solution.py:413
  147.2 16.3 %collective-permute-start.14 = (bf16[128,512]{1,0:T(8,128)(2,1)}, bf16[128,512]{1,0:T(8,128)(2,1)S(1)}, u32[]{:S(2)}, u32[]{:S(2)}) collective-permute-start(bf16[128,512]{1,0:T(8,128)(2,1)} %get-tuple-element.99), channel_id=1, source_target_pairs={{0,96},{32,64},{64,32},{96,0},{128,224},{160,192},{192,160},{224,1... | collective-permute-start | bytes 393224 | tf_op jit(solution)/shard_map/ppermute | solution.py:413
  (13 other events, 275.0 us)

commit v6 on v4

--- a/solution.py
+++ b/solution.py
@@ -6,6 +6,7 @@
 from jax import lax
 from jax.experimental import pallas as pl
 from jax.experimental.pallas import tpu as pltpu
+from jax.sharding import Mesh
 from jax.sharding import PartitionSpec as P
 
 P_SIZE = 64
@@ -14,6 +15,7 @@
 PAIR = 2 * P_SIZE
 LOG_ROWS = 16
 GROUP = 4
+SEQ = ("far", "near")
 
 beta_one = 0.9
 beta_two = 0.95
@@ -312,11 +314,12 @@
         copies[k] = out
 
 
-def update_kernel(streams, size, me, got, shard, weight, moment_one, moment_two, new_w, new_m, new_s, rates, skips):
+def update_kernel(fars, size, me, got, shard, weight, moment_one, moment_two, new_w, new_m, new_s, rates, skips):
+    tensors = got.shape[0] // fars
     total = jnp.sum(got[...], axis=0)
-    mine = got[me[2] * streams]
-    for k in range(1, streams):
-        mine = mine + got[me[2] * streams + k]
+    mine = got[me[2]]
+    for k in range(1, fars):
+        mine = mine + got[k * tensors + me[2]]
     here = (iota((8, 128), 0) == 0) & (iota((8, 128), 1) == 127)
     square = jnp.sum(jnp.where(here, total, 0.0), keepdims=True)
     heads = rates.shape[1]
@@ -336,32 +339,65 @@
     new_s[...] = second
 
 
-def call(kernel, out_shapes, *args, scratch=(), flops=0, limit=32):
+def call(kernel, out_shapes, *args, scratch=(), flops=0, limit=32, hbm=(), stay=()):
     size = sum(math.prod(a.shape) * a.dtype.itemsize for a in (*args, *out_shapes))
     whole = pl.BlockSpec(memory_space=pltpu.VMEM)
     scalars = pl.BlockSpec(memory_space=pltpu.SMEM)
+    far = pl.BlockSpec(memory_space=pltpu.HBM)
+    count = len(out_shapes)
+    args = [
+        pltpu.with_memory_space_constraint(a, pltpu.HBM) if at in stay else a
+        for at, a in enumerate(args)
+    ]
+
+    def body(*refs):
+        ins, rest = refs[: len(args)], refs[len(args) :]
+        outs, own, held = rest[:count], rest[count : count + len(scratch)], rest[count + len(scratch) :]
+        shown = list(outs)
+        for k, at in enumerate(hbm):
+            shown[at] = held[k]
+        kernel(*ins, *shown, *own)
+        copies = [
+            pltpu.make_async_copy(held[k], outs[at], held[-1].at[k]) for k, at in enumerate(hbm)
+        ]
+        for copy in copies:
+            copy.start()
+        for copy in copies:
+            copy.wait()
+
+    held = [pltpu.VMEM(out_shapes[at].shape, out_shapes[at].dtype) for at in hbm]
+    if hbm:
+        held.append(pltpu.SemaphoreType.DMA((len(hbm),)))
     out = pl.pallas_call(
-        kernel,
-        out_shape=tuple(out_shapes),
-        in_specs=[scalars if a.shape == (3,) else whole for a in args],
-        scratch_shapes=list(scratch),
+        body,
+        out_shape=tuple(
+            pltpu.HBM(o.shape, o.dtype) if at in hbm else o for at, o in enumerate(out_shapes)
+        ),
+        in_specs=[
+            far if at in stay else scalars if a.shape == (3,) else whole
+            for at, a in enumerate(args)
+        ],
+        out_specs=tuple(
+            far if at in hbm else whole for at in range(count)
+        ),
+        scratch_shapes=[*scratch, *held],
         compiler_params=pltpu.CompilerParams(vmem_limit_bytes=limit * 1024 * 1024),
         cost_estimate=pl.CostEstimate(flops=flops, bytes_accessed=size, transcendentals=0),
     )(*args)
-    return out[0] if len(out_shapes) == 1 else out
+    return out[0] if count == 1 else out
 
 
 def shift(a, senders, step):
-    count = lax.axis_size("seq")
-    return lax.ppermute(a, "seq", [(i, (i + step) % count) for i in senders])
+    count = lax.axis_size(SEQ)
+    return lax.ppermute(a, SEQ, [(i, (i + step) % count) for i in senders])
 
 
 def shaped(shape, dtype):
     return jax.ShapeDtypeStruct(shape, dtype)
 
 
-def swap(a, axis, groups=None):
-    return lax.all_to_all(a, axis, 0, 0, tiled=True, axis_index_groups=groups)
+def swap(a, axis):
+    return lax.all_to_all(a, axis, 0, 0, tiled=True)
 
 
 def trade(a, axis, k):
@@ -383,13 +419,12 @@
     moment_one,
     moment_two,
 ):
-    seqs, streams, tensors = (lax.axis_size(a) for a in ("seq", "dp", "tensor"))
-    me = jnp.stack([lax.axis_index(a) for a in ("seq", "dp", "tensor")]).astype(jnp.int32)
+    seqs, streams, tensors = (lax.axis_size(a) for a in (SEQ, "dp", "tensor"))
+    me = jnp.stack([lax.axis_index(a) for a in (SEQ, "dp", "tensor")]).astype(jnp.int32)
     x, dy, b, c = seq_values[0], grad_out[0], proj_b[0], proj_c[0]
     heads = skip_gain.shape[0]
     width = heads * P_SIZE
     piece = width // GROUP
-    near = [[i + k for k in range(GROUP)] for i in range(0, seqs, GROUP)]
     tile = shaped((SPAN, 128), f32)
     small_tile = shaped((8, 128), f32)
     wide = shaped((SPAN, width), bf16)
@@ -407,7 +442,7 @@
         limit=60,
     )
     layer, st = lax.optimization_barrier((layer_input[0], st))
-    got = swap(st, "seq", near)
+    got = swap(st, "near")
 
     rows = weight_c.shape[0]
     block = layer.shape[1] // streams
@@ -437,6 +472,7 @@
         skip_gain[None],
         scratch=[pltpu.VMEM((SPAN, SPAN), f32)],
         flops=20 * SPAN * SPAN * width,
+        hbm=(0, 1, 2, 4, 5),
     )
     up, down = call(
         group_kernel,
@@ -466,7 +502,7 @@
     left, right = trade(mine, "tensor", 1), trade(mine, "tensor", 3)
     far_a = trade(right[:half], "tensor", 1)
     far_b = trade(left[half:], "tensor", 3)
-    states = swap(states, "seq", near)
+    states = swap(states, "near")
     grad_c, copies = call(
         grad_c_kernel,
         [shaped((SPAN, N), bf16), shaped((streams, SPAN, N), bf16)],
@@ -474,6 +510,7 @@
         dye,
         states,
         flops=2 * SPAN * N * width,
+        hbm=(1,),
     )
     all_c = swap(copies, "dp")
     partial = call(
@@ -488,7 +525,7 @@
         far_b,
         flops=2 * tensors * layer.shape[1] * SPAN * N,
     )
-    parts = swap(partial, "seq")
+    parts = swap(partial, SEQ)
     grad_x, grad_b, small = call(
         rest_kernel,
         [wide, shaped((SPAN, N), bf16), small_tile],
@@ -508,19 +545,20 @@
     )
     shard, sums = call(
         shard_kernel,
-        [shaped((rows, N), f32), shaped((seqs, 8, 128), f32)],
+        [shaped((rows, N), f32), shaped((GROUP * streams, 8, 128), f32)],
         parts,
         small,
         flops=seqs * rows * N,
     )
-    sums = call(sum_kernel, [shaped((tensors * streams, 8, 128), f32)], swap(sums, "seq"))
+    fars = seqs // GROUP
+    sums = call(sum_kernel, [shaped((fars * tensors, 8, 128), f32)], swap(sums, ("near", "dp")))
     matrix = shaped((rows, N), f32)
     size = rows * seqs * streams * N * tensors
     new_weight, new_moment, new_second, rates, skips = call(
-        functools.partial(update_kernel, streams, size),
+        functools.partial(update_kernel, fars, size),
         [matrix, matrix, matrix, shaped((decay_rate.shape[1], heads), f32), shaped((1, heads), f32)],
         me,
-        swap(sums, ("tensor", "dp")),
+        swap(sums, ("far", "tensor")),
         shard,
         weight_c,
         moment_one,
@@ -539,8 +577,11 @@
 
 
 def solution(mesh):
-    wide = P("dp", "seq", "tensor")
-    shard = P(("seq", "dp"), "tensor")
+    sizes = dict(mesh.shape)
+    devices = mesh.devices.reshape(-1, GROUP, sizes["tensor"], sizes["dp"])
+    mesh = Mesh(devices, (*SEQ, "tensor", "dp"))
+    wide = P("dp", SEQ, "tensor")
+    shard = P((*SEQ, "dp"), "tensor")
     return jax.shard_map(
         local,
         mesh=mesh,

time: 193 us -> 197 us (1.021)
  local copies, waits for them, and re-layouts: 13 us -> 8.51 us
  blocking collectives: 36 us -> 39.8 us
  waiting for transfers between devices: 49 us -> 51.6 us
  Pallas kernels: 21.7 us -> 23.7 us
    unnamed x52 -> x40, local copies, waits for them, and re-layouts: 11.5 us -> 7.03 us
    all_to_all x2, blocking collectives: 36 us -> 39.8 us  [swap(): return lax.all_to_all(a, axis, 0, 0, tiled=True)]
    ppermute x4, waiting for transfers between devices: 17.7 us -> 20.2 us  [shift(): return lax.ppermute(a, SEQ, [(i, (i + step) % count) for i in senders])]
    pallas_call x13, Pallas kernels: 21.7 us -> 23.7 us  [call(): pl.pallas_call(body, out_shape=tuple((pltpu.HBM(o.shape, o.dtype) if at i...]
where the time goes in v6:
time: 197 us; the launch traced here: 195 us
  starting transfers between devices  70.9 us (36%)
  waiting for transfers between devices  51.6 us (26%)
  blocking collectives  39.8 us (20%)
  Pallas kernels  23.7 us (12%)
  local copies, waits for them, and re-layouts  8.51 us (4%)
    all_to_all x2, blocking collectives, swap(): return lax.all_to_all(a, axis, 0, 0, tiled=True)  39.8 us
    ppermute x8, starting transfers between devices, trade(): return lax.ppermute(a, axis, [(i, i ^ k) for i in range(count)])  28.2 us
    all_to_all x4, starting transfers between devices, swap(): return lax.all_to_all(a, axis, 0, 0, tiled=True)  28.1 us
    pallas_call x13, Pallas kernels, call(): pl.pallas_call(body, out_shape=tuple((pltpu.HBM(o.shape, o.dtype) if at i...  23.7 us
    ppermute x4, waiting for transfers between devices, shift(): return lax.ppermute(a, SEQ, [(i, (i + step) % count) for i in senders])  20.2 us
    all_to_all x4, waiting for transfers between devices, swap(): return lax.all_to_all(a, axis, 0, 0, tiled=True)  17.9 us
    ppermute x4, starting transfers between devices, shift(): return lax.ppermute(a, SEQ, [(i, (i + step) % count) for i in senders])  14.6 us
    ppermute x8, waiting for transfers between devices, trade(): return lax.ppermute(a, axis, [(i, i ^ k) for i in range(count)])  13.4 us
  transfers between devices with their start and end apart: 16, of which 12 were waited for; matrix products, arithmetic and copies ran while one was open for 1% of the time, Pallas kernels for 6%

profile of v6, /device:TPU:1, one launch (start us, length us, event | category | flops | bytes accessed | tf_op | source)
XLA Modules:
  0.0 195.5 jit_solution(18036250505015916055)
XLA Ops:
  0.6 4.2 %shard_map.179 = (bf16[4,272,512]{2,1,0:T(8,128)(2,1)}, f32[128,128]{1,0:T(8,128)}, f32[128,128]{1,0:T(8,128)}, f32[8,128]{1,0:T(8,128)}) custom-call(f32[32,128]{1,0:T(8,128)} %bitcast.33, s32[1,32]{1,0:T(1,128)} %bitcast.35, f32[8,32]{1,0:T(8,128)} %bitcast.34, bf16[128,2048]{1,0:T(8,128)(2,1)} %bitcast.19, bf16[128,2048]{1,0:T(8,128)(2,1)} %bitcast.22, ...), custom_call_target="tpu_custom_call" | custom-call | flops 134217728 | bytes 2380928 | tf_op jit(solution)/shard_map/pallas_call | solution.py:371
  4.8 6.6 %all-to-all-start = ((bf16[4,272,512]{2,1,0:T(8,128)(2,1)}), bf16[4,272,512]{2,1,0:T(8,128)(2,1)S(1)}, u32[]{:S(2)}, u32[]{:S(2)}) async-start(bf16[4,272,512]{2,1,0:T(8,128)(2,1)} %get-tuple-element.54), calls=%async_computation | async-start | bytes 2228224 | tf_op jit(solution)/shard_map/all_to_all | solution.py:400
  12.3 5.9 %collective-permute-start = (bf16[4,256,128]{2,1,0:T(8,128)(2,1)S(1)}, bf16[4,256,128]{2,1,0:T(8,128)(2,1)S(1)}, u32[]{:S(2)}, u32[]{:S(2)}) collective-permute-start(bf16[4,256,128]{2,1,0:T(8,128)(2,1)S(1)} %get-tuple-element.57), channel_id=1, source_target_pairs={{0,1},{1,0},{2,3},{3,2},{4,5},{5,4},{6,7},{7,6},{8,9},{9,8},{10,11... | collective-permute-start | bytes 786440 | tf_op jit(solution)/shard_map/ppermute | solution.py:405
  21.3 2.5 %collective-permute-start.2 = (bf16[2,256,128]{2,1,0:T(8,128)(2,1)S(1)}, bf16[2,256,128]{2,1,0:T(8,128)(2,1)S(1)}, u32[]{:S(2)}, u32[]{:S(2)}) collective-permute-start(bf16[2,256,128]{2,1,0:T(8,128)(2,1)S(1)} %get-tuple-element.60), channel_id=1, source_target_pairs={{0,4},{1,5},{2,6},{3,7},{4,0},{5,1},{6,2},{7,3},{8,12},{9,13},{10,... | collective-permute-start | bytes 393224 | tf_op jit(solution)/shard_map/ppermute | solution.py:405
  23.9 5.1 %collective-permute-start.3 = (bf16[2,256,128]{2,1,0:T(8,128)(2,1)S(1)}, bf16[2,256,128]{2,1,0:T(8,128)(2,1)S(1)}, u32[]{:S(2)}, u32[]{:S(2)}) collective-permute-start(bf16[2,256,128]{2,1,0:T(8,128)(2,1)S(1)} %get-tuple-element.61), channel_id=1, source_target_pairs={{0,6},{1,7},{2,4},{3,5},{4,2},{5,3},{6,0},{7,1},{8,14},{9,15},{10,... | collective-permute-start | bytes 393224 | tf_op jit(solution)/shard_map/ppermute | solution.py:405
  29.4 2.5 %collective-permute-done.3.refs_3_ = bf16[2,256,128]{2,1,0:T(8,128)(2,1)S(1)} collective-permute-done((bf16[2,256,128]{2,1,0:T(8,128)(2,1)S(1)}, bf16[2,256,128]{2,1,0:T(8,128)(2,1)S(1)}, u32[]{:S(2)}, u32[]{:S(2)}) %collective-permute-start.3) | collective-permute-done | bytes 131104 | tf_op jit(solution)/shard_map/ppermute | solution.py:405
  31.9 5.7 %all-to-all-done.refs_1_ = bf16[4,272,512]{2,1,0:T(8,128)(2,1)S(1)} async-done(((bf16[4,272,512]{2,1,0:T(8,128)(2,1)}), bf16[4,272,512]{2,1,0:T(8,128)(2,1)S(1)}, u32[]{:S(2)}, u32[]{:S(2)}) %all-to-all-start) | async-done | bytes 1114144 | tf_op jit(solution)/shard_map/all_to_all | solution.py:400
  38.5 9.2 %collective-permute-start.4 = (bf16[144,512]{1,0:T(8,128)(2,1)S(1)}, bf16[144,512]{1,0:T(8,128)(2,1)S(1)}, u32[]{:S(2)}, u32[]{:S(2)}) collective-permute-start(bf16[144,512]{1,0:T(8,128)(2,1)S(1)} %get-tuple-element.63), channel_id=1, source_target_pairs={{0,128},{32,160},{64,192},{96,224},{128,256},{160,288},{192,320},{... | collective-permute-start | bytes 442376 | tf_op jit(solution)/shard_map/ppermute | solution.py:392
  47.7 3.5 %collective-permute-start.5 = (bf16[144,512]{1,0:T(8,128)(2,1)S(1)}, bf16[144,512]{1,0:T(8,128)(2,1)S(1)}, u32[]{:S(2)}, u32[]{:S(2)}) collective-permute-start(bf16[144,512]{1,0:T(8,128)(2,1)S(1)} %get-tuple-element.64), channel_id=1, source_target_pairs={{0,384},{32,416},{64,448},{96,480},{128,0},{160,32},{192,64},{224,... | collective-permute-start | bytes 442376 | tf_op jit(solution)/shard_map/ppermute | solution.py:392
  52.9 12.6 %collective-permute-done.5.refs_3_ = bf16[144,512]{1,0:T(8,128)(2,1)S(1)} collective-permute-done((bf16[144,512]{1,0:T(8,128)(2,1)S(1)}, bf16[144,512]{1,0:T(8,128)(2,1)S(1)}, u32[]{:S(2)}, u32[]{:S(2)}) %collective-permute-start.5) | collective-permute-done | bytes 147488 | tf_op jit(solution)/shard_map/ppermute | solution.py:392
  66.8 6.2 %shard_map.183 = (f32[128,2048]{1,0:T(8,128)}, bf16[128,2048]{1,0:T(8,128)(2,1)}, bf16[128,2048]{1,0:T(8,128)(2,1)}, f32[128,128]{1,0:T(8,128)S(1)}, f32[128,128]{1,0:T(8,128)}, /*index=5*/f32[128,128]{1,0:T(8,128)}) custom-call(f32[128,128]{1,0:T(8,128)S(1)} %copy-done.11, bf16[128,2048]{1,0:T(8,128)(2,1)S(1)} %bitcast.20, bf16[128,2048]{1,0:T(8,128)(2,1)S(1)} %bitcast.23, ...), custom_call_target="tpu_custom_call" | custom-call | flops 671088640 | bytes 3473536 | tf_op jit(solution)/shard_map/pallas_call | solution.py:371
  73.0 6.6 %collective-permute-done.7.refs_5_ = bf16[144,512]{1,0:T(8,128)(2,1)S(1)} collective-permute-done((bf16[144,512]{1,0:T(8,128)(2,1)S(1)}, bf16[144,512]{1,0:T(8,128)(2,1)S(1)}, u32[]{:S(2)}, u32[]{:S(2)}) %collective-permute-start.7) | collective-permute-done | bytes 147488 | tf_op jit(solution)/shard_map/ppermute | solution.py:392
  81.7 5.7 %all-to-all-start.1 = ((bf16[4,256,512]{2,1,0:T(8,128)(2,1)}), bf16[4,256,512]{2,1,0:T(8,128)(2,1)S(1)}, u32[]{:S(2)}, u32[]{:S(2)}) async-start(bf16[4,256,512]{2,1,0:T(8,128)(2,1)} %shard_map.184), calls=%async_computation.1 | async-start | bytes 2097152 | tf_op jit(solution)/shard_map/all_to_all | solution.py:400
  87.4 4.7 %collective-permute-start.9 = (bf16[8,256,128]{2,1,0:T(8,128)(2,1)S(1)}, bf16[8,256,128]{2,1,0:T(8,128)(2,1)S(1)}, u32[]{:S(2)}, u32[]{:S(2)}) collective-permute-start(bf16[8,256,128]{2,1,0:T(8,128)(2,1)S(1)} %shard_map.187.refs_2_), channel_id=1, source_target_pairs={{0,24},{8,16},{16,8},{24,0},{1,25},{9,17},{17,9},{25,1},{2,26},{10... | collective-permute-start | bytes 1572872 | tf_op jit(solution)/shard_map/ppermute | solution.py:405
  94.1 9.0 %collective-permute-done.9.refs_4_ = bf16[8,256,128]{2,1,0:T(8,128)(2,1)S(1)} collective-permute-done((bf16[8,256,128]{2,1,0:T(8,128)(2,1)S(1)}, bf16[8,256,128]{2,1,0:T(8,128)(2,1)S(1)}, u32[]{:S(2)}, u32[]{:S(2)}) %collective-permute-start.9) | collective-permute-done | bytes 524320 | tf_op jit(solution)/shard_map/ppermute | solution.py:405
  107.0 4.1 %collective-permute-start.11 = (bf16[4,256,128]{2,1,0:T(8,128)(2,1)}, bf16[4,256,128]{2,1,0:T(8,128)(2,1)}, u32[]{:S(2)}, u32[]{:S(2)}) collective-permute-start(bf16[4,256,128]{2,1,0:T(8,128)(2,1)} %slice.9), channel_id=1, source_target_pairs={{0,24},{8,16},{16,8},{24,0},{1,25},{9,17},{17,9},{25,1},{2,26},{10... | collective-permute-start | bytes 786440 | tf_op jit(solution)/shard_map/ppermute | solution.py:405
  115.3 6.2 %all-to-all-start.2 = ((bf16[8,128,128]{2,1,0:T(8,128)(2,1)}), bf16[8,128,128]{2,1,0:T(8,128)(2,1)S(1)}, u32[]{:S(2)}, u32[]{:S(2)}) async-start(bf16[8,128,128]{2,1,0:T(8,128)(2,1)} %get-tuple-element.85), calls=%async_computation.2 | async-start | bytes 524288 | tf_op jit(solution)/shard_map/all_to_all | solution.py:400
  121.6 6.5 %all-to-all-done.2.refs_1_ = bf16[8,128,128]{2,1,0:T(8,128)(2,1)S(1)} async-done(((bf16[8,128,128]{2,1,0:T(8,128)(2,1)}), bf16[8,128,128]{2,1,0:T(8,128)(2,1)S(1)}, u32[]{:S(2)}, u32[]{:S(2)}) %all-to-all-start.2) | async-done | bytes 262176 | tf_op jit(solution)/shard_map/all_to_all | solution.py:400
  129.1 2.5 %shard_map.188 = bf16[16,64,128]{2,1,0:T(8,128)(2,1)} custom-call(s32[3]{0:T(128)S(1)} %pad_add_fusion.refs_0_, bf16[8,128,128]{2,1,0:T(8,128)(2,1)S(1)} %all-to-all-done.2.refs_1_, bf16[8,256,128]{2,1,0:T(8,128)(2,1)S(1)} %shard_map.187.refs_2_, bf16[8,256,128]{2,1,0:T(8,128)(2,1)S(1)} %copy-done.3, ...), custom_call_target="tpu_custom_call" | custom-call | flops 268435456 | bytes 2621452 | tf_op jit(solution)/shard_map/pallas_call | solution.py:371
  131.6 9.6 %all-to-all-start.3 = ((bf16[16,64,128]{2,1,0:T(8,128)(2,1)}), bf16[16,64,128]{2,1,0:T(8,128)(2,1)S(1)}, u32[]{:S(2)}, u32[]{:S(2)}) async-start(bf16[16,64,128]{2,1,0:T(8,128)(2,1)} %shard_map.188), calls=%async_computation.3 | async-start | bytes 524288 | tf_op jit(solution)/shard_map/all_to_all | solution.py:400
  145.9 3.9 %shard_map.185 = (bf16[128,2048]{1,0:T(8,128)(2,1)}, bf16[128,128]{1,0:T(8,128)(2,1)}, f32[8,128]{1,0:T(8,128)S(1)}) custom-call(bf16[4,256,512]{2,1,0:T(8,128)(2,1)S(1)} %all-to-all-done.1.refs_0_.refs_2_, bf16[128,2048]{1,0:T(8,128)(2,1)S(1)} %bitcast.21, bf16[128,2048]{1,0:T(8,128)(2,1)S(1)} %bitcast.24, bf16[128,2048]{1,0:T(8,128)(2,1)S(1)} %copy-done.5, ...), custom_call_target="tpu_custom_call" | custom-call | flops 201326592 | bytes 4562944 | tf_op jit(solution)/shard_map/pallas_call | solution.py:371
  149.9 4.2 %all-to-all-done.3.refs_0_ = bf16[16,64,128]{2,1,0:T(8,128)(2,1)S(1)} async-done(((bf16[16,64,128]{2,1,0:T(8,128)(2,1)}), bf16[16,64,128]{2,1,0:T(8,128)(2,1)S(1)}, u32[]{:S(2)}, u32[]{:S(2)}) %all-to-all-start.3) | async-done | bytes 262176 | tf_op jit(solution)/shard_map/all_to_all | solution.py:400
  154.2 19.9 %all_to_all.30.refs_0_ = f32[32,8,128]{2,1,0:T(8,128)S(1)} all-to-all(f32[32,8,128]{2,1,0:T(8,128)S(1)} %get-tuple-element.91), channel_id=1, replica_groups=mesh['far'=4,'near'=4,'tensor'=4,'dp'=8] {'near','dp'}, dimensions={0} | all-to-all | bytes 262144 | tf_op jit(solution)/shard_map/all_to_all | solution.py:400
  174.2 19.9 %all_to_all.31.refs_1_ = f32[16,8,128]{2,1,0:T(8,128)S(1)} all-to-all(f32[16,8,128]{2,1,0:T(8,128)S(1)} %shard_map.190), channel_id=1, replica_groups=mesh['far'=4,'near'=4,'tensor'=4,'dp'=8] {'far','tensor'}, dimensions={0} | all-to-all | bytes 131072 | tf_op jit(solution)/shard_map/all_to_all | solution.py:400
  (66 shorter events, 27.7 us)
Async XLA Ops:
  4.8 32.8 %all-to-all-start = ((bf16[4,272,512]{2,1,0:T(8,128)(2,1)}), bf16[4,272,512]{2,1,0:T(8,128)(2,1)S(1)}, u32[]{:S(2)}, u32[]{:S(2)}) async-start(bf16[4,272,512]{2,1,0:T(8,128)(2,1)} %get-tuple-element.54), calls=%async_computation | async-start | bytes 2228224 | tf_op jit(solution)/shard_map/all_to_all | solution.py:400
  11.4 55.3 %copy-start = (bf16[1,128,2048]{2,1,0:T(8,128)(2,1)S(1)}, bf16[1,128,2048]{2,1,0:T(8,128)(2,1)}, u32[]{:S(2)}) copy-start(bf16[1,128,2048]{2,1,0:T(8,128)(2,1)} %param.12) | copy-start | bytes 1572868
  11.4 55.3 %copy-start.1 = (bf16[1,128,2048]{2,1,0:T(8,128)(2,1)S(1)}, bf16[1,128,2048]{2,1,0:T(8,128)(2,1)}, u32[]{:S(2)}) copy-start(bf16[1,128,2048]{2,1,0:T(8,128)(2,1)} %param.19) | copy-start | bytes 1572868
  11.4 55.3 %copy-start.8 = (bf16[1,128,128]{2,1,0:T(8,128)(2,1)S(1)}, bf16[1,128,128]{2,1,0:T(8,128)(2,1)}, u32[]{:S(2)}) copy-start(bf16[1,128,128]{2,1,0:T(8,128)(2,1)} %param.13) | copy-start | bytes 98308
  11.4 55.3 %copy-start.9 = (bf16[1,128,128]{2,1,0:T(8,128)(2,1)S(1)}, bf16[1,128,128]{2,1,0:T(8,128)(2,1)}, u32[]{:S(2)}) copy-start(bf16[1,128,128]{2,1,0:T(8,128)(2,1)} %param.14) | copy-start | bytes 98308
  11.4 55.3 %copy-start.11 = (f32[128,128]{1,0:T(8,128)S(1)}, f32[128,128]{1,0:T(8,128)}, u32[]{:S(2)}) copy-start(f32[128,128]{1,0:T(8,128)} %get-tuple-element.65.refs_0_.refs_4_) | copy-start | bytes 196612
  11.4 55.3 %copy-start.19 = (f32[32]{0:T(128)S(1)}, f32[32]{0:T(128)}, u32[]{:S(2)}) copy-start(f32[32]{0:T(128)} %param.18) | copy-start | bytes 388
  12.3 7.0 %collective-permute-start = (bf16[4,256,128]{2,1,0:T(8,128)(2,1)S(1)}, bf16[4,256,128]{2,1,0:T(8,128)(2,1)S(1)}, u32[]{:S(2)}, u32[]{:S(2)}) collective-permute-start(bf16[4,256,128]{2,1,0:T(8,128)(2,1)S(1)} %get-tuple-element.57), channel_id=1, source_target_pairs={{0,1},{1,0},{2,3},{3,2},{4,5},{5,4},{6,7},{7,6},{8,9},{9,8},{10,11... | collective-permute-start | bytes 786440 | tf_op jit(solution)/shard_map/ppermute | solution.py:405
  19.4 9.6 %collective-permute-start.1 = (bf16[2,256,128]{2,1,0:T(8,128)(2,1)S(1)}, bf16[2,256,128]{2,1,0:T(8,128)(2,1)S(1)}, u32[]{:S(2)}, u32[]{:S(2)}) collective-permute-start(bf16[2,256,128]{2,1,0:T(8,128)(2,1)S(1)} %get-tuple-element.59), channel_id=1, source_target_pairs={{0,2},{1,3},{2,0},{3,1},{4,6},{5,7},{6,4},{7,5},{8,10},{9,11},{10,... | collective-permute-start | bytes 393224 | tf_op jit(solution)/shard_map/ppermute | solution.py:405
  21.3 8.1 %collective-permute-start.2 = (bf16[2,256,128]{2,1,0:T(8,128)(2,1)S(1)}, bf16[2,256,128]{2,1,0:T(8,128)(2,1)S(1)}, u32[]{:S(2)}, u32[]{:S(2)}) collective-permute-start(bf16[2,256,128]{2,1,0:T(8,128)(2,1)S(1)} %get-tuple-element.60), channel_id=1, source_target_pairs={{0,4},{1,5},{2,6},{3,7},{4,0},{5,1},{6,2},{7,3},{8,12},{9,13},{10,... | collective-permute-start | bytes 393224 | tf_op jit(solution)/shard_map/ppermute | solution.py:405
  23.9 8.1 %collective-permute-start.3 = (bf16[2,256,128]{2,1,0:T(8,128)(2,1)S(1)}, bf16[2,256,128]{2,1,0:T(8,128)(2,1)S(1)}, u32[]{:S(2)}, u32[]{:S(2)}) collective-permute-start(bf16[2,256,128]{2,1,0:T(8,128)(2,1)S(1)} %get-tuple-element.61), channel_id=1, source_target_pairs={{0,6},{1,7},{2,4},{3,5},{4,2},{5,3},{6,0},{7,1},{8,14},{9,15},{10,... | collective-permute-start | bytes 393224 | tf_op jit(solution)/shard_map/ppermute | solution.py:405
  38.5 13.8 %collective-permute-start.4 = (bf16[144,512]{1,0:T(8,128)(2,1)S(1)}, bf16[144,512]{1,0:T(8,128)(2,1)S(1)}, u32[]{:S(2)}, u32[]{:S(2)}) collective-permute-start(bf16[144,512]{1,0:T(8,128)(2,1)S(1)} %get-tuple-element.63), channel_id=1, source_target_pairs={{0,128},{32,160},{64,192},{96,224},{128,256},{160,288},{192,320},{... | collective-permute-start | bytes 442376 | tf_op jit(solution)/shard_map/ppermute | solution.py:392
  47.7 17.7 %collective-permute-start.5 = (bf16[144,512]{1,0:T(8,128)(2,1)S(1)}, bf16[144,512]{1,0:T(8,128)(2,1)S(1)}, u32[]{:S(2)}, u32[]{:S(2)}) collective-permute-start(bf16[144,512]{1,0:T(8,128)(2,1)S(1)} %get-tuple-element.64), channel_id=1, source_target_pairs={{0,384},{32,416},{64,448},{96,480},{128,0},{160,32},{192,64},{224,... | collective-permute-start | bytes 442376 | tf_op jit(solution)/shard_map/ppermute | solution.py:392
  52.2 20.7 %collective-permute-start.6 = (bf16[144,512]{1,0:T(8,128)(2,1)S(1)}, bf16[144,512]{1,0:T(8,128)(2,1)S(1)}, u32[]{:S(2)}, u32[]{:S(2)}) collective-permute-start(bf16[144,512]{1,0:T(8,128)(2,1)S(1)} %collective-permute-done.4.refs_2_), channel_id=1, source_target_pairs={{128,256},{160,288},{192,320},{224,352},{256,384},{288,416},{320,4... | collective-permute-start | bytes 442376 | tf_op jit(solution)/shard_map/ppermute | solution.py:392
  65.4 14.2 %collective-permute-start.7 = (bf16[144,512]{1,0:T(8,128)(2,1)S(1)}, bf16[144,512]{1,0:T(8,128)(2,1)S(1)}, u32[]{:S(2)}, u32[]{:S(2)}) collective-permute-start(bf16[144,512]{1,0:T(8,128)(2,1)S(1)} %collective-permute-done.5.refs_3_), channel_id=1, source_target_pairs={{128,0},{160,32},{192,64},{224,96},{256,128},{288,160},{320,192},{... | collective-permute-start | bytes 442376 | tf_op jit(solution)/shard_map/ppermute | solution.py:392
  81.7 31.0 %all-to-all-start.1 = ((bf16[4,256,512]{2,1,0:T(8,128)(2,1)}), bf16[4,256,512]{2,1,0:T(8,128)(2,1)S(1)}, u32[]{:S(2)}, u32[]{:S(2)}) async-start(bf16[4,256,512]{2,1,0:T(8,128)(2,1)} %shard_map.184), calls=%async_computation.1 | async-start | bytes 2097152 | tf_op jit(solution)/shard_map/all_to_all | solution.py:400
  87.4 15.7 %collective-permute-start.9 = (bf16[8,256,128]{2,1,0:T(8,128)(2,1)S(1)}, bf16[8,256,128]{2,1,0:T(8,128)(2,1)S(1)}, u32[]{:S(2)}, u32[]{:S(2)}) collective-permute-start(bf16[8,256,128]{2,1,0:T(8,128)(2,1)S(1)} %shard_map.187.refs_2_), channel_id=1, source_target_pairs={{0,24},{8,16},{16,8},{24,0},{1,25},{9,17},{17,9},{25,1},{2,26},{10... | collective-permute-start | bytes 1572872 | tf_op jit(solution)/shard_map/ppermute | solution.py:405
  92.2 14.0 %collective-permute-start.8 = (bf16[8,256,128]{2,1,0:T(8,128)(2,1)S(1)}, bf16[8,256,128]{2,1,0:T(8,128)(2,1)S(1)}, u32[]{:S(2)}, u32[]{:S(2)}) collective-permute-start(bf16[8,256,128]{2,1,0:T(8,128)(2,1)S(1)} %shard_map.187.refs_2_), channel_id=1, source_target_pairs={{0,8},{8,0},{16,24},{24,16},{1,9},{9,1},{17,25},{25,17},{2,10},{10... | collective-permute-start | bytes 1572872 | tf_op jit(solution)/shard_map/ppermute | solution.py:405
  103.8 17.7 %collective-permute-start.10 = (bf16[4,256,128]{2,1,0:T(8,128)(2,1)}, bf16[4,256,128]{2,1,0:T(8,128)(2,1)}, u32[]{:S(2)}, u32[]{:S(2)}) collective-permute-start(bf16[4,256,128]{2,1,0:T(8,128)(2,1)} %slice.8), channel_id=1, source_target_pairs={{0,8},{8,0},{16,24},{24,16},{1,9},{9,1},{17,25},{25,17},{2,10},{10... | collective-permute-start | bytes 786440 | tf_op jit(solution)/shard_map/ppermute | solution.py:405
  107.0 14.5 %collective-permute-start.11 = (bf16[4,256,128]{2,1,0:T(8,128)(2,1)}, bf16[4,256,128]{2,1,0:T(8,128)(2,1)}, u32[]{:S(2)}, u32[]{:S(2)}) collective-permute-start(bf16[4,256,128]{2,1,0:T(8,128)(2,1)} %slice.9), channel_id=1, source_target_pairs={{0,24},{8,16},{16,8},{24,0},{1,25},{9,17},{17,9},{25,1},{2,26},{10... | collective-permute-start | bytes 786440 | tf_op jit(solution)/shard_map/ppermute | solution.py:405
  115.3 12.7 %all-to-all-start.2 = ((bf16[8,128,128]{2,1,0:T(8,128)(2,1)}), bf16[8,128,128]{2,1,0:T(8,128)(2,1)S(1)}, u32[]{:S(2)}, u32[]{:S(2)}) async-start(bf16[8,128,128]{2,1,0:T(8,128)(2,1)} %get-tuple-element.85), calls=%async_computation.2 | async-start | bytes 524288 | tf_op jit(solution)/shard_map/all_to_all | solution.py:400
  131.6 22.5 %all-to-all-start.3 = ((bf16[16,64,128]{2,1,0:T(8,128)(2,1)}), bf16[16,64,128]{2,1,0:T(8,128)(2,1)S(1)}, u32[]{:S(2)}, u32[]{:S(2)}) async-start(bf16[16,64,128]{2,1,0:T(8,128)(2,1)} %shard_map.188), calls=%async_computation.3 | async-start | bytes 524288 | tf_op jit(solution)/shard_map/all_to_all | solution.py:400
  145.9 48.2 %copy-start.16 = (f32[64,128]{1,0:T(8,128)S(1)}, f32[64,128]{1,0:T(8,128)}, u32[]{:S(2)}) copy-start(f32[64,128]{1,0:T(8,128)} %refs_4_.1) | copy-start | bytes 98308
  145.9 48.2 %copy-start.17 = (f32[64,128]{1,0:T(8,128)S(1)}, f32[64,128]{1,0:T(8,128)}, u32[]{:S(2)}) copy-start(f32[64,128]{1,0:T(8,128)} %refs_5_.1) | copy-start | bytes 98308
  (12 other events, 114.3 us)

commit v7 on v4

--- a/solution.py
+++ b/solution.py
@@ -14,6 +14,7 @@
 PAIR = 2 * P_SIZE
 LOG_ROWS = 16
 GROUP = 4
+PARTS = 2
 
 beta_one = 0.9
 beta_two = 0.95
@@ -97,7 +98,12 @@
         st[piece, 2 * N :, spot] = log_rows(spread(last, j, first))
 
 
-def group_kernel(me, got, up, down):
+def place(at, ref):
+    width = ref.shape[1]
+    return at // width, slice(at % width, at % width + PAIR)
+
+
+def group_kernel(me, got, *outs):
     here = me[0] // GROUP
     count = got.shape[0]
     for at in range(0, got.shape[2], PAIR):
@@ -110,18 +116,26 @@
         for k in reversed(range(count)):
             back = decay[k] * back + got[k, N : 2 * N, lanes].astype(f32)
         rows = log_rows(sum(logs[1:], logs[0]))
-        up[:N, lanes] = jnp.where(here < 3, ahead, back).astype(bf16)
-        up[N:, lanes] = rows
-        down[:N, lanes] = jnp.where(here > 0, back, ahead).astype(bf16)
-        down[N:, lanes] = rows
-
-
-def scan_kernel(me, got, up, down, up_two, down_two, out):
+        part, spot = place(at, outs[0])
+        up, down = outs[part], outs[PARTS + part]
+        up[:N, spot] = jnp.where(here < 3, ahead, back).astype(bf16)
+        up[N:, spot] = rows
+        down[:N, spot] = jnp.where(here > 0, back, ahead).astype(bf16)
+        down[N:, spot] = rows
+
+
+def scan_kernel(me, got, *refs):
+    moved, out = refs[:-1], refs[-1]
+    up, down, up_two, down_two = (moved[k : k + PARTS] for k in range(0, 4 * PARTS, PARTS))
     here = me[0] // GROUP
     count = got.shape[0]
 
-    def pick(options, lanes):
-        parts = [(k, ref[:N, lanes].astype(f32), row_logs(ref[N:, lanes])) for k, ref in options]
+    def pick(options, at):
+        at_part, spot = place(at, moved[0])
+        parts = [
+            (k, refs[at_part][:N, spot].astype(f32), row_logs(refs[at_part][N:, spot]))
+            for k, refs in options
+        ]
         _, part, log = parts[0]
         for k, other, other_log in parts[1:]:
             part = jnp.where(here == k, other, part)
@@ -135,10 +149,10 @@
         decay = [jnp.exp(row_logs(got[k, 2 * N :, lanes])) for k in range(count)]
         state = back = jnp.zeros((N, PAIR), f32)
         for k, options in enumerate(before):
-            part, fade = pick(options, lanes)
+            part, fade = pick(options, at)
             state = jnp.where(k < here, fade * state + part, state)
         for k, options in enumerate(after):
-            part, fade = pick(options, lanes)
+            part, fade = pick(options, at)
             back = jnp.where(3 - k > here, fade * back + part, back)
         for k in range(count):
             out[k, :N, lanes] = state.astype(bf16)
@@ -438,16 +452,19 @@
         scratch=[pltpu.VMEM((SPAN, SPAN), f32)],
         flops=20 * SPAN * SPAN * width,
     )
-    up, down = call(
+    sent = call(
         group_kernel,
-        [shaped((N + LOG_ROWS, piece), bf16)] * 2,
+        [shaped((N + LOG_ROWS, piece // PARTS), bf16)] * (2 * PARTS),
         me,
         got,
         flops=8 * N * width,
     )
-    up, down = shift(up, range(seqs), GROUP), shift(down, range(seqs), -GROUP)
+    up, down = sent[:PARTS], sent[PARTS:]
     inner = range(GROUP, seqs - GROUP)
-    up_two, down_two = shift(up, inner, GROUP), shift(down, inner, -GROUP)
+    up = [shift(a, range(seqs), GROUP) for a in up]
+    down = [shift(a, range(seqs), -GROUP) for a in down]
+    up_two = [shift(a, inner, GROUP) for a in up]
+    down_two = [shift(a, inner, -GROUP) for a in down]
     up_two, down_two, dye = lax.optimization_barrier((up_two, down_two, dye))
     plan = ((0, ((0, 0),)), (1, ((1, 0),)), (3, ((2, 0),)), (2, ((3, 0), (4, half))))
     states = call(
@@ -455,10 +472,10 @@
         [shaped((GROUP, 2 * N, piece), bf16)],
         me,
         got,
-        up,
-        down,
-        up_two,
-        down_two,
+        *up,
+        *down,
+        *up_two,
+        *down_two,
         flops=8 * N * width,
     )
     states, *pairs = lax.optimization_barrier((states, *pairs))

time: 193 us -> 199 us (1.031)
  starting transfers between devices: 70.9 us -> 78.8 us
    ppermute x4 -> x8, starting transfers between devices: 14.6 us -> 25.8 us  [shift(): return lax.ppermute(a, 'seq', [(i, (i + step) % count) for i in senders])]
    all_to_all x4, starting transfers between devices: 28.1 us -> 24.9 us  [swap(): return lax.all_to_all(a, axis, 0, 0, tiled=True, axis_index_groups=groups)]
    ppermute x4 -> x8, waiting for transfers between devices: 17.7 us -> 15.9 us  [shift(): return lax.ppermute(a, 'seq', [(i, (i + step) % count) for i in senders])]
    unnamed x52 -> x56, local copies, waits for them, and re-layouts: 11.5 us -> 11.7 us
  transfers between devices with their start and end apart: 16 -> 20, of which waited for: 12 -> 14; matrix products, arithmetic and copies ran while one was open for 1% -> 1% of each run, Pallas kernels for 6% -> 5%
where the time goes in v7:
time: 199 us; the launch traced here: 198 us
  starting transfers between devices  78.8 us (40%)
  waiting for transfers between devices  47.3 us (24%)
  blocking collectives  35.9 us (18%)
  Pallas kernels  21.7 us (11%)
  local copies, waits for them, and re-layouts  13.2 us (7%)
    all_to_all x2, blocking collectives, swap(): return lax.all_to_all(a, axis, 0, 0, tiled=True, axis_index_groups=groups)  35.9 us
    ppermute x8, starting transfers between devices, trade(): return lax.ppermute(a, axis, [(i, i ^ k) for i in range(count)])  28.1 us
    ppermute x8, starting transfers between devices, shift(): return lax.ppermute(a, 'seq', [(i, (i + step) % count) for i in senders])  25.8 us
    all_to_all x4, starting transfers between devices, swap(): return lax.all_to_all(a, axis, 0, 0, tiled=True, axis_index_groups=groups)  24.9 us
    pallas_call x13, Pallas kernels, call(): pl.pallas_call(kernel, out_shape=tuple(out_shapes), in_specs=[scalars if...  21.7 us
    all_to_all x4, waiting for transfers between devices, swap(): return lax.all_to_all(a, axis, 0, 0, tiled=True, axis_index_groups=groups)  17.3 us
    ppermute x8, waiting for transfers between devices, shift(): return lax.ppermute(a, 'seq', [(i, (i + step) % count) for i in senders])  15.9 us
    ppermute x8, waiting for transfers between devices, trade(): return lax.ppermute(a, axis, [(i, i ^ k) for i in range(count)])  14.1 us
  transfers between devices with their start and end apart: 20, of which 14 were waited for; matrix products, arithmetic and copies ran while one was open for 1% of the time, Pallas kernels for 5%

profile of v7, /device:TPU:1, one launch (start us, length us, event | category | flops | bytes accessed | tf_op | source)
XLA Modules:
  0.0 198.0 jit_solution(16388284139016209796)
XLA Ops:
  0.6 4.2 %shard_map.179 = (bf16[4,272,512]{2,1,0:T(8,128)(2,1)}, f32[128,128]{1,0:T(8,128)}, f32[128,128]{1,0:T(8,128)}, f32[8,128]{1,0:T(8,128)}) custom-call(f32[32,128]{1,0:T(8,128)} %bitcast.33, s32[1,32]{1,0:T(1,128)} %bitcast.35, f32[8,32]{1,0:T(8,128)} %bitcast.34, bf16[128,2048]{1,0:T(8,128)(2,1)} %bitcast.19, bf16[128,2048]{1,0:T(8,128)(2,1)} %bitcast.22, ...), custom_call_target="tpu_custom_call" | custom-call | flops 134217728 | bytes 2380928 | tf_op jit(solution)/shard_map/pallas_call | solution.py:357
  4.9 6.6 %all-to-all-start = ((bf16[4,272,512]{2,1,0:T(8,128)(2,1)}), bf16[4,272,512]{2,1,0:T(8,128)(2,1)S(1)}, u32[]{:S(2)}, u32[]{:S(2)}) async-start(bf16[4,272,512]{2,1,0:T(8,128)(2,1)} %get-tuple-element.58), calls=%async_computation | async-start | bytes 2228224 | tf_op jit(solution)/shard_map/all_to_all | solution.py:378
  12.4 5.9 %collective-permute-start = (bf16[4,256,128]{2,1,0:T(8,128)(2,1)S(1)}, bf16[4,256,128]{2,1,0:T(8,128)(2,1)S(1)}, u32[]{:S(2)}, u32[]{:S(2)}) collective-permute-start(bf16[4,256,128]{2,1,0:T(8,128)(2,1)S(1)} %get-tuple-element.61), channel_id=1, source_target_pairs={{0,1},{1,0},{2,3},{3,2},{4,5},{5,4},{6,7},{7,6},{8,9},{9,8},{10,11... | collective-permute-start | bytes 786440 | tf_op jit(solution)/shard_map/ppermute | solution.py:383
  21.4 2.5 %collective-permute-start.2 = (bf16[2,256,128]{2,1,0:T(8,128)(2,1)S(1)}, bf16[2,256,128]{2,1,0:T(8,128)(2,1)S(1)}, u32[]{:S(2)}, u32[]{:S(2)}) collective-permute-start(bf16[2,256,128]{2,1,0:T(8,128)(2,1)S(1)} %get-tuple-element.64), channel_id=1, source_target_pairs={{0,4},{1,5},{2,6},{3,7},{4,0},{5,1},{6,2},{7,3},{8,12},{9,13},{10,... | collective-permute-start | bytes 393224 | tf_op jit(solution)/shard_map/ppermute | solution.py:383
  23.9 5.1 %collective-permute-start.3 = (bf16[2,256,128]{2,1,0:T(8,128)(2,1)S(1)}, bf16[2,256,128]{2,1,0:T(8,128)(2,1)S(1)}, u32[]{:S(2)}, u32[]{:S(2)}) collective-permute-start(bf16[2,256,128]{2,1,0:T(8,128)(2,1)S(1)} %get-tuple-element.65), channel_id=1, source_target_pairs={{0,6},{1,7},{2,4},{3,5},{4,2},{5,3},{6,0},{7,1},{8,14},{9,15},{10,... | collective-permute-start | bytes 393224 | tf_op jit(solution)/shard_map/ppermute | solution.py:383
  29.5 2.5 %collective-permute-done.3.refs_3_ = bf16[2,256,128]{2,1,0:T(8,128)(2,1)S(1)} collective-permute-done((bf16[2,256,128]{2,1,0:T(8,128)(2,1)S(1)}, bf16[2,256,128]{2,1,0:T(8,128)(2,1)S(1)}, u32[]{:S(2)}, u32[]{:S(2)}) %collective-permute-start.3) | collective-permute-done | bytes 131104 | tf_op jit(solution)/shard_map/ppermute | solution.py:383
  32.0 5.7 %all-to-all-done.got = bf16[4,272,512]{2,1,0:T(8,128)(2,1)S(1)} async-done(((bf16[4,272,512]{2,1,0:T(8,128)(2,1)}), bf16[4,272,512]{2,1,0:T(8,128)(2,1)S(1)}, u32[]{:S(2)}, u32[]{:S(2)}) %all-to-all-start) | async-done | bytes 1114144 | tf_op jit(solution)/shard_map/all_to_all | solution.py:378
  38.5 9.2 %collective-permute-start.4 = (bf16[144,256]{1,0:T(8,128)(2,1)S(1)}, bf16[144,256]{1,0:T(8,128)(2,1)S(1)}, u32[]{:S(2)}, u32[]{:S(2)}) collective-permute-start(bf16[144,256]{1,0:T(8,128)(2,1)S(1)} %get-tuple-element.67), channel_id=1, source_target_pairs={{0,128},{32,160},{64,192},{96,224},{128,256},{160,288},{192,320},{... | collective-permute-start | bytes 221192 | tf_op jit(solution)/shard_map/ppermute | solution.py:370
  47.7 6.7 %collective-permute-start.5 = (bf16[144,256]{1,0:T(8,128)(2,1)S(1)}, bf16[144,256]{1,0:T(8,128)(2,1)S(1)}, u32[]{:S(2)}, u32[]{:S(2)}) collective-permute-start(bf16[144,256]{1,0:T(8,128)(2,1)S(1)} %get-tuple-element.68), channel_id=1, source_target_pairs={{0,128},{32,160},{64,192},{96,224},{128,256},{160,288},{192,320},{... | collective-permute-start | bytes 221192 | tf_op jit(solution)/shard_map/ppermute | solution.py:370
  56.9 3.5 %collective-permute-start.7 = (bf16[144,256]{1,0:T(8,128)(2,1)S(1)}, bf16[144,256]{1,0:T(8,128)(2,1)S(1)}, u32[]{:S(2)}, u32[]{:S(2)}) collective-permute-start(bf16[144,256]{1,0:T(8,128)(2,1)S(1)} %get-tuple-element.70), channel_id=1, source_target_pairs={{0,384},{32,416},{64,448},{96,480},{128,0},{160,32},{192,64},{224,... | collective-permute-start | bytes 221192 | tf_op jit(solution)/shard_map/ppermute | solution.py:370
  66.4 6.6 %collective-permute-done.7.refs_3_ = bf16[144,256]{1,0:T(8,128)(2,1)S(1)} collective-permute-done((bf16[144,256]{1,0:T(8,128)(2,1)S(1)}, bf16[144,256]{1,0:T(8,128)(2,1)S(1)}, u32[]{:S(2)}, u32[]{:S(2)}) %collective-permute-start.7) | collective-permute-done | bytes 73760 | tf_op jit(solution)/shard_map/ppermute | solution.py:370
  74.3 4.9 %shard_map.183 = (f32[128,2048]{1,0:T(8,128)S(1)}, bf16[128,2048]{1,0:T(8,128)(2,1)S(1)}, bf16[128,2048]{1,0:T(8,128)(2,1)S(1)}, f32[128,128]{1,0:T(8,128)S(1)},...) custom-call(f32[128,128]{1,0:T(8,128)S(1)} %copy-done.15, bf16[128,2048]{1,0:T(8,128)(2,1)S(1)} %bitcast.20, ...), custom_call_target="tpu_custom_call" | custom-call | flops 671088640 | bytes 3473536 | tf_op jit(solution)/shard_map/pallas_call | solution.py:357
  83.1 4.4 %collective-permute-done.10.refs_6_ = bf16[144,256]{1,0:T(8,128)(2,1)S(1)} collective-permute-done((bf16[144,256]{1,0:T(8,128)(2,1)S(1)}, bf16[144,256]{1,0:T(8,128)(2,1)S(1)}, u32[]{:S(2)}, u32[]{:S(2)}) %collective-permute-start.10) | collective-permute-done | bytes 73760 | tf_op jit(solution)/shard_map/ppermute | solution.py:370
  91.2 3.5 %all-to-all-start.1 = ((bf16[4,256,512]{2,1,0:T(8,128)(2,1)}), bf16[4,256,512]{2,1,0:T(8,128)(2,1)S(1)}, u32[]{:S(2)}, u32[]{:S(2)}) async-start(bf16[4,256,512]{2,1,0:T(8,128)(2,1)} %shard_map.184), calls=%async_computation.1 | async-start | bytes 2097152 | tf_op jit(solution)/shard_map/all_to_all | solution.py:378
  94.8 4.6 %collective-permute-start.13 = (bf16[8,256,128]{2,1,0:T(8,128)(2,1)S(1)}, bf16[8,256,128]{2,1,0:T(8,128)(2,1)S(1)}, u32[]{:S(2)}, u32[]{:S(2)}) collective-permute-start(bf16[8,256,128]{2,1,0:T(8,128)(2,1)S(1)} %shard_map.187.refs_0_), channel_id=1, source_target_pairs={{0,24},{8,16},{16,8},{24,0},{1,25},{9,17},{17,9},{25,1},{2,26},{10... | collective-permute-start | bytes 1572872 | tf_op jit(solution)/shard_map/ppermute | solution.py:383
  101.3 9.7 %collective-permute-done.13.refs_2_ = bf16[8,256,128]{2,1,0:T(8,128)(2,1)S(1)} collective-permute-done((bf16[8,256,128]{2,1,0:T(8,128)(2,1)S(1)}, bf16[8,256,128]{2,1,0:T(8,128)(2,1)S(1)}, u32[]{:S(2)}, u32[]{:S(2)}) %collective-permute-start.13) | collective-permute-done | bytes 524320 | tf_op jit(solution)/shard_map/ppermute | solution.py:383
  114.9 4.2 %collective-permute-start.15 = (bf16[4,256,128]{2,1,0:T(8,128)(2,1)}, bf16[4,256,128]{2,1,0:T(8,128)(2,1)}, u32[]{:S(2)}, u32[]{:S(2)}) collective-permute-start(bf16[4,256,128]{2,1,0:T(8,128)(2,1)} %slice.9), channel_id=1, source_target_pairs={{0,24},{8,16},{16,8},{24,0},{1,25},{9,17},{17,9},{25,1},{2,26},{10... | collective-permute-start | bytes 786440 | tf_op jit(solution)/shard_map/ppermute | solution.py:383
  122.7 5.8 %all-to-all-start.2 = ((bf16[8,128,128]{2,1,0:T(8,128)(2,1)}), bf16[8,128,128]{2,1,0:T(8,128)(2,1)S(1)}, u32[]{:S(2)}, u32[]{:S(2)}) async-start(bf16[8,128,128]{2,1,0:T(8,128)(2,1)} %copy-done.11), calls=%async_computation.2 | async-start | bytes 524288 | tf_op jit(solution)/shard_map/all_to_all | solution.py:378
  128.5 6.5 %all-to-all-done.2.all_c = bf16[8,128,128]{2,1,0:T(8,128)(2,1)S(1)} async-done(((bf16[8,128,128]{2,1,0:T(8,128)(2,1)}), bf16[8,128,128]{2,1,0:T(8,128)(2,1)S(1)}, u32[]{:S(2)}, u32[]{:S(2)}) %all-to-all-start.2) | async-done | bytes 262176 | tf_op jit(solution)/shard_map/all_to_all | solution.py:378
  138.5 9.1 %all-to-all-start.3 = ((bf16[16,64,128]{2,1,0:T(8,128)(2,1)}), bf16[16,64,128]{2,1,0:T(8,128)(2,1)S(1)}, u32[]{:S(2)}, u32[]{:S(2)}) async-start(bf16[16,64,128]{2,1,0:T(8,128)(2,1)} %shard_map.188), calls=%async_computation.3 | async-start | bytes 524288 | tf_op jit(solution)/shard_map/all_to_all | solution.py:378
  152.4 3.9 %shard_map.185 = (bf16[128,2048]{1,0:T(8,128)(2,1)}, bf16[128,128]{1,0:T(8,128)(2,1)}, f32[8,128]{1,0:T(8,128)S(1)}) custom-call(bf16[4,256,512]{2,1,0:T(8,128)(2,1)S(1)} %all-to-all-done.1.states, bf16[128,2048]{1,0:T(8,128)(2,1)S(1)} %bitcast.21, bf16[128,2048]{1,0:T(8,128)(2,1)S(1)} %bitcast.24, bf16[128,2048]{1,0:T(8,128)(2,1)S(1)} %copy-done.7, ...), custom_call_target="tpu_custom_call" | custom-call | flops 201326592 | bytes 4562944 | tf_op jit(solution)/shard_map/pallas_call | solution.py:357
  156.3 4.2 %all-to-all-done.3.parts = bf16[16,64,128]{2,1,0:T(8,128)(2,1)S(1)} async-done(((bf16[16,64,128]{2,1,0:T(8,128)(2,1)}), bf16[16,64,128]{2,1,0:T(8,128)(2,1)S(1)}, u32[]{:S(2)}, u32[]{:S(2)}) %all-to-all-start.3) | async-done | bytes 262176 | tf_op jit(solution)/shard_map/all_to_all | solution.py:378
  160.7 22.5 %all_to_all.30.got = f32[16,8,128]{2,1,0:T(8,128)S(1)} all-to-all(f32[16,8,128]{2,1,0:T(8,128)S(1)} %get-tuple-element.99), channel_id=1, replica_groups=mesh['seq'=16,'tensor'=4,'dp'=8] {'seq'}, dimensions={0} | all-to-all | bytes 131072 | tf_op jit(solution)/shard_map/all_to_all | solution.py:378
  183.2 13.4 %all_to_all.31.got = f32[32,8,128]{2,1,0:T(8,128)S(1)} all-to-all(f32[32,8,128]{2,1,0:T(8,128)S(1)} %shard_map.190), channel_id=1, replica_groups=mesh['seq'=16,'tensor'=4,'dp'=8] {'tensor','dp'}, dimensions={0} | all-to-all | bytes 262144 | tf_op jit(solution)/shard_map/all_to_all | solution.py:378
  (90 shorter events, 41.8 us)
Async XLA Ops:
  4.9 32.8 %all-to-all-start = ((bf16[4,272,512]{2,1,0:T(8,128)(2,1)}), bf16[4,272,512]{2,1,0:T(8,128)(2,1)S(1)}, u32[]{:S(2)}, u32[]{:S(2)}) async-start(bf16[4,272,512]{2,1,0:T(8,128)(2,1)} %get-tuple-element.58), calls=%async_computation | async-start | bytes 2228224 | tf_op jit(solution)/shard_map/all_to_all | solution.py:378
  11.4 62.9 %copy-start.12 = (bf16[1,128,128]{2,1,0:T(8,128)(2,1)S(1)}, bf16[1,128,128]{2,1,0:T(8,128)(2,1)}, u32[]{:S(2)}) copy-start(bf16[1,128,128]{2,1,0:T(8,128)(2,1)} %param.13) | copy-start | bytes 98308
  11.4 62.9 %copy-start.13 = (bf16[1,128,128]{2,1,0:T(8,128)(2,1)S(1)}, bf16[1,128,128]{2,1,0:T(8,128)(2,1)}, u32[]{:S(2)}) copy-start(bf16[1,128,128]{2,1,0:T(8,128)(2,1)} %param.14) | copy-start | bytes 98308
  11.5 62.9 %copy-start.15 = (f32[128,128]{1,0:T(8,128)S(1)}, f32[128,128]{1,0:T(8,128)}, u32[]{:S(2)}) copy-start(f32[128,128]{1,0:T(8,128)} %get-tuple-element.71.cum) | copy-start | bytes 196612
  11.5 62.9 %copy-start.27 = (f32[32]{0:T(128)S(1)}, f32[32]{0:T(128)}, u32[]{:S(2)}) copy-start(f32[32]{0:T(128)} %param.18) | copy-start | bytes 388
  12.4 7.0 %collective-permute-start = (bf16[4,256,128]{2,1,0:T(8,128)(2,1)S(1)}, bf16[4,256,128]{2,1,0:T(8,128)(2,1)S(1)}, u32[]{:S(2)}, u32[]{:S(2)}) collective-permute-start(bf16[4,256,128]{2,1,0:T(8,128)(2,1)S(1)} %get-tuple-element.61), channel_id=1, source_target_pairs={{0,1},{1,0},{2,3},{3,2},{4,5},{5,4},{6,7},{7,6},{8,9},{9,8},{10,11... | collective-permute-start | bytes 786440 | tf_op jit(solution)/shard_map/ppermute | solution.py:383
  19.4 9.6 %collective-permute-start.1 = (bf16[2,256,128]{2,1,0:T(8,128)(2,1)S(1)}, bf16[2,256,128]{2,1,0:T(8,128)(2,1)S(1)}, u32[]{:S(2)}, u32[]{:S(2)}) collective-permute-start(bf16[2,256,128]{2,1,0:T(8,128)(2,1)S(1)} %get-tuple-element.63), channel_id=1, source_target_pairs={{0,2},{1,3},{2,0},{3,1},{4,6},{5,7},{6,4},{7,5},{8,10},{9,11},{10,... | collective-permute-start | bytes 393224 | tf_op jit(solution)/shard_map/ppermute | solution.py:383
  21.4 8.1 %collective-permute-start.2 = (bf16[2,256,128]{2,1,0:T(8,128)(2,1)S(1)}, bf16[2,256,128]{2,1,0:T(8,128)(2,1)S(1)}, u32[]{:S(2)}, u32[]{:S(2)}) collective-permute-start(bf16[2,256,128]{2,1,0:T(8,128)(2,1)S(1)} %get-tuple-element.64), channel_id=1, source_target_pairs={{0,4},{1,5},{2,6},{3,7},{4,0},{5,1},{6,2},{7,3},{8,12},{9,13},{10,... | collective-permute-start | bytes 393224 | tf_op jit(solution)/shard_map/ppermute | solution.py:383
  23.9 8.1 %collective-permute-start.3 = (bf16[2,256,128]{2,1,0:T(8,128)(2,1)S(1)}, bf16[2,256,128]{2,1,0:T(8,128)(2,1)S(1)}, u32[]{:S(2)}, u32[]{:S(2)}) collective-permute-start(bf16[2,256,128]{2,1,0:T(8,128)(2,1)S(1)} %get-tuple-element.65), channel_id=1, source_target_pairs={{0,6},{1,7},{2,4},{3,5},{4,2},{5,3},{6,0},{7,1},{8,14},{9,15},{10,... | collective-permute-start | bytes 393224 | tf_op jit(solution)/shard_map/ppermute | solution.py:383
  38.5 21.9 %collective-permute-start.4 = (bf16[144,256]{1,0:T(8,128)(2,1)S(1)}, bf16[144,256]{1,0:T(8,128)(2,1)S(1)}, u32[]{:S(2)}, u32[]{:S(2)}) collective-permute-start(bf16[144,256]{1,0:T(8,128)(2,1)S(1)} %get-tuple-element.67), channel_id=1, source_target_pairs={{0,128},{32,160},{64,192},{96,224},{128,256},{160,288},{192,320},{... | collective-permute-start | bytes 221192 | tf_op jit(solution)/shard_map/ppermute | solution.py:370
  47.7 14.4 %collective-permute-start.5 = (bf16[144,256]{1,0:T(8,128)(2,1)S(1)}, bf16[144,256]{1,0:T(8,128)(2,1)S(1)}, u32[]{:S(2)}, u32[]{:S(2)}) collective-permute-start(bf16[144,256]{1,0:T(8,128)(2,1)S(1)} %get-tuple-element.68), channel_id=1, source_target_pairs={{0,128},{32,160},{64,192},{96,224},{128,256},{160,288},{192,320},{... | collective-permute-start | bytes 221192 | tf_op jit(solution)/shard_map/ppermute | solution.py:370
  54.5 10.7 %collective-permute-start.6 = (bf16[144,256]{1,0:T(8,128)(2,1)S(1)}, bf16[144,256]{1,0:T(8,128)(2,1)S(1)}, u32[]{:S(2)}, u32[]{:S(2)}) collective-permute-start(bf16[144,256]{1,0:T(8,128)(2,1)S(1)} %get-tuple-element.69), channel_id=1, source_target_pairs={{0,384},{32,416},{64,448},{96,480},{128,0},{160,32},{192,64},{224,... | collective-permute-start | bytes 221192 | tf_op jit(solution)/shard_map/ppermute | solution.py:370
  56.9 16.1 %collective-permute-start.7 = (bf16[144,256]{1,0:T(8,128)(2,1)S(1)}, bf16[144,256]{1,0:T(8,128)(2,1)S(1)}, u32[]{:S(2)}, u32[]{:S(2)}) collective-permute-start(bf16[144,256]{1,0:T(8,128)(2,1)S(1)} %get-tuple-element.70), channel_id=1, source_target_pairs={{0,384},{32,416},{64,448},{96,480},{128,0},{160,32},{192,64},{224,... | collective-permute-start | bytes 221192 | tf_op jit(solution)/shard_map/ppermute | solution.py:370
  60.4 22.7 %collective-permute-start.8 = (bf16[144,256]{1,0:T(8,128)(2,1)S(1)}, bf16[144,256]{1,0:T(8,128)(2,1)S(1)}, u32[]{:S(2)}, u32[]{:S(2)}) collective-permute-start(bf16[144,256]{1,0:T(8,128)(2,1)S(1)} %collective-permute-done.4.refs_0_), channel_id=1, source_target_pairs={{128,256},{160,288},{192,320},{224,352},{256,384},{288,416},{320,4... | collective-permute-start | bytes 221192 | tf_op jit(solution)/shard_map/ppermute | solution.py:370
  62.2 21.0 %collective-permute-start.9 = (bf16[144,256]{1,0:T(8,128)(2,1)S(1)}, bf16[144,256]{1,0:T(8,128)(2,1)S(1)}, u32[]{:S(2)}, u32[]{:S(2)}) collective-permute-start(bf16[144,256]{1,0:T(8,128)(2,1)S(1)} %collective-permute-done.5.refs_1_), channel_id=1, source_target_pairs={{128,256},{160,288},{192,320},{224,352},{256,384},{288,416},{320,4... | collective-permute-start | bytes 221192 | tf_op jit(solution)/shard_map/ppermute | solution.py:370
  65.1 22.4 %collective-permute-start.10 = (bf16[144,256]{1,0:T(8,128)(2,1)S(1)}, bf16[144,256]{1,0:T(8,128)(2,1)S(1)}, u32[]{:S(2)}, u32[]{:S(2)}) collective-permute-start(bf16[144,256]{1,0:T(8,128)(2,1)S(1)} %collective-permute-done.6.refs_2_), channel_id=1, source_target_pairs={{128,0},{160,32},{192,64},{224,96},{256,128},{288,160},{320,192},{... | collective-permute-start | bytes 221192 | tf_op jit(solution)/shard_map/ppermute | solution.py:370
  73.0 16.1 %collective-permute-start.11 = (bf16[144,256]{1,0:T(8,128)(2,1)S(1)}, bf16[144,256]{1,0:T(8,128)(2,1)S(1)}, u32[]{:S(2)}, u32[]{:S(2)}) collective-permute-start(bf16[144,256]{1,0:T(8,128)(2,1)S(1)} %collective-permute-done.7.refs_3_), channel_id=1, source_target_pairs={{128,0},{160,32},{192,64},{224,96},{256,128},{288,160},{320,192},{... | collective-permute-start | bytes 221192 | tf_op jit(solution)/shard_map/ppermute | solution.py:370
  91.2 28.8 %all-to-all-start.1 = ((bf16[4,256,512]{2,1,0:T(8,128)(2,1)}), bf16[4,256,512]{2,1,0:T(8,128)(2,1)S(1)}, u32[]{:S(2)}, u32[]{:S(2)}) async-start(bf16[4,256,512]{2,1,0:T(8,128)(2,1)} %shard_map.184), calls=%async_computation.1 | async-start | bytes 2097152 | tf_op jit(solution)/shard_map/all_to_all | solution.py:378
  94.8 16.2 %collective-permute-start.13 = (bf16[8,256,128]{2,1,0:T(8,128)(2,1)S(1)}, bf16[8,256,128]{2,1,0:T(8,128)(2,1)S(1)}, u32[]{:S(2)}, u32[]{:S(2)}) collective-permute-start(bf16[8,256,128]{2,1,0:T(8,128)(2,1)S(1)} %shard_map.187.refs_0_), channel_id=1, source_target_pairs={{0,24},{8,16},{16,8},{24,0},{1,25},{9,17},{17,9},{25,1},{2,26},{10... | collective-permute-start | bytes 1572872 | tf_op jit(solution)/shard_map/ppermute | solution.py:383
  99.4 14.6 %collective-permute-start.12 = (bf16[8,256,128]{2,1,0:T(8,128)(2,1)S(1)}, bf16[8,256,128]{2,1,0:T(8,128)(2,1)S(1)}, u32[]{:S(2)}, u32[]{:S(2)}) collective-permute-start(bf16[8,256,128]{2,1,0:T(8,128)(2,1)S(1)} %shard_map.187.refs_0_), channel_id=1, source_target_pairs={{0,8},{8,0},{16,24},{24,16},{1,9},{9,1},{17,25},{25,17},{2,10},{10... | collective-permute-start | bytes 1572872 | tf_op jit(solution)/shard_map/ppermute | solution.py:383
  111.7 16.8 %collective-permute-start.14 = (bf16[4,256,128]{2,1,0:T(8,128)(2,1)}, bf16[4,256,128]{2,1,0:T(8,128)(2,1)}, u32[]{:S(2)}, u32[]{:S(2)}) collective-permute-start(bf16[4,256,128]{2,1,0:T(8,128)(2,1)} %slice.8), channel_id=1, source_target_pairs={{0,8},{8,0},{16,24},{24,16},{1,9},{9,1},{17,25},{25,17},{2,10},{10... | collective-permute-start | bytes 786440 | tf_op jit(solution)/shard_map/ppermute | solution.py:383
  114.9 13.6 %collective-permute-start.15 = (bf16[4,256,128]{2,1,0:T(8,128)(2,1)}, bf16[4,256,128]{2,1,0:T(8,128)(2,1)}, u32[]{:S(2)}, u32[]{:S(2)}) collective-permute-start(bf16[4,256,128]{2,1,0:T(8,128)(2,1)} %slice.9), channel_id=1, source_target_pairs={{0,24},{8,16},{16,8},{24,0},{1,25},{9,17},{17,9},{25,1},{2,26},{10... | collective-permute-start | bytes 786440 | tf_op jit(solution)/shard_map/ppermute | solution.py:383
  122.7 12.3 %all-to-all-start.2 = ((bf16[8,128,128]{2,1,0:T(8,128)(2,1)}), bf16[8,128,128]{2,1,0:T(8,128)(2,1)S(1)}, u32[]{:S(2)}, u32[]{:S(2)}) async-start(bf16[8,128,128]{2,1,0:T(8,128)(2,1)} %copy-done.11), calls=%async_computation.2 | async-start | bytes 524288 | tf_op jit(solution)/shard_map/all_to_all | solution.py:378
  138.5 22.0 %all-to-all-start.3 = ((bf16[16,64,128]{2,1,0:T(8,128)(2,1)}), bf16[16,64,128]{2,1,0:T(8,128)(2,1)S(1)}, u32[]{:S(2)}, u32[]{:S(2)}) async-start(bf16[16,64,128]{2,1,0:T(8,128)(2,1)} %shard_map.188), calls=%async_computation.3 | async-start | bytes 524288 | tf_op jit(solution)/shard_map/all_to_all | solution.py:378
  (24 other events, 360.7 us)

commit v8 on v5

--- a/solution.py
+++ b/solution.py
@@ -97,7 +97,7 @@
         st[piece, 2 * N :, spot] = log_rows(spread(last, j, first))
 
 
-def group_kernel(me, got, up, down):
+def group_kernel(me, got, out):
     here = me[0] // GROUP
     count = got.shape[0]
     for at in range(0, got.shape[2], PAIR):
@@ -110,37 +110,25 @@
         for k in reversed(range(count)):
             back = decay[k] * back + got[k, N : 2 * N, lanes].astype(f32)
         rows = log_rows(sum(logs[1:], logs[0]))
-        up[:N, lanes] = jnp.where(here < 3, ahead, back).astype(bf16)
-        up[N:, lanes] = rows
-        down[:N, lanes] = jnp.where(here > 0, back, ahead).astype(bf16)
-        down[N:, lanes] = rows
-
-
-def scan_kernel(me, got, up, down, up_two, down_two, ahead, *refs):
+        for k in range(out.shape[0]):
+            out[k, :N, lanes] = jnp.where(k > here, ahead, back).astype(bf16)
+            out[k, N:, lanes] = rows
+
+
+def scan_kernel(me, got, groups, ahead, *refs):
     backs, held = refs[:-1], refs[-1]
     here = me[0] // GROUP
     count = got.shape[0]
-
-    def pick(options, lanes):
-        parts = [(k, ref[:N, lanes].astype(f32), row_logs(ref[N:, lanes])) for k, ref in options]
-        _, part, log = parts[0]
-        for k, other, other_log in parts[1:]:
-            part = jnp.where(here == k, other, part)
-            log = jnp.where(here == k, other_log, log)
-        return part, jnp.exp(log)
-
-    before = (((1, up), (2, up_two), (3, down)), ((2, up), (3, up_two)), ((3, up),))
-    after = (((2, down), (1, down_two), (0, up)), ((1, down), (0, down_two)), ((0, down),))
     for at in range(0, got.shape[2], PAIR):
         lanes = slice(at, at + PAIR)
         decay = [jnp.exp(row_logs(got[k, 2 * N :, lanes])) for k in range(count)]
         state = back = jnp.zeros((N, PAIR), f32)
-        for k, options in enumerate(before):
-            part, fade = pick(options, lanes)
-            state = jnp.where(k < here, fade * state + part, state)
-        for k, options in enumerate(after):
-            part, fade = pick(options, lanes)
-            back = jnp.where(3 - k > here, fade * back + part, back)
+        for k in range(groups.shape[0]):
+            new = jnp.exp(row_logs(groups[k, N:, lanes])) * state + groups[k, :N, lanes].astype(f32)
+            state = jnp.where(k < here, new, state)
+        for k in reversed(range(groups.shape[0])):
+            new = jnp.exp(row_logs(groups[k, N:, lanes])) * back + groups[k, :N, lanes].astype(f32)
+            back = jnp.where(k > here, new, back)
         for k in range(count):
             ahead[k, :, lanes] = state.astype(bf16)
             state = decay[k] * state + got[k, :N, lanes].astype(f32)
@@ -235,17 +223,11 @@
     db[...] = dot(high, c[...])
 
 
-def grad_c_kernel(dc, dye, starts, grad_c, copies, held, sems):
+def grad_c_kernel(dc, dye, starts, grad_c, copies):
+    total = dc[...]
     pieces, width = starts.shape[0], starts.shape[2]
-    moves = []
     for j in range(pieces):
-        lanes = slice(j * width, (j + 1) * width)
-        moves.append(pltpu.make_async_copy(dye.at[:, lanes], held.at[:, lanes], sems.at[j]))
-        moves[j].start()
-    total = dc[...]
-    for j in range(pieces):
-        moves[j].wait()
-        total = total + dot_nt(held[:, j * width : (j + 1) * width], starts[j])
+        total = total + dot_nt(dye[:, j * width : (j + 1) * width], starts[j])
     out = total.astype(bf16)
     grad_c[...] = out
     for k in range(copies.shape[0]):
@@ -395,11 +377,6 @@
     return out[0] if count == 1 else out
 
 
-def shift(a, senders, step):
-    count = lax.axis_size("seq")
-    return lax.ppermute(a, "seq", [(i, (i + step) % count) for i in senders])
-
-
 def shaped(shape, dtype):
     return jax.ShapeDtypeStruct(shape, dtype)
 
@@ -434,6 +411,7 @@
     width = heads * P_SIZE
     piece = width // GROUP
     near = [[i + k for k in range(GROUP)] for i in range(0, seqs, GROUP)]
+    far = [list(range(i, seqs, GROUP)) for i in range(GROUP)]
     tile = shaped((SPAN, 128), f32)
     small_tile = shaped((8, 128), f32)
     wide = shaped((SPAN, width), bf16)
@@ -469,6 +447,8 @@
     pairs = [pairs] if half == 1 else pairs
     pairs = [pairs[0]] + [trade(pairs[k], "dp", 2 * k) for k in range(1, half)]
     got, *pairs = lax.optimization_barrier((got, *pairs))
+    mine = call(stack_kernel, [shaped((streams, block, SPAN), bf16)], *pairs)
+    left, right = trade(mine, "tensor", 1), trade(mine, "tensor", 3)
 
     dxp, xt, dye, dc, db, dcum = call(
         intra_kernel,
@@ -483,49 +463,42 @@
         flops=20 * SPAN * SPAN * width,
         hbm=(0, 1, 2, 4, 5),
     )
-    up, down = call(
+    ahead = call(
         group_kernel,
-        [shaped((N + LOG_ROWS, piece), bf16)] * 2,
+        [shaped((seqs // GROUP, N + LOG_ROWS, piece), bf16)],
         me,
         got,
         flops=8 * N * width,
     )
-    up, down = shift(up, range(seqs), GROUP), shift(down, range(seqs), -GROUP)
-    inner = range(GROUP, seqs - GROUP)
-    up_two, down_two = shift(up, inner, GROUP), shift(down, inner, -GROUP)
-    up_two, down_two, dye = lax.optimization_barrier((up_two, down_two, dye))
+    groups = swap(ahead, "seq", far)
+    groups, left, right = lax.optimization_barrier((groups, left, right))
+    far_a = trade(right[:half], "tensor", 1)
+    far_b = trade(left[half:], "tensor", 3)
     plan = ((0, ((0, 0),)), (1, ((1, 0),)), (3, ((2, 0),)), (2, ((3, 0), (4, half))))
     starts, *ends = call(
         scan_kernel,
         [shaped((GROUP, N, piece), bf16)] + [shaped((N, piece), bf16)] * GROUP,
         me,
         got,
-        up,
-        down,
-        up_two,
-        down_two,
+        groups,
         scratch=[pltpu.VMEM((GROUP, N, piece), bf16)],
         flops=8 * N * width,
         hbm=range(GROUP + 1),
     )
-    starts, *pairs = lax.optimization_barrier((starts, *pairs))
-    mine = call(stack_kernel, [shaped((streams, block, SPAN), bf16)], *pairs)
-    left, right = trade(mine, "tensor", 1), trade(mine, "tensor", 3)
-    far_a = trade(right[:half], "tensor", 1)
-    far_b = trade(left[half:], "tensor", 3)
     starts = swap(starts, "seq", near)
+    starts, far_a, far_b = lax.optimization_barrier((starts, far_a, far_b))
     grad_c, copies = call(
         grad_c_kernel,
         [shaped((SPAN, N), bf16), shaped((streams, SPAN, N), bf16)],
         dc,
         dye,
         starts,
-        scratch=[pltpu.VMEM((SPAN, width), bf16), pltpu.SemaphoreType.DMA((GROUP,))],
-        stay=(1,),
         flops=2 * SPAN * N * width,
-        hbm=(1,),
-    )
+    )
+    copies, *ends = lax.optimization_barrier((copies, *ends))
     all_c = swap(copies, "dp")
+    ends = [ends[0]] + [trade(ends[k], "seq", k) for k in range(1, GROUP)]
+    all_c, *ends = lax.optimization_barrier((all_c, *ends))
     partial = call(
         functools.partial(weight_kernel, plan),
         [shaped((seqs, rows, N), bf16)],
@@ -538,9 +511,7 @@
         far_b,
         flops=2 * tensors * layer.shape[1] * SPAN * N,
     )
-    partial, *ends = lax.optimization_barrier((partial, *ends))
     parts = swap(partial, "seq")
-    ends = [ends[0]] + [trade(ends[k], "seq", k) for k in range(1, GROUP)]
     grad_x, grad_b, small = call(
         rest_kernel,
         [wide, shaped((SPAN, N), bf16), small_tile],

time: 212 us -> 200 us (0.943)
  waiting for transfers between devices: 59.8 us -> 41 us
  local copies, waits for them, and re-layouts: 7.19 us -> 17.9 us
  starting transfers between devices: 81.7 us -> 76.4 us
  blocking collectives: 35.7 us -> 38.9 us
  Pallas kernels: 25.5 us -> 23.3 us
    ppermute x4 -> x0, waiting for transfers between devices: 20.1 us -> none  [shift(): return lax.ppermute(a, 'seq', [(i, (i + step) % count) for i in senders])]
    ppermute x4 -> x0, starting transfers between devices: 14.6 us -> none  [shift(): return lax.ppermute(a, 'seq', [(i, (i + step) % count) for i in senders])]
    unnamed x36 -> x66, local copies, waits for them, and re-layouts: 5.74 us -> 17.9 us
    all_to_all x4 -> x5, starting transfers between devices: 29.4 us -> 38.3 us  [swap(): return lax.all_to_all(a, axis, 0, 0, tiled=True, axis_index_groups=groups)]
    all_to_all x4 -> x5, waiting for transfers between devices: 12.2 us -> 17.8 us  [swap(): return lax.all_to_all(a, axis, 0, 0, tiled=True, axis_index_groups=groups)]
    ppermute x11, waiting for transfers between devices: 27.5 us -> 23.2 us  [trade(): return lax.ppermute(a, axis, [(i, i ^ k) for i in range(count)])]
    all_to_all x2, blocking collectives: 35.7 us -> 38.9 us  [swap(): return lax.all_to_all(a, axis, 0, 0, tiled=True, axis_index_groups=groups)]
    pallas_call x13, Pallas kernels: 25.5 us -> 23.3 us  [call(): pl.pallas_call(body, out_shape=tuple((pltpu.HBM(o.shape, o.dtype) if at i...]
  transfers between devices with their start and end apart: 19 -> 16, of which waited for: 12 -> 8; matrix products, arithmetic and copies ran while one was open for 1% -> 0% of each run, Pallas kernels for 7% -> 6%
where the time goes in v8:
time: 200 us; the launch traced here: 199 us
  starting transfers between devices  76.4 us (38%)
  waiting for transfers between devices  41 us (20%)
  blocking collectives  38.9 us (19%)
  Pallas kernels  23.3 us (12%)
  local copies, waits for them, and re-layouts  17.9 us (9%)
    all_to_all x2, blocking collectives, swap(): return lax.all_to_all(a, axis, 0, 0, tiled=True, axis_index_groups=groups)  38.9 us
    all_to_all x5, starting transfers between devices, swap(): return lax.all_to_all(a, axis, 0, 0, tiled=True, axis_index_groups=groups)  38.3 us
    ppermute x11, starting transfers between devices, trade(): return lax.ppermute(a, axis, [(i, i ^ k) for i in range(count)])  38.1 us
    pallas_call x13, Pallas kernels, call(): pl.pallas_call(body, out_shape=tuple((pltpu.HBM(o.shape, o.dtype) if at i...  23.3 us
    ppermute x11, waiting for transfers between devices, trade(): return lax.ppermute(a, axis, [(i, i ^ k) for i in range(count)])  23.2 us
    unnamed x66, local copies, waits for them, and re-layouts  17.9 us
    all_to_all x5, waiting for transfers between devices, swap(): return lax.all_to_all(a, axis, 0, 0, tiled=True, axis_index_groups=groups)  17.8 us
  transfers between devices with their start and end apart: 16, of which 8 were waited for; matrix products, arithmetic and copies ran while one was open for 0% of the time, Pallas kernels for 6%

profile of v8, /device:TPU:1, one launch (start us, length us, event | category | flops | bytes accessed | tf_op | source)
XLA Modules:
  0.0 198.6 jit_solution(3789153692978817213)
XLA Ops:
  0.6 4.2 %shard_map.179 = (bf16[4,272,512]{2,1,0:T(8,128)(2,1)}, f32[128,128]{1,0:T(8,128)}, f32[128,128]{1,0:T(8,128)}, f32[8,128]{1,0:T(8,128)}) custom-call(f32[32,128]{1,0:T(8,128)} %bitcast.33, s32[1,32]{1,0:T(1,128)} %bitcast.35, f32[8,32]{1,0:T(8,128)} %bitcast.34, bf16[128,2048]{1,0:T(8,128)(2,1)} %bitcast.19, bf16[128,2048]{1,0:T(8,128)(2,1)} %bitcast.22, ...), custom_call_target="tpu_custom_call" | custom-call | flops 134217728 | bytes 2380928 | tf_op jit(solution)/shard_map/pallas_call | solution.py:361
  4.9 6.6 %all-to-all-start = ((bf16[4,272,512]{2,1,0:T(8,128)(2,1)}), bf16[4,272,512]{2,1,0:T(8,128)(2,1)S(1)}, u32[]{:S(2)}, u32[]{:S(2)}) async-start(bf16[4,272,512]{2,1,0:T(8,128)(2,1)} %get-tuple-element.65), calls=%async_computation | async-start | bytes 2228224 | tf_op jit(solution)/shard_map/all_to_all | solution.py:385
  12.3 5.9 %collective-permute-start = (bf16[4,256,128]{2,1,0:T(8,128)(2,1)S(1)}, bf16[4,256,128]{2,1,0:T(8,128)(2,1)S(1)}, u32[]{:S(2)}, u32[]{:S(2)}) collective-permute-start(bf16[4,256,128]{2,1,0:T(8,128)(2,1)S(1)} %get-tuple-element.68), channel_id=1, source_target_pairs={{0,1},{1,0},{2,3},{3,2},{4,5},{5,4},{6,7},{7,6},{8,9},{9,8},{10,11... | collective-permute-start | bytes 786440 | tf_op jit(solution)/shard_map/ppermute | solution.py:390
  21.3 2.5 %collective-permute-start.2 = (bf16[2,256,128]{2,1,0:T(8,128)(2,1)S(1)}, bf16[2,256,128]{2,1,0:T(8,128)(2,1)S(1)}, u32[]{:S(2)}, u32[]{:S(2)}) collective-permute-start(bf16[2,256,128]{2,1,0:T(8,128)(2,1)S(1)} %get-tuple-element.71), channel_id=1, source_target_pairs={{0,4},{1,5},{2,6},{3,7},{4,0},{5,1},{6,2},{7,3},{8,12},{9,13},{10,... | collective-permute-start | bytes 393224 | tf_op jit(solution)/shard_map/ppermute | solution.py:390
  23.8 5.1 %collective-permute-start.3 = (bf16[2,256,128]{2,1,0:T(8,128)(2,1)S(1)}, bf16[2,256,128]{2,1,0:T(8,128)(2,1)S(1)}, u32[]{:S(2)}, u32[]{:S(2)}) collective-permute-start(bf16[2,256,128]{2,1,0:T(8,128)(2,1)S(1)} %get-tuple-element.72), channel_id=1, source_target_pairs={{0,6},{1,7},{2,4},{3,5},{4,2},{5,3},{6,0},{7,1},{8,14},{9,15},{10,... | collective-permute-start | bytes 393224 | tf_op jit(solution)/shard_map/ppermute | solution.py:390
  29.4 2.5 %collective-permute-done.3.refs_3_ = bf16[2,256,128]{2,1,0:T(8,128)(2,1)S(1)} collective-permute-done((bf16[2,256,128]{2,1,0:T(8,128)(2,1)S(1)}, bf16[2,256,128]{2,1,0:T(8,128)(2,1)S(1)}, u32[]{:S(2)}, u32[]{:S(2)}) %collective-permute-start.3) | collective-permute-done | bytes 131104 | tf_op jit(solution)/shard_map/ppermute | solution.py:390
  31.9 5.8 %all-to-all-done.refs_1_ = bf16[4,272,512]{2,1,0:T(8,128)(2,1)S(1)} async-done(((bf16[4,272,512]{2,1,0:T(8,128)(2,1)}), bf16[4,272,512]{2,1,0:T(8,128)(2,1)S(1)}, u32[]{:S(2)}, u32[]{:S(2)}) %all-to-all-start) | async-done | bytes 1114144 | tf_op jit(solution)/shard_map/all_to_all | solution.py:385
  39.3 13.1 %all-to-all-start.1 = ((bf16[4,144,512]{2,1,0:T(8,128)(2,1)}), bf16[4,144,512]{2,1,0:T(8,128)(2,1)S(1)}, u32[]{:S(2)}, u32[]{:S(2)}) async-start(bf16[4,144,512]{2,1,0:T(8,128)(2,1)} %shard_map.182), calls=%async_computation.1 | async-start | bytes 1179648 | tf_op jit(solution)/shard_map/all_to_all | solution.py:385
  52.5 4.6 %collective-permute-start.5 = (bf16[8,256,128]{2,1,0:T(8,128)(2,1)S(1)}, bf16[8,256,128]{2,1,0:T(8,128)(2,1)S(1)}, u32[]{:S(2)}, u32[]{:S(2)}) collective-permute-start(bf16[8,256,128]{2,1,0:T(8,128)(2,1)S(1)} %shard_map.183.refs_2_), channel_id=1, source_target_pairs={{0,24},{8,16},{16,8},{24,0},{1,25},{9,17},{17,9},{25,1},{2,26},{10... | collective-permute-start | bytes 1572872 | tf_op jit(solution)/shard_map/ppermute | solution.py:390
  59.1 8.4 %collective-permute-done.5.refs_4_ = bf16[8,256,128]{2,1,0:T(8,128)(2,1)S(1)} collective-permute-done((bf16[8,256,128]{2,1,0:T(8,128)(2,1)S(1)}, bf16[8,256,128]{2,1,0:T(8,128)(2,1)S(1)}, u32[]{:S(2)}, u32[]{:S(2)}) %collective-permute-start.5) | collective-permute-done | bytes 524320 | tf_op jit(solution)/shard_map/ppermute | solution.py:390
  67.5 3.0 %collective-permute-done.4.refs_3_ = bf16[8,256,128]{2,1,0:T(8,128)(2,1)S(1)} collective-permute-done((bf16[8,256,128]{2,1,0:T(8,128)(2,1)S(1)}, bf16[8,256,128]{2,1,0:T(8,128)(2,1)S(1)}, u32[]{:S(2)}, u32[]{:S(2)}) %collective-permute-start.4) | collective-permute-done | bytes 524320 | tf_op jit(solution)/shard_map/ppermute | solution.py:390
  70.5 12.1 %all-to-all-done.1.refs_2_ = bf16[4,144,512]{2,1,0:T(8,128)(2,1)S(1)} async-done(((bf16[4,144,512]{2,1,0:T(8,128)(2,1)}), bf16[4,144,512]{2,1,0:T(8,128)(2,1)S(1)}, u32[]{:S(2)}, u32[]{:S(2)}) %all-to-all-start.1) | async-done | bytes 589856 | tf_op jit(solution)/shard_map/all_to_all | solution.py:385
  82.6 2.1 %shard_map.184 = (bf16[4,128,512]{2,1,0:T(8,128)(2,1)}, bf16[128,512]{1,0:T(8,128)(2,1)}, bf16[128,512]{1,0:T(8,128)(2,1)}, bf16[128,512]{1,0:T(8,128)(2,1)}, bf16[128,512]{1,0:T(8,128)(2,1)}) custom-call(s32[3]{0:T(128)S(1)} %pad_add_fusion.refs_0_, bf16[4,272,512]{2,1,0:T(8,128)(2,1)S(1)} %all-to-all-done.refs_1_, ...), custom_call_target="tpu_custom_call" | custom-call | flops 2097152 | bytes 2752524 | tf_op jit(solution)/shard_map/pallas_call | solution.py:361
  84.7 3.6 %all-to-all-start.2 = ((bf16[4,128,512]{2,1,0:T(8,128)(2,1)}), bf16[4,128,512]{2,1,0:T(8,128)(2,1)S(1)}, u32[]{:S(2)}, u32[]{:S(2)}) async-start(bf16[4,128,512]{2,1,0:T(8,128)(2,1)} %get-tuple-element.79), calls=%async_computation.2 | async-start | bytes 1048576 | tf_op jit(solution)/shard_map/all_to_all | solution.py:385
  88.4 4.6 %collective-permute-start.7 = (bf16[4,256,128]{2,1,0:T(8,128)(2,1)S(1)}, bf16[4,256,128]{2,1,0:T(8,128)(2,1)S(1)}, u32[]{:S(2)}, u32[]{:S(2)}) collective-permute-start(bf16[4,256,128]{2,1,0:T(8,128)(2,1)S(1)} %slice.7), channel_id=1, source_target_pairs={{0,24},{8,16},{16,8},{24,0},{1,25},{9,17},{17,9},{25,1},{2,26},{10... | collective-permute-start | bytes 786440 | tf_op jit(solution)/shard_map/ppermute | solution.py:390
  95.1 6.2 %shard_map.185 = (f32[128,2048]{1,0:T(8,128)}, bf16[128,2048]{1,0:T(8,128)(2,1)}, bf16[128,2048]{1,0:T(8,128)(2,1)}, f32[128,128]{1,0:T(8,128)S(1)}, f32[128,128]{1,0:T(8,128)}, /*index=5*/f32[128,128]{1,0:T(8,128)}) custom-call(f32[128,128]{1,0:T(8,128)S(1)} %copy-done.24, bf16[128,2048]{1,0:T(8,128)(2,1)S(1)} %bitcast.20, bf16[128,2048]{1,0:T(8,128)(2,1)S(1)} %bitcast.23, ...), custom_call_target="tpu_custom_call" | custom-call | flops 671088640 | bytes 3473536 | tf_op jit(solution)/shard_map/pallas_call | solution.py:361
  105.4 7.0 %all-to-all-start.3 = ((bf16[8,128,128]{2,1,0:T(8,128)(2,1)}), bf16[8,128,128]{2,1,0:T(8,128)(2,1)S(1)}, u32[]{:S(2)}, u32[]{:S(2)}) async-start(bf16[8,128,128]{2,1,0:T(8,128)(2,1)} %copy-done.7), calls=%async_computation.3 | async-start | bytes 524288 | tf_op jit(solution)/shard_map/all_to_all | solution.py:385
  112.4 3.6 %collective-permute-start.8 = (bf16[128,512]{1,0:T(8,128)(2,1)}, bf16[128,512]{1,0:T(8,128)(2,1)S(1)}, u32[]{:S(2)}, u32[]{:S(2)}) collective-permute-start(bf16[128,512]{1,0:T(8,128)(2,1)} %get-tuple-element.93), channel_id=1, source_target_pairs={{0,32},{32,0},{64,96},{96,64},{128,160},{160,128},{192,224},{224,1... | collective-permute-start | bytes 393224 | tf_op jit(solution)/shard_map/ppermute | solution.py:390
  116.0 4.0 %collective-permute-start.9 = (bf16[128,512]{1,0:T(8,128)(2,1)}, bf16[128,512]{1,0:T(8,128)(2,1)S(1)}, u32[]{:S(2)}, u32[]{:S(2)}) collective-permute-start(bf16[128,512]{1,0:T(8,128)(2,1)} %get-tuple-element.94), channel_id=1, source_target_pairs={{0,64},{32,96},{64,0},{96,32},{128,192},{160,224},{192,128},{224,1... | collective-permute-start | bytes 393224 | tf_op jit(solution)/shard_map/ppermute | solution.py:390
  122.0 7.7 %collective-permute-done.9.refs_4_ = bf16[128,512]{1,0:T(8,128)(2,1)S(1)} collective-permute-done((bf16[128,512]{1,0:T(8,128)(2,1)}, bf16[128,512]{1,0:T(8,128)(2,1)S(1)}, u32[]{:S(2)}, u32[]{:S(2)}) %collective-permute-start.9) | collective-permute-done | bytes 131104 | tf_op jit(solution)/shard_map/ppermute | solution.py:390
  134.9 7.9 %all-to-all-start.4 = ((bf16[16,64,128]{2,1,0:T(8,128)(2,1)}), bf16[16,64,128]{2,1,0:T(8,128)(2,1)S(1)}, u32[]{:S(2)}, u32[]{:S(2)}) async-start(bf16[16,64,128]{2,1,0:T(8,128)(2,1)} %copy-done.3), calls=%async_computation.4 | async-start | bytes 524288 | tf_op jit(solution)/shard_map/all_to_all | solution.py:385
  153.6 4.5 %shard_map.187 = (bf16[128,2048]{1,0:T(8,128)(2,1)}, bf16[128,128]{1,0:T(8,128)(2,1)}, f32[8,128]{1,0:T(8,128)S(1)}) custom-call(s32[3]{0:T(128)S(1)} %pad_add_fusion.refs_0_, bf16[4,128,512]{2,1,0:T(8,128)(2,1)S(1)} %all-to-all-done.2.refs_2_.refs_1_, bf16[128,512]{1,0:T(8,128)(2,1)S(1)} %copy-done.16, bf16[128,512]{1,0:T(8,128)(2,1)S(1)} %copy-done.18, ...), custom_call_target="tpu_custom_call" | custom-call | flops 201326592 | bytes 4562956 | tf_op jit(solution)/shard_map/pallas_call | solution.py:361
  158.3 22.8 %all_to_all.35.refs_0_ = f32[16,8,128]{2,1,0:T(8,128)S(1)} all-to-all(f32[16,8,128]{2,1,0:T(8,128)S(1)} %get-tuple-element.113), channel_id=1, replica_groups=mesh['seq'=16,'tensor'=4,'dp'=8] {'seq'}, dimensions={0} | all-to-all | bytes 131072 | tf_op jit(solution)/shard_map/all_to_all | solution.py:385
  181.2 16.0 %all_to_all.36.refs_1_ = f32[32,8,128]{2,1,0:T(8,128)S(1)} all-to-all(f32[32,8,128]{2,1,0:T(8,128)S(1)} %shard_map.190), channel_id=1, replica_groups=mesh['seq'=16,'tensor'=4,'dp'=8] {'tensor','dp'}, dimensions={0} | all-to-all | bytes 262144 | tf_op jit(solution)/shard_map/all_to_all | solution.py:385
  (92 shorter events, 33.5 us)
Async XLA Ops:
  4.9 32.8 %all-to-all-start = ((bf16[4,272,512]{2,1,0:T(8,128)(2,1)}), bf16[4,272,512]{2,1,0:T(8,128)(2,1)S(1)}, u32[]{:S(2)}, u32[]{:S(2)}) async-start(bf16[4,272,512]{2,1,0:T(8,128)(2,1)} %get-tuple-element.65), calls=%async_computation | async-start | bytes 2228224 | tf_op jit(solution)/shard_map/all_to_all | solution.py:385
  12.3 7.0 %collective-permute-start = (bf16[4,256,128]{2,1,0:T(8,128)(2,1)S(1)}, bf16[4,256,128]{2,1,0:T(8,128)(2,1)S(1)}, u32[]{:S(2)}, u32[]{:S(2)}) collective-permute-start(bf16[4,256,128]{2,1,0:T(8,128)(2,1)S(1)} %get-tuple-element.68), channel_id=1, source_target_pairs={{0,1},{1,0},{2,3},{3,2},{4,5},{5,4},{6,7},{7,6},{8,9},{9,8},{10,11... | collective-permute-start | bytes 786440 | tf_op jit(solution)/shard_map/ppermute | solution.py:390
  19.4 9.6 %collective-permute-start.1 = (bf16[2,256,128]{2,1,0:T(8,128)(2,1)S(1)}, bf16[2,256,128]{2,1,0:T(8,128)(2,1)S(1)}, u32[]{:S(2)}, u32[]{:S(2)}) collective-permute-start(bf16[2,256,128]{2,1,0:T(8,128)(2,1)S(1)} %get-tuple-element.70), channel_id=1, source_target_pairs={{0,2},{1,3},{2,0},{3,1},{4,6},{5,7},{6,4},{7,5},{8,10},{9,11},{10,... | collective-permute-start | bytes 393224 | tf_op jit(solution)/shard_map/ppermute | solution.py:390
  21.3 8.1 %collective-permute-start.2 = (bf16[2,256,128]{2,1,0:T(8,128)(2,1)S(1)}, bf16[2,256,128]{2,1,0:T(8,128)(2,1)S(1)}, u32[]{:S(2)}, u32[]{:S(2)}) collective-permute-start(bf16[2,256,128]{2,1,0:T(8,128)(2,1)S(1)} %get-tuple-element.71), channel_id=1, source_target_pairs={{0,4},{1,5},{2,6},{3,7},{4,0},{5,1},{6,2},{7,3},{8,12},{9,13},{10,... | collective-permute-start | bytes 393224 | tf_op jit(solution)/shard_map/ppermute | solution.py:390
  23.8 8.0 %collective-permute-start.3 = (bf16[2,256,128]{2,1,0:T(8,128)(2,1)S(1)}, bf16[2,256,128]{2,1,0:T(8,128)(2,1)S(1)}, u32[]{:S(2)}, u32[]{:S(2)}) collective-permute-start(bf16[2,256,128]{2,1,0:T(8,128)(2,1)S(1)} %get-tuple-element.72), channel_id=1, source_target_pairs={{0,6},{1,7},{2,4},{3,5},{4,2},{5,3},{6,0},{7,1},{8,14},{9,15},{10,... | collective-permute-start | bytes 393224 | tf_op jit(solution)/shard_map/ppermute | solution.py:390
  39.3 43.2 %all-to-all-start.1 = ((bf16[4,144,512]{2,1,0:T(8,128)(2,1)}), bf16[4,144,512]{2,1,0:T(8,128)(2,1)S(1)}, u32[]{:S(2)}, u32[]{:S(2)}) async-start(bf16[4,144,512]{2,1,0:T(8,128)(2,1)} %shard_map.182), calls=%async_computation.1 | async-start | bytes 1179648 | tf_op jit(solution)/shard_map/all_to_all | solution.py:385
  52.5 15.0 %collective-permute-start.5 = (bf16[8,256,128]{2,1,0:T(8,128)(2,1)S(1)}, bf16[8,256,128]{2,1,0:T(8,128)(2,1)S(1)}, u32[]{:S(2)}, u32[]{:S(2)}) collective-permute-start(bf16[8,256,128]{2,1,0:T(8,128)(2,1)S(1)} %shard_map.183.refs_2_), channel_id=1, source_target_pairs={{0,24},{8,16},{16,8},{24,0},{1,25},{9,17},{17,9},{25,1},{2,26},{10... | collective-permute-start | bytes 1572872 | tf_op jit(solution)/shard_map/ppermute | solution.py:390
  57.2 13.3 %collective-permute-start.4 = (bf16[8,256,128]{2,1,0:T(8,128)(2,1)S(1)}, bf16[8,256,128]{2,1,0:T(8,128)(2,1)S(1)}, u32[]{:S(2)}, u32[]{:S(2)}) collective-permute-start(bf16[8,256,128]{2,1,0:T(8,128)(2,1)S(1)} %shard_map.183.refs_2_), channel_id=1, source_target_pairs={{0,8},{8,0},{16,24},{24,16},{1,9},{9,1},{17,25},{25,17},{2,10},{10... | collective-permute-start | bytes 1572872 | tf_op jit(solution)/shard_map/ppermute | solution.py:390
  84.7 10.3 %copy-start = (bf16[1,128,2048]{2,1,0:T(8,128)(2,1)S(1)}, bf16[1,128,2048]{2,1,0:T(8,128)(2,1)}, u32[]{:S(2)}) copy-start(bf16[1,128,2048]{2,1,0:T(8,128)(2,1)} %param.12) | copy-start | bytes 1572868
  84.7 10.3 %copy-start.1 = (bf16[1,128,2048]{2,1,0:T(8,128)(2,1)S(1)}, bf16[1,128,2048]{2,1,0:T(8,128)(2,1)}, u32[]{:S(2)}) copy-start(bf16[1,128,2048]{2,1,0:T(8,128)(2,1)} %param.19) | copy-start | bytes 1572868
  84.7 10.3 %copy-start.12 = (bf16[1,128,128]{2,1,0:T(8,128)(2,1)S(1)}, bf16[1,128,128]{2,1,0:T(8,128)(2,1)}, u32[]{:S(2)}) copy-start(bf16[1,128,128]{2,1,0:T(8,128)(2,1)} %param.13) | copy-start | bytes 98308
  84.7 18.0 %all-to-all-start.2 = ((bf16[4,128,512]{2,1,0:T(8,128)(2,1)}), bf16[4,128,512]{2,1,0:T(8,128)(2,1)S(1)}, u32[]{:S(2)}, u32[]{:S(2)}) async-start(bf16[4,128,512]{2,1,0:T(8,128)(2,1)} %get-tuple-element.79), calls=%async_computation.2 | async-start | bytes 1048576 | tf_op jit(solution)/shard_map/all_to_all | solution.py:385
  88.4 12.9 %collective-permute-start.7 = (bf16[4,256,128]{2,1,0:T(8,128)(2,1)S(1)}, bf16[4,256,128]{2,1,0:T(8,128)(2,1)S(1)}, u32[]{:S(2)}, u32[]{:S(2)}) collective-permute-start(bf16[4,256,128]{2,1,0:T(8,128)(2,1)S(1)} %slice.7), channel_id=1, source_target_pairs={{0,24},{8,16},{16,8},{24,0},{1,25},{9,17},{17,9},{25,1},{2,26},{10... | collective-permute-start | bytes 786440 | tf_op jit(solution)/shard_map/ppermute | solution.py:390
  93.1 8.9 %collective-permute-start.6 = (bf16[4,256,128]{2,1,0:T(8,128)(2,1)S(1)}, bf16[4,256,128]{2,1,0:T(8,128)(2,1)S(1)}, u32[]{:S(2)}, u32[]{:S(2)}) collective-permute-start(bf16[4,256,128]{2,1,0:T(8,128)(2,1)S(1)} %slice.6), channel_id=1, source_target_pairs={{0,8},{8,0},{16,24},{24,16},{1,9},{9,1},{17,25},{25,17},{2,10},{10... | collective-permute-start | bytes 786440 | tf_op jit(solution)/shard_map/ppermute | solution.py:390
  105.4 37.4 %copy-start.31 = (f32[8,128]{1,0:T(8,128)S(1)}, f32[8,128]{1,0:T(8,128)}, u32[]{:S(2)}) copy-start(f32[8,128]{1,0:T(8,128)} %get-tuple-element.102.refs_11_) | copy-start | bytes 12292
  105.4 25.6 %all-to-all-start.3 = ((bf16[8,128,128]{2,1,0:T(8,128)(2,1)}), bf16[8,128,128]{2,1,0:T(8,128)(2,1)S(1)}, u32[]{:S(2)}, u32[]{:S(2)}) async-start(bf16[8,128,128]{2,1,0:T(8,128)(2,1)} %copy-done.7), calls=%async_computation.3 | async-start | bytes 524288 | tf_op jit(solution)/shard_map/all_to_all | solution.py:385
  112.4 9.5 %collective-permute-start.8 = (bf16[128,512]{1,0:T(8,128)(2,1)}, bf16[128,512]{1,0:T(8,128)(2,1)S(1)}, u32[]{:S(2)}, u32[]{:S(2)}) collective-permute-start(bf16[128,512]{1,0:T(8,128)(2,1)} %get-tuple-element.93), channel_id=1, source_target_pairs={{0,32},{32,0},{64,96},{96,64},{128,160},{160,128},{192,224},{224,1... | collective-permute-start | bytes 393224 | tf_op jit(solution)/shard_map/ppermute | solution.py:390
  116.0 13.7 %collective-permute-start.9 = (bf16[128,512]{1,0:T(8,128)(2,1)}, bf16[128,512]{1,0:T(8,128)(2,1)S(1)}, u32[]{:S(2)}, u32[]{:S(2)}) collective-permute-start(bf16[128,512]{1,0:T(8,128)(2,1)} %get-tuple-element.94), channel_id=1, source_target_pairs={{0,64},{32,96},{64,0},{96,32},{128,192},{160,224},{192,128},{224,1... | collective-permute-start | bytes 393224 | tf_op jit(solution)/shard_map/ppermute | solution.py:390
  120.0 10.3 %collective-permute-start.10 = (bf16[128,512]{1,0:T(8,128)(2,1)}, bf16[128,512]{1,0:T(8,128)(2,1)S(1)}, u32[]{:S(2)}, u32[]{:S(2)}) collective-permute-start(bf16[128,512]{1,0:T(8,128)(2,1)} %get-tuple-element.95), channel_id=1, source_target_pairs={{0,96},{32,64},{64,32},{96,0},{128,224},{160,192},{192,160},{224,1... | collective-permute-start | bytes 393224 | tf_op jit(solution)/shard_map/ppermute | solution.py:390
  122.0 12.2 %copy-start.17 = (bf16[128,512]{1,0:T(8,128)(2,1)}, bf16[128,512]{1,0:T(8,128)(2,1)S(1)}, u32[]{:S(2)}) copy-start(bf16[128,512]{1,0:T(8,128)(2,1)S(1)} %collective-permute-done.8.refs_3_) | copy-start | bytes 393220
  134.9 23.2 %all-to-all-start.4 = ((bf16[16,64,128]{2,1,0:T(8,128)(2,1)}), bf16[16,64,128]{2,1,0:T(8,128)(2,1)S(1)}, u32[]{:S(2)}, u32[]{:S(2)}) async-start(bf16[16,64,128]{2,1,0:T(8,128)(2,1)} %copy-done.3), calls=%async_computation.4 | async-start | bytes 524288 | tf_op jit(solution)/shard_map/all_to_all | solution.py:385
  153.6 43.6 %copy-start.28 = (f32[64,128]{1,0:T(8,128)S(1)}, f32[64,128]{1,0:T(8,128)}, u32[]{:S(2)}) copy-start(f32[64,128]{1,0:T(8,128)} %refs_3_.1) | copy-start | bytes 98308
  153.6 43.6 %copy-start.29 = (f32[64,128]{1,0:T(8,128)S(1)}, f32[64,128]{1,0:T(8,128)}, u32[]{:S(2)}) copy-start(f32[64,128]{1,0:T(8,128)} %refs_4_.1) | copy-start | bytes 98308
  153.6 43.6 %copy-start.30 = (f32[64,128]{1,0:T(8,128)S(1)}, f32[64,128]{1,0:T(8,128)}, u32[]{:S(2)}) copy-start(f32[64,128]{1,0:T(8,128)} %refs_5_.1) | copy-start | bytes 98308
  (25 other events, 55.5 us)
